TPU v7x, 256 devices: a whole 4x4x8 slice. The times are simulated.
256 devices in a mesh: row: 8 (over y, core), col: 32 (over z, x).
Axes of the slice: x: 4, y: 4, z: 8, core: 2. Of those that a mesh axis runs over, the one named last changes fastest.
Arguments:
- upper_vectors: float32 [16384, 16384], P('row', 'col'), may hold values from -6 to 6
- lower_vectors: float32 [16384, 16384], P('row', 'col'), may hold values from -6 to 6
- secular_roots: float32 [512], replicated, may hold values from 0 to 512
- pole_values: float32 [2, 16384], P(None, ('col', 'row')), may hold values from -1 to 512, as said below
- pole_weights: float32 [2, 16384], P(None, ('col', 'row')), may hold values from -3 to 3, as said below
- undeflated: int32 [2, 16384], P(None, ('col', 'row')), may hold values from 0 to 1
Outputs:
- merged_vectors: float32 [16384, 2, 512], P(('row', 'col'))
Inputs may be any that keep to these rules, and one draw needn't show every extreme that they name: `pole_values`: every pole differs from every root by 0.15 or more. `pole_weights`: magnitudes are 0.3 or more.
All inputs are finite; a program needn't handle non-finite values.
Results may differ from a plain program's by a relative error of at most 0.0003.
Values sent between devices are 32-bit elements; how exact they have to be, the bound alone decides.
No kernel may reach another device: no remote copies, remote signals or barrier semaphores. Data moves between devices by JAX's collectives and lax.ppermute only.
A program may use at most 64 MiB of HBM per device.

v0:
```python
import jax
import jax.numpy as jnp
from jax import lax
from jax.sharding import PartitionSpec as P


def column_norms(partial_squares):
    return jnp.sqrt(lax.psum(partial_squares, "col"))


def local(upper_vectors, lower_vectors, secular_roots, pole_values, pole_weights, undeflated):
    scaled = pole_weights * undeflated.astype(jnp.float32)
    block_poles, block_weights = (
        lax.all_gather(pole_values, "row", axis=1, tiled=True),
        lax.all_gather(scaled, "row", axis=1, tiled=True),
    )
    coefficient = block_weights[:, :, None] / (
        block_poles[:, :, None] - secular_roots[None, None, :]
    )
    partial_squares = jnp.sum(coefficient * coefficient, axis=(0, 1))
    coefficient = coefficient / column_norms(partial_squares)
    upper_term = jnp.dot(
        upper_vectors,
        coefficient[0],
        precision=lax.Precision.HIGHEST,
        preferred_element_type=jnp.float32,
    )
    lower_term = jnp.dot(
        lower_vectors,
        coefficient[1],
        precision=lax.Precision.HIGHEST,
        preferred_element_type=jnp.float32,
    )
    return lax.psum_scatter(
        jnp.stack([upper_term, lower_term], axis=1), "col", scatter_dimension=0, tiled=True
    )


def solution(mesh):
    return jax.shard_map(
        local,
        mesh=mesh,
        in_specs=(
            P("row", "col"),
            P("row", "col"),
            P(),
            P(None, ("col", "row")),
            P(None, ("col", "row")),
            P(None, ("col", "row")),
        ),
        out_specs=P(("row", "col"), None, None),
        check_vma=False,
    )
```

profile of v0, /device:TPU:2, one launch (start us, length us, event | category | flops | bytes accessed | tf_op | source)
XLA Modules:
  0.0 366.4 jit_solution(5564185389410197202)
XLA Ops:
  6.5 0.0 all-reduce.3.cloned.1.call-start
  6.5 0.7 multiply_bitcast_fusion
  7.2 10.8 %all-gather = f32[8,64,2]{1,2,0:T(2,128)S(1)} all-gather(f32[1,64,2]{1,2,0:T(2,128)S(1)} %multiply_bitcast_fusion), channel_id=1, replica_groups=mesh['row'=8,'col'=32] {'row'}, dimensions={0}, use_global_device_ids=true | all-gather | bytes 4608 | tf_op jit(solution)/shard_map/all_gather | solution.py:15
  18.0 0.1 reshape.5
  18.1 8.4 %all-gather.1 = f32[8,64,2]{1,2,0:T(2,128)S(1)} all-gather(f32[1,64,2]{1,2,0:T(2,128)} %bitcast.34), channel_id=1, replica_groups=mesh['row'=8,'col'=32] {'row'}, dimensions={0}, use_global_device_ids=true | all-gather | bytes 4608 | tf_op jit(solution)/shard_map/all_gather | solution.py:14
  26.5 0.1 reshape.7
  26.5 1.1 fusion.1
  27.7 73.7 %psum.7 = f32[512]{0:T(512)S(1)} all-reduce(f32[512]{0:T(512)S(1)} %fusion.1), channel_id=1, replica_groups=mesh['row'=8,'col'=32] {'col'}, use_global_device_ids=true, to_apply=%region_1.0 | all-reduce | flops 512 | bytes 4096 | tf_op jit(solution)/shard_map/psum | solution.py:8
  101.3 1.0 fusion.2
  102.4 0.0 copy-start
  102.4 15.8 %convolution_bitcast_fusion = f32[2048,1,512]{0,2,1:T(8,128)S(1)} fusion(f32[2048,512]{1,0:T(8,128)} %param.7, f32[2,512,512]{2,1,0:T(8,128)S(1)} %fusion.2), kind=kOutput, calls=%fused_computation.1 | convolution fusion | flops 6442450944 | bytes 9437184 | tf_op jit(solution)/shard_map/dot_general | solution.py:28
  118.2 0.0 copy-done
  118.2 13.7 %convolution_bitcast_fusion.1 = f32[2048,1,512]{0,2,1:T(8,128)S(1)} fusion(f32[2048,512]{1,0:T(8,128)S(1)} %copy-done, f32[2,512,512]{2,1,0:T(8,128)S(1)} %fusion.2), kind=kOutput, calls=%fused_computation.2 | convolution fusion | flops 6442450944 | bytes 9437184 | tf_op jit(solution)/shard_map/dot_general | solution.py:22
  131.9 3.8 %pad_maximum_fusion = f32[2048,2,512]{0,2,1:T(8,128)} fusion(f32[2048,1,512]{0,2,1:T(8,128)S(1)} %convolution_bitcast_fusion, f32[2048,1,512]{0,2,1:T(8,128)S(1)} %convolution_bitcast_fusion.1), kind=kLoop, calls=%fused_computation | loop fusion | flops 2097152 | bytes 16777216 | tf_op jit(solution)/shard_map/stack | solution.py:35
  135.7 13.2 %copy.17 = f32[2048,2,512]{2,1,0:T(2,128)} copy(f32[2048,2,512]{0,2,1:T(8,128)} %pad_maximum_fusion) | data formatting | bytes 16777216 | tf_op jit(solution)/shard_map/stack | solution.py:35
  148.8 0.0 copy-start.1
  148.8 0.0 all-reduce.3.cloned.1.call-update
  148.9 0.6 copy-done.1
  149.5 0.6 dynamic-slice
  150.7 207.1 %all-reduce.3.cloned.1.call-done = f32[2048,2,512]{2,1,0:T(2,128)} async-done(((f32[2048,2,512]{2,1,0:T(2,128)}), f32[2048,2,512]{2,1,0:T(2,128)}) %all-reduce.3.cloned.1.call-update) | async-done | bytes 8388624
  357.9 1.7 constant_dynamic-slice_fusion
  (3 shorter events, 0.0 us)
Async XLA Ops:
  6.5 351.3 %all-reduce.3.cloned.1.call-start = ((), (), s32[]{:S(2)}) async-start(), calls=%async_computation | async-start | bytes 16777216
  102.4 15.8 %copy-start = (f32[2048,512]{1,0:T(8,128)S(1)}, f32[2048,512]{1,0:T(8,128)}, u32[]{:S(2)}) copy-start(f32[2048,512]{1,0:T(8,128)} %param.6) | copy-start | bytes 12582916
  148.8 0.7 copy-start.1
Sparse Core Ops, SparseCore 0:
  149.0 208.8 all-reduce.2
where the time goes:
time: 368 us; the launch traced here: 366 us
  waiting for transfers between devices  207 us (56%)
  blocking collectives  92.8 us (25%)
  matrix products  29.4 us (8%)
  local copies, waits for them, and re-layouts  16.2 us (4%)
  between operations  14.1 us (4%)
  other arithmetic  6.63 us (2%)
    unnamed x2, waiting for transfers between devices  207 us
    psum x1, blocking collectives, column_norms(): return jnp.sqrt(lax.psum(partial_squares, 'col'))  73.7 us
    dot_general x1, matrix products, local(): jnp.dot(lower_vectors, coefficient[1], precision=lax.Precision.HIGHEST, p...  15.8 us
    dot_general x1, matrix products, local(): jnp.dot(upper_vectors, coefficient[0], precision=lax.Precision.HIGHEST, p...  13.7 us
    another operation x1, local copies, waits for them, and re-layouts, local(): jnp.stack([upper_term, lower_term], axis=1)  13.2 us
    all_gather x1, blocking collectives, local(): lax.all_gather(scaled, 'row', axis=1, tiled=True)  10.8 us
    all_gather x1, blocking collectives, local(): lax.all_gather(pole_values, 'row', axis=1, tiled=True)  8.35 us
  transfers between devices with their start and end apart: 1, of which 1 were waited for; matrix products, arithmetic and copies ran while one was open for 0% of the time, Pallas kernels for 0%

commit v1 on v0

v1 whole, which is shorter than its diff:
```python
import functools

import jax
import jax.numpy as jnp
from jax import lax
from jax.experimental import pallas as pl
from jax.experimental.pallas import tpu as pltpu
from jax.sharding import PartitionSpec as P

F32 = jnp.float32
BF16 = jnp.bfloat16
ROWS = 64
WIDE = 512
HBM = pl.BlockSpec(memory_space=pltpu.HBM)
VMEM = pl.BlockSpec(memory_space=pltpu.VMEM)
KERNEL = pltpu.CompilerParams(vmem_limit_bytes=24 << 20)


def pair_e(x):
    return x ^ 1


def pair_f(x):
    return (((x + 1) ^ 1) + 3) & 3


def pair_a(z):
    return z ^ 1


def pair_b(z):
    return (((z + 1) ^ 1) + 7) & 7


def pair_c(z):
    return (11 + 4 * (((z + 1) >> 1) & 1) - z) & 7


def pair_d(z):
    return (13 - 4 * ((z >> 1) & 1) - z) & 7


X_PAIRS = ((pair_e, pair_f), (pair_f, pair_e))
Z_PAIRS = ((pair_a, pair_b, pair_c), (pair_b, pair_a, pair_d))


def partners(stream, phase):
    (e, f), (a, b, c) = X_PAIRS[stream], Z_PAIRS[stream]
    steps = (
        (("x", e), ("x", f), ("z", a), ("z", b), ("z", c)),
        (("z", a), ("z", b), ("x", e), ("x", f), ("z", c)),
    )
    pairs = []
    for row in range(8):
        for col in range(32):
            axis, pair = steps[row % 2][phase]
            z, x = divmod(col, 4)
            to = z * 4 + pair(x) if axis == "x" else pair(z) * 4 + x
            pairs.append((row * 32 + col, row * 32 + to))
    return pairs


PARTNERS = tuple(tuple(partners(stream, phase) for phase in range(5)) for stream in range(2))


def exchange(block, stream, phase):
    return lax.ppermute(block, ("row", "col"), PARTNERS[stream][phase])


def chunk_order(stream, count, first):
    core = lax.axis_index("row") & 1
    col = lax.axis_index("col")
    z, x = col >> 2, col & 3
    (e, f), (a, b, c) = X_PAIRS[stream], Z_PAIRS[stream]

    def walk(start, pairs, bits):
        for pair, bit in zip(pairs, bits):
            start = pair(start) if bit else start
        return start

    xs = {(i, j): walk(x, (e, f), (i, j)) for i in (0, 1) for j in (0, 1)}
    zs = {
        (i, j, k): walk(z, (a, b, c), (i, j, k)) for i in (0, 1) for j in (0, 1) for k in (0, 1)
    }
    order = []
    for k in range(first, first + count):
        b4, b3, b2, b1, b0 = [(k >> s) & 1 for s in (4, 3, 2, 1, 0)]
        on0 = zs[b2, b1, b0] * 4 + xs[b4, b3]
        on1 = zs[b4, b3, b0] * 4 + xs[b2, b1]
        order.append(jnp.where(core == 0, on0, on1))
    return order


def pick_kernel(stream, first, vectors, out, sems):
    copies = []
    for k, chunk in enumerate(chunk_order(stream, 16, first)):
        copies.append(
            pltpu.make_async_copy(
                vectors.at[pl.ds(pl.multiple_of(chunk * ROWS, ROWS), ROWS), :],
                out.at[pl.ds(k * ROWS, ROWS), :],
                sems.at[k],
            )
        )
    for copy in copies:
        copy.start()
    for copy in copies:
        copy.wait()


def pick(vectors, stream, first):
    return pl.pallas_call(
        functools.partial(pick_kernel, stream, first),
        out_shape=jax.ShapeDtypeStruct((16 * ROWS, WIDE), F32),
        in_specs=[HBM],
        out_specs=VMEM,
        scratch_shapes=[pltpu.SemaphoreType.DMA((16,))],
        compiler_params=KERNEL,
        cost_estimate=pl.CostEstimate(flops=0, bytes_accessed=4 << 20, transcendentals=0),
        name=("pick_upper", "pick_lower")[stream] + ("_send" if first else "_keep"),
    )(vectors)


def pack_kernel(poles, weights, undeflated, out):
    out[...] = jnp.zeros_like(out)
    out[0:2, 0:64] = poles[...]
    out[2:4, 0:64] = weights[...] * undeflated[...].astype(F32)


def pack(*arrays):
    return pl.pallas_call(
        pack_kernel,
        out_shape=jax.ShapeDtypeStruct((8, 128), F32),
        in_specs=[VMEM] * 3,
        out_specs=VMEM,
        name="pack",
    )(*arrays)


def loewner(half, root, poles, out):
    columns = poles.T
    total = jnp.zeros((8, WIDE), F32)
    for r in range(8):
        at = 8 * r + half
        value = columns[0:64, at + 2 : at + 3] / (columns[0:64, at : at + 1] - root)
        high = value.astype(BF16)
        rows = slice(r * 64, r * 64 + 64)
        out[0, rows, :] = high
        out[1, rows, :] = (value - high.astype(F32)).astype(BF16)
        total = total + jnp.sum((value * value).reshape(8, 8, WIDE), axis=0)
    return total


COEFFICIENT = jax.ShapeDtypeStruct((2, WIDE, WIDE), BF16)
SQUARES = jax.ShapeDtypeStruct((8, WIDE), F32)


def own_loewner_kernel(roots, poles, upper, lower, upper_squares, lower_squares):
    upper_squares[...] = loewner(0, roots[...], poles[...], upper)
    lower_squares[...] = loewner(1, roots[...], poles[...], lower)


def own_loewner(roots, poles):
    return pl.pallas_call(
        own_loewner_kernel,
        out_shape=[COEFFICIENT, COEFFICIENT, SQUARES, SQUARES],
        in_specs=[VMEM] * 2,
        out_specs=[VMEM] * 4,
        compiler_params=KERNEL,
        cost_estimate=pl.CostEstimate(flops=1 << 23, bytes_accessed=2 << 20, transcendentals=1 << 19),
        name="loewner",
    )(roots, poles)


def product(vectors, high, low):
    a = vectors.astype(BF16)
    rest = (vectors - a.astype(F32)).astype(BF16)
    dot = functools.partial(jnp.dot, preferred_element_type=F32)
    return dot(a, high) + (dot(a, low) + dot(rest, high))


def own_kernel(vectors, coefficient, out):
    for k in range(0, 16 * ROWS, 256):
        out[k : k + 256, :] = product(vectors[k : k + 256, :], coefficient[0], coefficient[1])


def own_products(vectors, coefficient, name):
    return pl.pallas_call(
        own_kernel,
        out_shape=jax.ShapeDtypeStruct((16 * ROWS, WIDE), F32),
        in_specs=[VMEM] * 2,
        out_specs=VMEM,
        compiler_params=KERNEL,
        cost_estimate=pl.CostEstimate(flops=3 << 30, bytes_accessed=6 << 20, transcendentals=0),
        name=name,
    )(vectors, coefficient)


def meet_kernel(stream, roots, poles, vectors, own, squares, send, coefficient, sums):
    total = squares[...] + loewner(stream, roots[...], poles[...], coefficient)
    for k in range(0, 8 * ROWS, 256):
        rows = slice(8 * ROWS + k, 8 * ROWS + k + 256)
        send[k : k + 256, :] = own[rows, :] + product(
            vectors[rows, :], coefficient[0], coefficient[1]
        )
    send[8 * ROWS :, :] = total
    sums[...] = total


def meet(stream, *arrays):
    return pl.pallas_call(
        functools.partial(meet_kernel, stream),
        out_shape=[jax.ShapeDtypeStruct((8 * ROWS + 8, WIDE), F32), COEFFICIENT, SQUARES],
        in_specs=[VMEM] * 5,
        out_specs=[VMEM] * 3,
        compiler_params=KERNEL,
        cost_estimate=pl.CostEstimate(flops=3 << 29, bytes_accessed=6 << 20, transcendentals=0),
        name=f"meet_{stream}",
    )(*arrays)


def rest_kernel(vectors, coefficient, own, out):
    for k in range(0, 8 * ROWS, 256):
        rows = slice(k, k + 256)
        out[rows, :] = own[rows, :] + product(vectors[rows, :], coefficient[0], coefficient[1])


def rest(stream, *arrays):
    return pl.pallas_call(
        rest_kernel,
        out_shape=jax.ShapeDtypeStruct((8 * ROWS, WIDE), F32),
        in_specs=[VMEM] * 3,
        out_specs=VMEM,
        compiler_params=KERNEL,
        cost_estimate=pl.CostEstimate(flops=3 << 29, bytes_accessed=6 << 20, transcendentals=0),
        name=f"rest_{stream}",
    )(*arrays)


def add_kernel(half, kept, arrived, squares, send, keep, sums):
    send[:half, :] = kept[half:, :] + arrived[half : 2 * half, :]
    total = squares[...] + arrived[2 * half :, :]
    send[half:, :] = total
    sums[...] = total
    keep[...] = kept[:half, :] + arrived[:half, :]


def add(half, kept, arrived, squares, name):
    return pl.pallas_call(
        functools.partial(add_kernel, half),
        out_shape=[
            jax.ShapeDtypeStruct((half + 8, WIDE), F32),
            jax.ShapeDtypeStruct((half, WIDE), F32),
            jax.ShapeDtypeStruct((8, WIDE), F32),
        ],
        in_specs=[VMEM] * 3,
        out_specs=[VMEM] * 3,
        compiler_params=KERNEL,
        name=name,
    )(kept, arrived, squares)


def finish_kernel(upper, lower, to_upper, to_lower, upper_squares, lower_squares, out):
    squares = upper_squares[...] + lower_squares[...] + to_upper[ROWS:, :] + to_lower[ROWS:, :]
    norm = jnp.sqrt(jnp.sum(squares, axis=0, keepdims=True))
    out[:, 0, :] = (upper[...] + to_upper[:ROWS, :]) / norm
    out[:, 1, :] = (lower[...] + to_lower[:ROWS, :]) / norm


def local(upper_vectors, lower_vectors, secular_roots, pole_values, pole_weights, undeflated):
    vectors = [pltpu.with_memory_space_constraint(v, pltpu.HBM) for v in (upper_vectors, lower_vectors)]
    roots = secular_roots.reshape(1, WIDE)
    sent = [pick(vectors[s], s, 16) for s in (0, 1)]
    packed = pack(pole_values, pole_weights, undeflated)
    *sent, packed = lax.optimization_barrier((*sent, packed))
    arrived = [exchange(sent[s], s, 0) for s in (0, 1)]
    poles = lax.all_gather(packed, "row", axis=0, tiled=True)
    met = [exchange(poles, s, 0) for s in (0, 1)]
    mine = [pick(vectors[s], s, 0) for s in (0, 1)]
    *coefficients, upper_squares, lower_squares = own_loewner(roots, poles)
    squares = [upper_squares, lower_squares]
    own = [own_products(mine[s], coefficients[s], f"own_{s}") for s in (0, 1)]
    send, keep = [None] * 2, [None] * 2
    for s in (0, 1):
        send[s], coefficients[s], squares[s] = meet(s, roots, met[s], arrived[s], own[s], squares[s])
    for s in (0, 1):
        keep[s] = rest(s, arrived[s], coefficients[s], own[s])
    for phase in (1, 2, 3):
        half = ROWS << (3 - phase)
        for s in (0, 1):
            arrived[s] = exchange(send[s], s, phase)
        for s in (0, 1):
            send[s], keep[s], squares[s] = add(half, keep[s], arrived[s], squares[s], f"add_{phase}_{s}")
    arrived = [exchange(send[s], s, 4) for s in (0, 1)]
    return pl.pallas_call(
        finish_kernel,
        out_shape=jax.ShapeDtypeStruct((ROWS, 2, WIDE), F32),
        in_specs=[VMEM] * 6,
        out_specs=VMEM,
        compiler_params=KERNEL,
        name="finish",
    )(*keep, *arrived, *squares)


def solution(mesh):
    return jax.shard_map(
        local,
        mesh=mesh,
        in_specs=(
            P("row", "col"),
            P("row", "col"),
            P(),
            P(None, ("col", "row")),
            P(None, ("col", "row")),
            P(None, ("col", "row")),
        ),
        out_specs=P(("row", "col"), None, None),
        check_vma=False,
    )
```

time: 368 us -> 92.2 us (0.25)
  the two profiles are of different devices: /device:TPU:2 before, /device:TPU:20 now
where the time goes in v1:
time: 92.2 us; the launch traced here: 92 us
  starting transfers between devices  32.2 us (35%)
  waiting for transfers between devices  24.9 us (27%)
  Pallas kernels  18.6 us (20%)
  blocking collectives  14.7 us (16%)
  local copies, waits for them, and re-layouts  1.32 us (1%)
    ppermute x12, starting transfers between devices, exchange(): return lax.ppermute(block, ('row', 'col'), PARTNERS[stream][phase])  32.2 us
    ppermute x12, waiting for transfers between devices, exchange(): return lax.ppermute(block, ('row', 'col'), PARTNERS[stream][phase])  24.9 us
    all_gather x1, blocking collectives, local(): poles = lax.all_gather(packed, 'row', axis=0, tiled=True)  14.7 us
    pallas_call x4, Pallas kernels, pick(): pl.pallas_call(functools.partial(pick_kernel, stream, first), out_shape=j...  6.98 us
    pallas_call x2, Pallas kernels, own_products(): pl.pallas_call(own_kernel, out_shape=jax.ShapeDtypeStruct((16 * ROWS, WID...  3.59 us
    pallas_call x2, Pallas kernels, meet(): pl.pallas_call(functools.partial(meet_kernel, stream), out_shape=[jax.Sha...  2.76 us
    pallas_call x2, Pallas kernels, rest(): pl.pallas_call(rest_kernel, out_shape=jax.ShapeDtypeStruct((8 * ROWS, WID...  1.98 us
  transfers between devices with their start and end apart: 12, of which 6 were waited for; matrix products, arithmetic and copies ran while one was open for 0% of the time, Pallas kernels for 14%

profile of v1, /device:TPU:20, one launch (start us, length us, event | category | flops | bytes accessed | tf_op | source)
XLA Modules:
  0.0 92.0 jit_solution(5599155349449457734)
XLA Ops:
  0.0 1.7 %pick_upper_send.1 = f32[1024,512]{1,0:T(8,128)S(1)} custom-call(f32[2048,512]{1,0:T(8,128)} %vectors.6), custom_call_target="tpu_custom_call" | custom-call | bytes 4194304 | tf_op jit(solution)/shard_map/pick_upper_send/pallas_call | solution.py:111
  1.7 1.8 %pick_lower_send.1 = f32[1024,512]{1,0:T(8,128)S(1)} custom-call(f32[2048,512]{1,0:T(8,128)} %vectors.7), custom_call_target="tpu_custom_call" | custom-call | bytes 4194304 | tf_op jit(solution)/shard_map/pick_lower_send/pallas_call | solution.py:111
  3.5 1.3 %copy-done = f32[1024,512]{1,0:T(8,128)} copy-done((f32[1024,512]{1,0:T(8,128)}, f32[1024,512]{1,0:T(8,128)S(1)}, u32[]{:S(2)}) %copy-start) | copy-done | bytes 2097176
  4.8 1.3 %pack.1 = f32[8,128]{1,0:T(8,128)} custom-call(f32[2,64]{1,0:T(2,128)} %poles.1, f32[2,64]{1,0:T(2,128)} %weights.1, s32[2,64]{1,0:T(2,128)} %undeflated.1), custom_call_target="tpu_custom_call" | custom-call | tf_op jit(solution)/shard_map/pack/pallas_call | solution.py:130
  6.1 0.5 collective-permute-start.5
  6.7 1.1 %collective-permute-start = (f32[1024,512]{1,0:T(8,128)S(1)}, f32[1024,512]{1,0:T(8,128)S(1)}, u32[]{:S(2)}, u32[]{:S(2)}) collective-permute-start(f32[1024,512]{1,0:T(8,128)S(1)} %pick_upper_send.1), channel_id=1, source_target_pairs={{0,1},{1,0},{2,3},{3,2},{4,5},{5,4},{6,7},{7,6},{8,9},{9,8},{10,11... | collective-permute-start | bytes 6291464 | tf_op jit(solution)/shard_map/ppermute | solution.py:67
  7.8 14.7 %all_gather.3.poles = f32[64,128]{1,0:T(8,128)S(1)} all-gather(f32[8,128]{1,0:T(8,128)} %pack.1), channel_id=1, replica_groups=mesh['row'=8,'col'=32] {'row'}, dimensions={0}, use_global_device_ids=true | all-gather | bytes 36864 | tf_op jit(solution)/shard_map/all_gather | solution.py:276
  22.6 0.5 collective-permute-start.6
  23.1 1.1 %collective-permute-start.1 = (f32[64,128]{1,0:T(8,128)S(1)}, f32[64,128]{1,0:T(8,128)S(1)}, u32[]{:S(2)}, u32[]{:S(2)}) collective-permute-start(f32[64,128]{1,0:T(8,128)S(1)} %all_gather.3.poles), channel_id=1, source_target_pairs={{0,1},{1,0},{2,3},{3,2},{4,5},{5,4},{6,7},{7,6},{8,9},{9,8},{10,11... | collective-permute-start | bytes 98312 | tf_op jit(solution)/shard_map/ppermute | solution.py:67
  24.2 1.7 %pick_lower_keep.1.vectors = f32[1024,512]{1,0:T(8,128)S(1)} custom-call(f32[2048,512]{1,0:T(8,128)} %vectors.7), custom_call_target="tpu_custom_call" | custom-call | bytes 4194304 | tf_op jit(solution)/shard_map/pick_lower_keep/pallas_call | solution.py:111
  26.0 0.8 loewner.1
  26.8 1.8 %own_1.1.own = f32[1024,512]{1,0:T(8,128)S(1)} custom-call(f32[1024,512]{1,0:T(8,128)S(1)} %pick_lower_keep.1.vectors, bf16[2,512,512]{2,1,0:T(8,128)(2,1)S(1)} %get-tuple-element.51.coefficient), custom_call_target="tpu_custom_call" | custom-call | flops 3221225472 | bytes 6291456 | tf_op jit(solution)/shard_map/own_1/pallas_call | solution.py:187
  28.6 1.8 %pick_upper_keep.1.vectors = f32[1024,512]{1,0:T(8,128)S(1)} custom-call(f32[2048,512]{1,0:T(8,128)} %vectors.6), custom_call_target="tpu_custom_call" | custom-call | bytes 4194304 | tf_op jit(solution)/shard_map/pick_upper_keep/pallas_call | solution.py:111
  30.3 2.4 %collective-permute-done.6.poles = f32[64,128]{1,0:T(8,128)S(1)} collective-permute-done((f32[64,128]{1,0:T(8,128)S(1)}, f32[64,128]{1,0:T(8,128)S(1)}, u32[]{:S(2)}, u32[]{:S(2)}) %collective-permute-start.6) | collective-permute-done | bytes 32800 | tf_op jit(solution)/shard_map/ppermute | solution.py:67
  32.7 1.4 %meet_1.1 = (f32[520,512]{1,0:T(8,128)S(1)}, bf16[2,512,512]{2,1,0:T(8,128)(2,1)S(1)}, f32[8,512]{1,0:T(8,128)S(1)}) custom-call(f32[1,512]{1,0:T(1,128)S(1)} %bitcast.2, f32[64,128]{1,0:T(8,128)S(1)} %collective-permute-done.6.poles, f32[1024,512]{1,0:T(8,128)S(1)} %collective-permute-done.5.vectors, f32[1024,512]{1,0:T(8,128)S(1)} %own_1.1.own, ...), custom_call_target="tpu_custom_call" | custom-call | flops 1610612736 | bytes 6291456 | tf_op jit(solution)/shard_map/meet_1/pallas_call | solution.py:210
  34.1 2.5 %collective-permute-start.7 = (f32[520,512]{1,0:T(8,128)S(1)}, f32[520,512]{1,0:T(8,128)S(1)}, u32[]{:S(2)}, u32[]{:S(2)}) collective-permute-start(f32[520,512]{1,0:T(8,128)S(1)} %get-tuple-element.54), channel_id=1, source_target_pairs={{0,1},{1,0},{2,3},{3,2},{4,5},{5,4},{6,7},{7,6},{8,9},{9,8},{10,11... | collective-permute-start | bytes 3194888 | tf_op jit(solution)/shard_map/ppermute | solution.py:67
  36.6 1.8 %own_0.1.own = f32[1024,512]{1,0:T(8,128)S(1)} custom-call(f32[1024,512]{1,0:T(8,128)S(1)} %pick_upper_keep.1.vectors, bf16[2,512,512]{2,1,0:T(8,128)(2,1)S(1)} %get-tuple-element.38.coefficient), custom_call_target="tpu_custom_call" | custom-call | flops 3221225472 | bytes 6291456 | tf_op jit(solution)/shard_map/own_0/pallas_call | solution.py:187
  38.5 1.4 %meet_0.1 = (f32[520,512]{1,0:T(8,128)S(1)}, bf16[2,512,512]{2,1,0:T(8,128)(2,1)S(1)}, f32[8,512]{1,0:T(8,128)S(1)}) custom-call(f32[1,512]{1,0:T(1,128)S(1)} %bitcast.3, f32[64,128]{1,0:T(8,128)S(1)} %collective-permute-done.1.poles, f32[1024,512]{1,0:T(8,128)S(1)} %collective-permute-done.vectors, f32[1024,512]{1,0:T(8,128)S(1)} %own_0.1.own, ...), custom_call_target="tpu_custom_call" | custom-call | flops 1610612736 | bytes 6291456 | tf_op jit(solution)/shard_map/meet_0/pallas_call | solution.py:210
  39.9 1.0 %rest_1.1.kept = f32[512,512]{1,0:T(8,128)S(1)} custom-call(f32[1024,512]{1,0:T(8,128)S(1)} %collective-permute-done.5.vectors, bf16[2,512,512]{2,1,0:T(8,128)(2,1)S(1)} %get-tuple-element.53.coefficient, f32[1024,512]{1,0:T(8,128)S(1)} %own_1.1.own), custom_call_target="tpu_custom_call" | custom-call | flops 1610612736 | bytes 6291456 | tf_op jit(solution)/shard_map/rest_1/pallas_call | solution.py:228
  40.9 8.6 %collective-permute-done.7.arrived = f32[520,512]{1,0:T(8,128)S(1)} collective-permute-done((f32[520,512]{1,0:T(8,128)S(1)}, f32[520,512]{1,0:T(8,128)S(1)}, u32[]{:S(2)}, u32[]{:S(2)}) %collective-permute-start.7) | collective-permute-done | bytes 1064992 | tf_op jit(solution)/shard_map/ppermute | solution.py:67
  49.7 5.9 %collective-permute-start.8 = (f32[264,512]{1,0:T(8,128)S(1)}, f32[264,512]{1,0:T(8,128)S(1)}, u32[]{:S(2)}, u32[]{:S(2)}) collective-permute-start(f32[264,512]{1,0:T(8,128)S(1)} %get-tuple-element.57), channel_id=1, source_target_pairs={{0,28},{1,29},{2,30},{3,31},{4,8},{5,9},{6,10},{7,11},{8,4},{9,5},... | collective-permute-start | bytes 1622024 | tf_op jit(solution)/shard_map/ppermute | solution.py:67
  55.6 1.0 %rest_0.1.kept = f32[512,512]{1,0:T(8,128)S(1)} custom-call(f32[1024,512]{1,0:T(8,128)S(1)} %collective-permute-done.vectors, bf16[2,512,512]{2,1,0:T(8,128)(2,1)S(1)} %get-tuple-element.40.coefficient, f32[1024,512]{1,0:T(8,128)S(1)} %own_0.1.own), custom_call_target="tpu_custom_call" | custom-call | flops 1610612736 | bytes 6291456 | tf_op jit(solution)/shard_map/rest_0/pallas_call | solution.py:228
  56.6 0.1 add_1_0.1
  56.8 3.0 %collective-permute-start.3 = (f32[264,512]{1,0:T(8,128)S(1)}, f32[264,512]{1,0:T(8,128)S(1)}, u32[]{:S(2)}, u32[]{:S(2)}) collective-permute-start(f32[264,512]{1,0:T(8,128)S(1)} %get-tuple-element.44), channel_id=1, source_target_pairs={{0,4},{1,5},{2,6},{3,7},{4,0},{5,1},{6,2},{7,3},{8,12},{9,13},{10,... | collective-permute-start | bytes 1622024 | tf_op jit(solution)/shard_map/ppermute | solution.py:67
  59.7 3.2 %collective-permute-done.8.arrived = f32[264,512]{1,0:T(8,128)S(1)} collective-permute-done((f32[264,512]{1,0:T(8,128)S(1)}, f32[264,512]{1,0:T(8,128)S(1)}, u32[]{:S(2)}, u32[]{:S(2)}) %collective-permute-start.8) | collective-permute-done | bytes 540704 | tf_op jit(solution)/shard_map/ppermute | solution.py:67
  63.1 3.9 %collective-permute-done.3.arrived = f32[264,512]{1,0:T(8,128)S(1)} collective-permute-done((f32[264,512]{1,0:T(8,128)S(1)}, f32[264,512]{1,0:T(8,128)S(1)}, u32[]{:S(2)}, u32[]{:S(2)}) %collective-permute-start.3) | collective-permute-done | bytes 540704 | tf_op jit(solution)/shard_map/ppermute | solution.py:67
  67.1 7.3 %collective-permute-start.4 = (f32[136,512]{1,0:T(8,128)S(1)}, f32[136,512]{1,0:T(8,128)S(1)}, u32[]{:S(2)}, u32[]{:S(2)}) collective-permute-start(f32[136,512]{1,0:T(8,128)S(1)} %get-tuple-element.47), channel_id=1, source_target_pairs={{0,28},{1,29},{2,30},{3,31},{4,8},{5,9},{6,10},{7,11},{8,4},{9,5},... | collective-permute-start | bytes 835592 | tf_op jit(solution)/shard_map/ppermute | solution.py:67
  74.5 8.0 %collective-permute-start.11 = (f32[72,512]{1,0:T(8,128)S(1)}, f32[72,512]{1,0:T(8,128)S(1)}, u32[]{:S(2)}, u32[]{:S(2)}) collective-permute-start(f32[72,512]{1,0:T(8,128)S(1)} %get-tuple-element.64), channel_id=1, source_target_pairs={{0,20},{1,21},{2,22},{3,23},{4,16},{5,17},{6,18},{7,19},{8,28},{9,... | collective-permute-start | bytes 442376 | tf_op jit(solution)/shard_map/ppermute | solution.py:67
  82.6 1.9 %collective-permute-start.10 = (f32[72,512]{1,0:T(8,128)S(1)}, f32[72,512]{1,0:T(8,128)S(1)}, u32[]{:S(2)}, u32[]{:S(2)}) collective-permute-start(f32[72,512]{1,0:T(8,128)S(1)} %get-tuple-element.63), channel_id=1, source_target_pairs={{0,12},{1,13},{2,14},{3,15},{4,24},{5,25},{6,26},{7,27},{8,20},{9,... | collective-permute-start | bytes 442376 | tf_op jit(solution)/shard_map/ppermute | solution.py:67
  84.5 2.1 %collective-permute-done.11.to_lower = f32[72,512]{1,0:T(8,128)S(1)} collective-permute-done((f32[72,512]{1,0:T(8,128)S(1)}, f32[72,512]{1,0:T(8,128)S(1)}, u32[]{:S(2)}, u32[]{:S(2)}) %collective-permute-start.11) | collective-permute-done | bytes 147488 | tf_op jit(solution)/shard_map/ppermute | solution.py:67
  86.6 4.6 %collective-permute-done.10.to_upper = f32[72,512]{1,0:T(8,128)S(1)} collective-permute-done((f32[72,512]{1,0:T(8,128)S(1)}, f32[72,512]{1,0:T(8,128)S(1)}, u32[]{:S(2)}, u32[]{:S(2)}) %collective-permute-start.10) | collective-permute-done | bytes 147488 | tf_op jit(solution)/shard_map/ppermute | solution.py:67
  91.2 0.8 finish.1
  (16 shorter events, 0.5 us)
Async XLA Ops:
  3.5 1.3 %copy-start = (f32[1024,512]{1,0:T(8,128)}, f32[1024,512]{1,0:T(8,128)S(1)}, u32[]{:S(2)}) copy-start(f32[1024,512]{1,0:T(8,128)S(1)} %pick_lower_send.1) | copy-start | bytes 6291460
  6.1 26.6 %collective-permute-start.5 = (f32[1024,512]{1,0:T(8,128)}, f32[1024,512]{1,0:T(8,128)S(1)}, u32[]{:S(2)}, u32[]{:S(2)}) collective-permute-start(f32[1024,512]{1,0:T(8,128)} %copy-done), channel_id=1, source_target_pairs={{0,3},{1,2},{2,1},{3,0},{4,7},{5,6},{6,5},{7,4},{8,11},{9,10},{10,... | collective-permute-start | bytes 6291464 | tf_op jit(solution)/shard_map/ppermute | solution.py:67
  6.7 31.8 %collective-permute-start = (f32[1024,512]{1,0:T(8,128)S(1)}, f32[1024,512]{1,0:T(8,128)S(1)}, u32[]{:S(2)}, u32[]{:S(2)}) collective-permute-start(f32[1024,512]{1,0:T(8,128)S(1)} %pick_upper_send.1), channel_id=1, source_target_pairs={{0,1},{1,0},{2,3},{3,2},{4,5},{5,4},{6,7},{7,6},{8,9},{9,8},{10,11... | collective-permute-start | bytes 6291464 | tf_op jit(solution)/shard_map/ppermute | solution.py:67
  22.6 3.4 %copy-start.1 = (f32[512]{0:T(512)S(1)}, f32[512]{0:T(512)}, u32[]{:S(2)}) copy-start(f32[512]{0:T(512)} %param.8) | copy-start | bytes 6148
  22.6 10.2 %collective-permute-start.6 = (f32[64,128]{1,0:T(8,128)S(1)}, f32[64,128]{1,0:T(8,128)S(1)}, u32[]{:S(2)}, u32[]{:S(2)}) collective-permute-start(f32[64,128]{1,0:T(8,128)S(1)} %all_gather.3.poles), channel_id=1, source_target_pairs={{0,3},{1,2},{2,1},{3,0},{4,7},{5,6},{6,5},{7,4},{8,11},{9,10},{10,... | collective-permute-start | bytes 98312 | tf_op jit(solution)/shard_map/ppermute | solution.py:67
  23.1 15.3 %collective-permute-start.1 = (f32[64,128]{1,0:T(8,128)S(1)}, f32[64,128]{1,0:T(8,128)S(1)}, u32[]{:S(2)}, u32[]{:S(2)}) collective-permute-start(f32[64,128]{1,0:T(8,128)S(1)} %all_gather.3.poles), channel_id=1, source_target_pairs={{0,1},{1,0},{2,3},{3,2},{4,5},{5,4},{6,7},{7,6},{8,9},{9,8},{10,11... | collective-permute-start | bytes 98312 | tf_op jit(solution)/shard_map/ppermute | solution.py:67
  34.1 15.4 %collective-permute-start.7 = (f32[520,512]{1,0:T(8,128)S(1)}, f32[520,512]{1,0:T(8,128)S(1)}, u32[]{:S(2)}, u32[]{:S(2)}) collective-permute-start(f32[520,512]{1,0:T(8,128)S(1)} %get-tuple-element.54), channel_id=1, source_target_pairs={{0,1},{1,0},{2,3},{3,2},{4,5},{5,4},{6,7},{7,6},{8,9},{9,8},{10,11... | collective-permute-start | bytes 3194888 | tf_op jit(solution)/shard_map/ppermute | solution.py:67
  39.8 16.8 %collective-permute-start.2 = (f32[520,512]{1,0:T(8,128)S(1)}, f32[520,512]{1,0:T(8,128)S(1)}, u32[]{:S(2)}, u32[]{:S(2)}) collective-permute-start(f32[520,512]{1,0:T(8,128)S(1)} %get-tuple-element.41), channel_id=1, source_target_pairs={{0,3},{1,2},{2,1},{3,0},{4,7},{5,6},{6,5},{7,4},{8,11},{9,10},{10,... | collective-permute-start | bytes 3194888 | tf_op jit(solution)/shard_map/ppermute | solution.py:67
  49.7 13.3 %collective-permute-start.8 = (f32[264,512]{1,0:T(8,128)S(1)}, f32[264,512]{1,0:T(8,128)S(1)}, u32[]{:S(2)}, u32[]{:S(2)}) collective-permute-start(f32[264,512]{1,0:T(8,128)S(1)} %get-tuple-element.57), channel_id=1, source_target_pairs={{0,28},{1,29},{2,30},{3,31},{4,8},{5,9},{6,10},{7,11},{8,4},{9,5},... | collective-permute-start | bytes 1622024 | tf_op jit(solution)/shard_map/ppermute | solution.py:67
  56.8 10.3 %collective-permute-start.3 = (f32[264,512]{1,0:T(8,128)S(1)}, f32[264,512]{1,0:T(8,128)S(1)}, u32[]{:S(2)}, u32[]{:S(2)}) collective-permute-start(f32[264,512]{1,0:T(8,128)S(1)} %get-tuple-element.44), channel_id=1, source_target_pairs={{0,4},{1,5},{2,6},{3,7},{4,0},{5,1},{6,2},{7,3},{8,12},{9,13},{10,... | collective-permute-start | bytes 1622024 | tf_op jit(solution)/shard_map/ppermute | solution.py:67
  63.0 11.4 %collective-permute-start.9 = (f32[136,512]{1,0:T(8,128)S(1)}, f32[136,512]{1,0:T(8,128)S(1)}, u32[]{:S(2)}, u32[]{:S(2)}) collective-permute-start(f32[136,512]{1,0:T(8,128)S(1)} %get-tuple-element.60), channel_id=1, source_target_pairs={{0,4},{1,5},{2,6},{3,7},{4,0},{5,1},{6,2},{7,3},{8,12},{9,13},{10,... | collective-permute-start | bytes 835592 | tf_op jit(solution)/shard_map/ppermute | solution.py:67
  67.1 15.4 %collective-permute-start.4 = (f32[136,512]{1,0:T(8,128)S(1)}, f32[136,512]{1,0:T(8,128)S(1)}, u32[]{:S(2)}, u32[]{:S(2)}) collective-permute-start(f32[136,512]{1,0:T(8,128)S(1)} %get-tuple-element.47), channel_id=1, source_target_pairs={{0,28},{1,29},{2,30},{3,31},{4,8},{5,9},{6,10},{7,11},{8,4},{9,5},... | collective-permute-start | bytes 835592 | tf_op jit(solution)/shard_map/ppermute | solution.py:67
  74.5 12.1 %collective-permute-start.11 = (f32[72,512]{1,0:T(8,128)S(1)}, f32[72,512]{1,0:T(8,128)S(1)}, u32[]{:S(2)}, u32[]{:S(2)}) collective-permute-start(f32[72,512]{1,0:T(8,128)S(1)} %get-tuple-element.64), channel_id=1, source_target_pairs={{0,20},{1,21},{2,22},{3,23},{4,16},{5,17},{6,18},{7,19},{8,28},{9,... | collective-permute-start | bytes 442376 | tf_op jit(solution)/shard_map/ppermute | solution.py:67
  82.6 8.6 %collective-permute-start.10 = (f32[72,512]{1,0:T(8,128)S(1)}, f32[72,512]{1,0:T(8,128)S(1)}, u32[]{:S(2)}, u32[]{:S(2)}) collective-permute-start(f32[72,512]{1,0:T(8,128)S(1)} %get-tuple-element.63), channel_id=1, source_target_pairs={{0,12},{1,13},{2,14},{3,15},{4,24},{5,25},{6,26},{7,27},{8,20},{9,... | collective-permute-start | bytes 442376 | tf_op jit(solution)/shard_map/ppermute | solution.py:67

commit v2 on v1

v2 whole, which is shorter than its diff:
```python
import functools

import jax
import jax.numpy as jnp
from jax import lax
from jax.experimental import pallas as pl
from jax.experimental.pallas import tpu as pltpu
from jax.sharding import PartitionSpec as P

F32 = jnp.float32
BF16 = jnp.bfloat16
ROWS = 64
PART = 32
WIDE = 512
HBM = pl.BlockSpec(memory_space=pltpu.HBM)
VMEM = pl.BlockSpec(memory_space=pltpu.VMEM)
KERNEL = pltpu.CompilerParams(vmem_limit_bytes=16 << 20)


def pair_e(x):
    return x ^ 1


def pair_f(x):
    return (((x + 1) ^ 1) + 3) & 3


def pair_a(z):
    return z ^ 1


def pair_b(z):
    return (((z + 1) ^ 1) + 7) & 7


def pair_c(z):
    return (11 + 4 * (((z + 1) >> 1) & 1) - z) & 7


def pair_d(z):
    return (13 - 4 * ((z >> 1) & 1) - z) & 7


STEPS = (
    (
        (("z", pair_a), ("z", pair_b), ("x", pair_f), ("x", pair_e), ("z", pair_c)),
        (("z", pair_b), ("z", pair_a), ("x", pair_e), ("x", pair_f), ("z", pair_d)),
    ),
    (
        (("x", pair_e), ("x", pair_f), ("z", pair_a), ("z", pair_b), ("z", pair_c)),
        (("x", pair_f), ("x", pair_e), ("z", pair_b), ("z", pair_a), ("z", pair_d)),
    ),
)


def partners(stream, phase):
    pairs = []
    for row in range(8):
        for col in range(32):
            axis, pair = STEPS[stream][row % 2][phase]
            z, x = divmod(col, 4)
            to = z * 4 + pair(x) if axis == "x" else pair(z) * 4 + x
            pairs.append((row * 32 + col, row * 32 + to))
    return pairs


PARTNERS = tuple(tuple(partners(stream, phase) for phase in range(5)) for stream in range(2))


def exchange(block, stream, phase):
    return lax.ppermute(block, ("row", "col"), PARTNERS[stream][phase])


def chunk_order(stream, count, first):
    core = lax.axis_index("row") & 1
    col = lax.axis_index("col")
    known = {}

    def place(side, axis, bits):
        key = (side, axis, bits)
        if key not in known:
            if not bits:
                known[key] = (col >> 2) if axis == "z" else (col & 3)
            else:
                pairs = [pair for on, pair in STEPS[stream][side] if on == axis]
                before = place(side, axis, bits[:-1])
                known[key] = pairs[len(bits) - 1](before) if bits[-1] else before
        return known[key]

    order = []
    for k in range(first, first + count):
        taken = [(k >> shift) & 1 for shift in (4, 3, 2, 1, 0)]
        on = []
        for side in (0, 1):
            bits = {
                axis: tuple(bit for bit, (at, _) in zip(taken, STEPS[stream][side]) if at == axis)
                for axis in ("x", "z")
            }
            on.append(place(side, "z", bits["z"]) * 4 + place(side, "x", bits["x"]))
        order.append(jnp.where(core == 0, on[0], on[1]))
    return order


def copy_rows(stream, first, vectors, out, sems):
    order = chunk_order(stream, 16, first)
    copies = []
    for n in range(32):
        batch, k = divmod(n, 16)
        at = pl.multiple_of(order[k] * ROWS + batch * PART, PART)
        copies.append(
            pltpu.make_async_copy(
                vectors.at[pl.ds(at, PART), :], out.at[pl.ds(n * PART, PART), :], sems.at[n]
            )
        )
    return copies


def pick_upper_kernel(vectors, out, rows, sems):
    arriving = copy_rows(0, 16, vectors, rows, sems.at[0])
    for copy in arriving:
        copy.start()
    leaving = []
    for k, copy in enumerate(arriving):
        copy.wait()
        at = pl.ds(k * PART, PART)
        leaving.append(pltpu.make_async_copy(rows.at[at, :], out.at[at, :], sems.at[1, k]))
        leaving[k].start()
    for copy in leaving:
        copy.wait()


def pick_lower_kernel(vectors, out, sems):
    copies = copy_rows(1, 16, vectors, out, sems)
    for copy in copies:
        copy.start()
    for copy in copies:
        copy.wait()


def pick_upper(vectors):
    return pl.pallas_call(
        pick_upper_kernel,
        out_shape=jax.ShapeDtypeStruct((16 * ROWS, WIDE), F32),
        in_specs=[HBM],
        out_specs=HBM,
        scratch_shapes=[pltpu.VMEM((16 * ROWS, WIDE), F32), pltpu.SemaphoreType.DMA((2, 32))],
        compiler_params=pltpu.CompilerParams(vmem_limit_bytes=4 << 20),
        cost_estimate=pl.CostEstimate(flops=0, bytes_accessed=4 << 20, transcendentals=0),
        name="pick_upper",
    )(vectors)


def pick_lower(vectors):
    return pl.pallas_call(
        pick_lower_kernel,
        out_shape=jax.ShapeDtypeStruct((16 * ROWS, WIDE), F32),
        in_specs=[HBM],
        out_specs=VMEM,
        scratch_shapes=[pltpu.SemaphoreType.DMA((32,))],
        compiler_params=pltpu.CompilerParams(vmem_limit_bytes=4 << 20),
        cost_estimate=pl.CostEstimate(flops=0, bytes_accessed=4 << 20, transcendentals=0),
        name="pick_lower",
    )(vectors)


def pack_kernel(poles, weights, undeflated, out):
    out[...] = jnp.zeros_like(out)
    scaled = weights[...] * undeflated[...].astype(F32)
    for r in range(8):
        out[8 * r : 8 * r + 2, 0:64] = poles[...]
        out[8 * r + 2 : 8 * r + 4, 0:64] = scaled


def pack(*arrays):
    return pl.pallas_call(
        pack_kernel,
        out_shape=jax.ShapeDtypeStruct((64, 128), F32),
        in_specs=[VMEM] * 3,
        out_specs=VMEM,
        name="pack",
    )(*arrays)


def loewner(half, root, poles, out):
    columns = poles.T
    total = jnp.zeros((8, WIDE), F32)
    for r in range(8):
        at = 8 * r + half
        value = columns[0:64, at + 2 : at + 3] / (columns[0:64, at : at + 1] - root)
        high = value.astype(BF16)
        rows = slice(r * 64, r * 64 + 64)
        out[0, rows, :] = high
        out[1, rows, :] = (value - high.astype(F32)).astype(BF16)
        total = total + jnp.sum((value * value).reshape(8, 8, WIDE), axis=0)
    return total


COEFFICIENT = jax.ShapeDtypeStruct((2, WIDE, WIDE), BF16)
SQUARES = jax.ShapeDtypeStruct((8, WIDE), F32)


def own_loewner_kernel(roots, poles, upper, lower, upper_squares, lower_squares):
    upper_squares[...] = loewner(0, roots[...], poles[...], upper)
    lower_squares[...] = loewner(1, roots[...], poles[...], lower)


def own_loewner(roots, poles):
    return pl.pallas_call(
        own_loewner_kernel,
        out_shape=[COEFFICIENT, COEFFICIENT, SQUARES, SQUARES],
        in_specs=[VMEM] * 2,
        out_specs=[VMEM] * 4,
        compiler_params=KERNEL,
        cost_estimate=pl.CostEstimate(flops=1 << 23, bytes_accessed=2 << 20, transcendentals=1 << 19),
        name="loewner",
    )(roots, poles)


def product(vectors, high, low):
    a = vectors.astype(BF16)
    rest = (vectors - a.astype(F32)).astype(BF16)
    dot = functools.partial(jnp.dot, preferred_element_type=F32)
    return dot(a, high) + (dot(a, low) + dot(rest, high))


def own_kernel(upper, lower, upper_part, lower_part, upper_out, lower_out, rows, sems):
    streams = ((upper, upper_part, upper_out), (lower, lower_part, lower_out))
    copies = [copy_rows(s, 0, streams[s][0], rows.at[s], sems.at[s]) for s in (0, 1)]
    for copy in copies[0] + copies[1]:
        copy.start()
    for s, (_, part, out) in enumerate(streams):
        for k in range(0, 32, 8):
            for copy in copies[s][k : k + 8]:
                copy.wait()
            at = slice(k * PART, k * PART + 256)
            out[at, :] = product(rows[s, at, :], part[0], part[1])


def own_products(upper, lower, upper_part, lower_part):
    out = jax.ShapeDtypeStruct((16 * ROWS, WIDE), F32)
    return pl.pallas_call(
        own_kernel,
        out_shape=[out, out],
        in_specs=[HBM] * 2 + [VMEM] * 2,
        out_specs=[VMEM] * 2,
        scratch_shapes=[pltpu.VMEM((2, 16 * ROWS, WIDE), F32), pltpu.SemaphoreType.DMA((2, 32))],
        compiler_params=KERNEL,
        cost_estimate=pl.CostEstimate(flops=6 << 30, bytes_accessed=8 << 20, transcendentals=0),
        name="own",
    )(upper, lower, upper_part, lower_part)


def shape(rows, squares=False):
    return jax.ShapeDtypeStruct((rows + 8 if squares else rows, WIDE), F32)


def call(kernel, out_shape, *arrays, name, flops=0, from_hbm=None, scratch=()):
    return pl.pallas_call(
        kernel,
        out_shape=out_shape,
        in_specs=[HBM if n == from_hbm else VMEM for n in range(len(arrays))],
        out_specs=jax.tree.map(lambda _: VMEM, out_shape),
        scratch_shapes=scratch,
        compiler_params=KERNEL,
        cost_estimate=pl.CostEstimate(flops=flops, bytes_accessed=1 << 20, transcendentals=0),
        name=name,
    )(*arrays)


def meet_kernel(stream, vectors, own, roots, poles, squares, send, coefficient, sums, rows, sems):
    copies = []
    for n, first in enumerate((256, 768, 0, 512)):
        at = pl.ds(first, 256)
        copies.append(pltpu.make_async_copy(vectors.at[at, :], rows.at[at, :], sems.at[n]))
        copies[n].start()
    total = squares[...] + loewner(stream, roots[...], poles[...], coefficient)
    send[256:, :] = total
    sums[...] = total
    copies[0].wait()
    send[:256, :] = own[256:512, :] + product(rows[256:512, :], coefficient[0], coefficient[1])
    for copy in copies[1:]:
        copy.wait()


def meet(stream, *arrays):
    return call(
        functools.partial(meet_kernel, stream),
        [shape(256, True), COEFFICIENT, SQUARES, shape(16 * ROWS)],
        *arrays,
        name=f"meet_{stream}",
        flops=1 << 30,
        from_hbm=0,
        scratch=[pltpu.SemaphoreType.DMA((4,))],
    )


def add_own_kernel(first, vectors, own, coefficient, out):
    at = slice(first, first + 256)
    out[...] = own[at, :] + product(vectors[at, :], coefficient[0], coefficient[1])


def add_own(first, *arrays, name):
    return call(functools.partial(add_own_kernel, first), shape(256), *arrays, name=name, flops=1 << 30)


def add_kernel(half, kept, arrived, *refs):
    if len(refs) > 3:
        squares, _, send, keep, sums = refs
        total = squares[...] + arrived[2 * half :, :]
        send[half:, :] = total
        sums[...] = total
    else:
        _, send, keep = refs
    send[:half, :] = kept[half:, :] + arrived[half : 2 * half, :]
    keep[...] = kept[:half, :] + arrived[:half, :]


def add(half, kept, arrived, squares, after, name):
    kernel = functools.partial(add_kernel, half)
    if squares is None:
        return *call(kernel, [shape(half), shape(half)], kept, arrived, after, name=name), None
    return call(kernel, [shape(half, True), shape(half), SQUARES], kept, arrived, squares, after, name=name)


def join_kernel(upper, lower, upper_in, lower_in, *refs):
    if len(refs) > 4:
        upper_squares, lower_squares, send, up, low, sums = refs
        total = upper_squares[...] + lower_squares[...]
        total = total + (upper_in[2 * PART :, :] + lower_in[2 * PART :, :])
        send[2 * PART :, :] = total
        sums[...] = total
    else:
        _, send, up, low = refs
    send[:PART, :] = upper[PART:, :] + upper_in[PART : 2 * PART, :]
    send[PART : 2 * PART, :] = lower[PART:, :] + lower_in[PART : 2 * PART, :]
    up[...] = upper[:PART, :] + upper_in[:PART, :]
    low[...] = lower[:PART, :] + lower_in[:PART, :]


def join(batch, *arrays):
    out = [shape(2 * PART, batch == 0), shape(PART), shape(PART)] + [SQUARES] * (batch == 0)
    return call(join_kernel, out, *arrays, name=f"join_{batch}")


def finish_kernel(squares, arrived, upper, lower, late, late_upper, late_lower, out):
    norm = jnp.sqrt(jnp.sum(squares[...] + arrived[2 * PART :, :], axis=0, keepdims=True))
    for first, up, low, came in ((0, upper, lower, arrived), (PART, late_upper, late_lower, late)):
        out[first : first + PART, 0, :] = (up[...] + came[:PART, :]) / norm
        out[first : first + PART, 1, :] = (low[...] + came[PART : 2 * PART, :]) / norm


def local(upper_vectors, lower_vectors, secular_roots, pole_values, pole_weights, undeflated):
    vectors = [pltpu.with_memory_space_constraint(v, pltpu.HBM) for v in (upper_vectors, lower_vectors)]
    roots = secular_roots.reshape(1, WIDE)
    sent = (pick_upper(vectors[0]), pick_lower(vectors[1]))
    raw = [pltpu.with_memory_space_constraint(exchange(sent[s], s, 0), pltpu.HBM) for s in (0, 1)]
    packed = pack(pole_values, pole_weights, undeflated)
    poles = lax.all_to_all(packed, "row", split_axis=0, concat_axis=0, tiled=True)
    met = [exchange(poles, s, 0) for s in (0, 1)]
    *coefficients, upper_squares, lower_squares = own_loewner(roots, poles)
    own = own_products(*vectors, *coefficients)

    streams = [(s, batch) for batch in (0, 1) for s in (0, 1)]
    squares = {(s, 1): None for s in (0, 1)} | {(0, 0): upper_squares, (1, 0): lower_squares}
    send, keep, arrived, parts = {}, {}, {}, {}
    for s in (0, 1):
        send[s, 0], parts[s], squares[s, 0], raw[s] = meet(s, raw[s], own[s], roots, met[s], squares[s, 0])
    for s in (0, 1):
        send[s, 1] = add_own(768, raw[s], own[s], parts[s], name=f"meet_{s}_late")
    for s, batch in streams:
        keep[s, batch] = add_own(512 * batch, raw[s], own[s], parts[s], name=f"rest_{s}_{batch}")
    after = send[1, 1]
    for phase in (1, 2):
        for at in streams:
            arrived[at] = exchange(send[at], at[0], phase)
        for at in streams:
            half, name = PART << (3 - phase), "add_{}_{}_{}".format(phase, *at)
            send[at], keep[at], squares[at] = add(half, keep[at], arrived[at], squares[at], after, name)
            after = keep[at]
    for at in streams:
        arrived[at] = exchange(send[at], at[0], 3)
    early = join(0, *(group[s, 0] for group in (keep, arrived, squares) for s in (0, 1)))
    late = join(1, *(group[s, 1] for group in (keep, arrived) for s in (0, 1)), early[1])
    return call(
        finish_kernel,
        jax.ShapeDtypeStruct((ROWS, 2, WIDE), F32),
        early[3],
        exchange(early[0], 0, 4),
        *early[1:3],
        exchange(late[0], 0, 4),
        *late[1:3],
        name="finish",
    )


def solution(mesh):
    return jax.shard_map(
        local,
        mesh=mesh,
        in_specs=(
            P("row", "col"),
            P("row", "col"),
            P(),
            P(None, ("col", "row")),
            P(None, ("col", "row")),
            P(None, ("col", "row")),
        ),
        out_specs=P(("row", "col"), None, None),
        check_vma=False,
    )
```

time: 92.2 us -> 82.9 us (0.90)
  the two profiles are of different devices: /device:TPU:20 before, /device:TPU:2 now
where the time goes in v2:
time: 82.9 us; the launch traced here: 81.4 us
  starting transfers between devices  27.5 us (33%)
  Pallas kernels  21.3 us (26%)
  waiting for transfers between devices  18.7 us (23%)
  blocking collectives  13.7 us (17%)
    ppermute x18, starting transfers between devices, exchange(): return lax.ppermute(block, ('row', 'col'), PARTNERS[stream][phase])  27.5 us
    ppermute x18, waiting for transfers between devices, exchange(): return lax.ppermute(block, ('row', 'col'), PARTNERS[stream][phase])  18.7 us
    all_to_all x1, blocking collectives, local(): lax.all_to_all(packed, 'row', split_axis=0, concat_axis=0, tiled=True)  13.7 us
    pallas_call x19, Pallas kernels, call(): pl.pallas_call(kernel, out_shape=out_shape, in_specs=[HBM if n == from_hb...  8.12 us
    pallas_call x1, Pallas kernels, own_products(): pl.pallas_call(own_kernel, out_shape=[out, out], in_specs=[HBM] * 2 + [VM...  6.41 us
    pallas_call x1, Pallas kernels, pick_upper(): pl.pallas_call(pick_upper_kernel, out_shape=jax.ShapeDtypeStruct((16 * RO...  2.86 us
    pallas_call x1, Pallas kernels, pick_lower(): pl.pallas_call(pick_lower_kernel, out_shape=jax.ShapeDtypeStruct((16 * RO...  1.83 us
  transfers between devices with their start and end apart: 18, of which 8 were waited for; matrix products, arithmetic and copies ran while one was open for 0% of the time, Pallas kernels for 22%

profile of v2, /device:TPU:2, one launch (start us, length us, event | category | flops | bytes accessed | tf_op | source)
XLA Modules:
  0.0 81.4 jit_solution(2327958597241671438)
XLA Ops:
  0.0 2.9 %pick_upper.1 = f32[1024,512]{1,0:T(8,128)} custom-call(f32[2048,512]{1,0:T(8,128)} %upper.1), custom_call_target="tpu_custom_call" | custom-call | bytes 4194304 | tf_op jit(solution)/shard_map/pick_upper/pallas_call | solution.py:141
  2.9 2.0 %collective-permute-start = (f32[1024,512]{1,0:T(8,128)}, f32[1024,512]{1,0:T(8,128)}, u32[]{:S(2)}, u32[]{:S(2)}) collective-permute-start(f32[1024,512]{1,0:T(8,128)} %pick_upper.1), channel_id=1, source_target_pairs={{0,4},{1,5},{2,6},{3,7},{4,0},{5,1},{6,2},{7,3},{8,12},{9,13},{10,... | collective-permute-start | bytes 6291464 | tf_op jit(solution)/shard_map/ppermute | solution.py:71
  4.9 1.8 %pick_lower.1 = f32[1024,512]{1,0:T(8,128)S(1)} custom-call(f32[2048,512]{1,0:T(8,128)} %vectors.3), custom_call_target="tpu_custom_call" | custom-call | bytes 4194304 | tf_op jit(solution)/shard_map/pick_lower/pallas_call | solution.py:154
  6.7 0.6 collective-permute-start.3
  7.3 1.3 %pack.1 = f32[64,128]{1,0:T(8,128)} custom-call(f32[2,64]{1,0:T(2,128)} %poles.1, f32[2,64]{1,0:T(2,128)} %weights.1, s32[2,64]{1,0:T(2,128)} %undeflated.1), custom_call_target="tpu_custom_call" | custom-call | tf_op jit(solution)/shard_map/pack/pallas_call | solution.py:175
  8.7 13.7 %all_to_all.11 = f32[8,8,128]{2,1,0:T(8,128)S(1)} all-to-all(f32[8,8,128]{2,1,0:T(8,128)} %bitcast.9), channel_id=1, replica_groups=mesh['row'=8,'col'=32] {'row'}, dimensions={0} | all-to-all | bytes 65536 | tf_op jit(solution)/shard_map/all_to_all | solution.py:358
  22.4 1.8 %collective-permute-start.4 = (f32[64,128]{1,0:T(8,128)S(1)}, f32[64,128]{1,0:T(8,128)S(1)}, u32[]{:S(2)}, u32[]{:S(2)}) collective-permute-start(f32[64,128]{1,0:T(8,128)S(1)} %bitcast.3), channel_id=1, source_target_pairs={{0,1},{1,0},{2,3},{3,2},{4,5},{5,4},{6,7},{7,6},{8,9},{9,8},{10,11... | collective-permute-start | bytes 98312 | tf_op jit(solution)/shard_map/ppermute | solution.py:71
  24.2 0.8 loewner.1
  24.9 6.4 %own.1 = (f32[1024,512]{1,0:T(8,128)S(1)}, f32[1024,512]{1,0:T(8,128)S(1)}) custom-call(f32[2048,512]{1,0:T(8,128)} %upper.1, f32[2048,512]{1,0:T(8,128)} %vectors.3, bf16[2,512,512]{2,1,0:T(8,128)(2,1)S(1)} %get-tuple-element.46.upper_part, bf16[2,512,512]{2,1,0:T(8,128)(2,1)S(1)} %get-tuple-element.47.lower_part), custom_call_target="tpu_custom_call" | custom-call | flops 6442450944 | bytes 8388608 | tf_op jit(solution)/shard_map/own/pallas_call | solution.py:241
  31.4 1.7 %meet_0.1 = (f32[264,512]{1,0:T(8,128)S(1)}, bf16[2,512,512]{2,1,0:T(8,128)(2,1)S(1)}, f32[8,512]{1,0:T(8,128)S(1)}, f32[1024,512]{1,0:T(8,128)S(1)}) custom-call(f32[1024,512]{1,0:T(8,128)} %collective-permute-done.vectors, f32[1024,512]{1,0:T(8,128)S(1)} %get-tuple-element.48.own, f32[1,512]{1,0:T(1,128)S(1)} %bitcast.7, ...), custom_call_target="tpu_custom_call" | custom-call | flops 1073741824 | bytes 1048576 | tf_op jit(solution)/shard_map/meet_0/pallas_call | solution.py:258
  33.1 4.1 %collective-permute-start.2 = (f32[264,512]{1,0:T(8,128)S(1)}, f32[264,512]{1,0:T(8,128)S(1)}, u32[]{:S(2)}, u32[]{:S(2)}) collective-permute-start(f32[264,512]{1,0:T(8,128)S(1)} %get-tuple-element.52), channel_id=1, source_target_pairs={{0,28},{1,29},{2,30},{3,31},{4,8},{5,9},{6,10},{7,11},{8,4},{9,5},... | collective-permute-start | bytes 1622024 | tf_op jit(solution)/shard_map/ppermute | solution.py:71
  37.2 1.7 %meet_1.1 = (f32[264,512]{1,0:T(8,128)S(1)}, bf16[2,512,512]{2,1,0:T(8,128)(2,1)S(1)}, f32[8,512]{1,0:T(8,128)S(1)}, f32[1024,512]{1,0:T(8,128)S(1)}) custom-call(f32[1024,512]{1,0:T(8,128)} %collective-permute-done.3.vectors, f32[1024,512]{1,0:T(8,128)S(1)} %get-tuple-element.54.own, f32[1,512]{1,0:T(1,128)S(1)} %bitcast.8, ...), custom_call_target="tpu_custom_call" | custom-call | flops 1073741824 | bytes 1048576 | tf_op jit(solution)/shard_map/meet_1/pallas_call | solution.py:258
  38.9 1.6 %collective-permute-start.8 = (f32[264,512]{1,0:T(8,128)S(1)}, f32[264,512]{1,0:T(8,128)S(1)}, u32[]{:S(2)}, u32[]{:S(2)}) collective-permute-start(f32[264,512]{1,0:T(8,128)S(1)} %get-tuple-element.61), channel_id=1, source_target_pairs={{0,3},{1,2},{2,1},{3,0},{4,7},{5,6},{6,5},{7,4},{8,11},{9,10},{10,... | collective-permute-start | bytes 1622024 | tf_op jit(solution)/shard_map/ppermute | solution.py:71
  41.0 1.0 %collective-permute-start.7 = (f32[256,512]{1,0:T(8,128)S(1)}, f32[256,512]{1,0:T(8,128)S(1)}, u32[]{:S(2)}, u32[]{:S(2)}) collective-permute-start(f32[256,512]{1,0:T(8,128)S(1)} %meet_0_late.1), channel_id=1, source_target_pairs={{0,28},{1,29},{2,30},{3,31},{4,8},{5,9},{6,10},{7,11},{8,4},{9,5},... | collective-permute-start | bytes 1572872 | tf_op jit(solution)/shard_map/ppermute | solution.py:71
  42.7 0.8 collective-permute-start.6
  43.5 0.6 rest_0_1.1.kept
  45.3 1.6 %collective-permute-start.5 = (f32[136,512]{1,0:T(8,128)S(1)}, f32[136,512]{1,0:T(8,128)S(1)}, u32[]{:S(2)}, u32[]{:S(2)}) collective-permute-start(f32[136,512]{1,0:T(8,128)S(1)} %get-tuple-element.59), channel_id=1, source_target_pairs={{0,3},{1,2},{2,1},{3,0},{4,7},{5,6},{6,5},{7,4},{8,11},{9,10},{10,... | collective-permute-start | bytes 835592 | tf_op jit(solution)/shard_map/ppermute | solution.py:71
  46.9 1.4 %collective-permute-done.8.arrived = f32[264,512]{1,0:T(8,128)S(1)} collective-permute-done((f32[264,512]{1,0:T(8,128)S(1)}, f32[264,512]{1,0:T(8,128)S(1)}, u32[]{:S(2)}, u32[]{:S(2)}) %collective-permute-start.8) | collective-permute-done | bytes 540704 | tf_op jit(solution)/shard_map/ppermute | solution.py:71
  48.5 0.6 rest_1_1.1.kept
  49.1 4.1 %collective-permute-done.7.arrived = f32[256,512]{1,0:T(8,128)S(1)} collective-permute-done((f32[256,512]{1,0:T(8,128)S(1)}, f32[256,512]{1,0:T(8,128)S(1)}, u32[]{:S(2)}, u32[]{:S(2)}) %collective-permute-start.7) | collective-permute-done | bytes 524320 | tf_op jit(solution)/shard_map/ppermute | solution.py:71
  53.3 0.6 collective-permute-done.6.arrived
  54.1 2.8 %collective-permute-done.5.arrived = f32[136,512]{1,0:T(8,128)S(1)} collective-permute-done((f32[136,512]{1,0:T(8,128)S(1)}, f32[136,512]{1,0:T(8,128)S(1)}, u32[]{:S(2)}, u32[]{:S(2)}) %collective-permute-start.5) | collective-permute-done | bytes 278560 | tf_op jit(solution)/shard_map/ppermute | solution.py:71
  57.0 1.8 %collective-permute-start.10 = (f32[72,512]{1,0:T(8,128)S(1)}, f32[72,512]{1,0:T(8,128)S(1)}, u32[]{:S(2)}, u32[]{:S(2)}) collective-permute-start(f32[72,512]{1,0:T(8,128)S(1)} %get-tuple-element.70), channel_id=1, source_target_pairs={{0,1},{1,0},{2,3},{3,2},{4,5},{5,4},{6,7},{7,6},{8,9},{9,8},{10,11... | collective-permute-start | bytes 442376 | tf_op jit(solution)/shard_map/ppermute | solution.py:71
  58.8 1.8 %collective-permute-start.11 = (f32[72,512]{1,0:T(8,128)S(1)}, f32[72,512]{1,0:T(8,128)S(1)}, u32[]{:S(2)}, u32[]{:S(2)}) collective-permute-start(f32[72,512]{1,0:T(8,128)S(1)} %get-tuple-element.71), channel_id=1, source_target_pairs={{0,28},{1,29},{2,30},{3,31},{4,8},{5,9},{6,10},{7,11},{8,4},{9,5},... | collective-permute-start | bytes 442376 | tf_op jit(solution)/shard_map/ppermute | solution.py:71
  60.7 0.7 collective-permute-done.13.arrived
  61.8 4.2 %collective-permute-start.16 = (f32[64,512]{1,0:T(8,128)S(1)}, f32[64,512]{1,0:T(8,128)S(1)}, u32[]{:S(2)}, u32[]{:S(2)}) collective-permute-start(f32[64,512]{1,0:T(8,128)S(1)} %get-tuple-element.83), channel_id=1, source_target_pairs={{0,28},{1,29},{2,30},{3,31},{4,8},{5,9},{6,10},{7,11},{8,4},{9,5},... | collective-permute-start | bytes 393224 | tf_op jit(solution)/shard_map/ppermute | solution.py:71
  66.0 1.8 %collective-permute-start.15 = (f32[64,512]{1,0:T(8,128)S(1)}, f32[64,512]{1,0:T(8,128)S(1)}, u32[]{:S(2)}, u32[]{:S(2)}) collective-permute-start(f32[64,512]{1,0:T(8,128)S(1)} %get-tuple-element.82), channel_id=1, source_target_pairs={{0,1},{1,0},{2,3},{3,2},{4,5},{5,4},{6,7},{7,6},{8,9},{9,8},{10,11... | collective-permute-start | bytes 393224 | tf_op jit(solution)/shard_map/ppermute | solution.py:71
  67.8 2.0 %collective-permute-start.12 = (f32[72,512]{1,0:T(8,128)S(1)}, f32[72,512]{1,0:T(8,128)S(1)}, u32[]{:S(2)}, u32[]{:S(2)}) collective-permute-start(f32[72,512]{1,0:T(8,128)S(1)} %get-tuple-element.75), channel_id=1, source_target_pairs={{0,12},{1,13},{2,14},{3,15},{4,24},{5,25},{6,26},{7,27},{8,20},{9,... | collective-permute-start | bytes 442376 | tf_op jit(solution)/shard_map/ppermute | solution.py:71
  69.8 4.0 %collective-permute-done.16.lower_in = f32[64,512]{1,0:T(8,128)S(1)} collective-permute-done((f32[64,512]{1,0:T(8,128)S(1)}, f32[64,512]{1,0:T(8,128)S(1)}, u32[]{:S(2)}, u32[]{:S(2)}) %collective-permute-start.16) | collective-permute-done | bytes 131104 | tf_op jit(solution)/shard_map/ppermute | solution.py:71
  73.8 2.1 %collective-permute-start.17 = (f32[64,512]{1,0:T(8,128)S(1)}, f32[64,512]{1,0:T(8,128)S(1)}, u32[]{:S(2)}, u32[]{:S(2)}) collective-permute-start(f32[64,512]{1,0:T(8,128)S(1)} %get-tuple-element.84), channel_id=1, source_target_pairs={{0,12},{1,13},{2,14},{3,15},{4,24},{5,25},{6,26},{7,27},{8,20},{9,... | collective-permute-start | bytes 393224 | tf_op jit(solution)/shard_map/ppermute | solution.py:71
  75.9 4.8 %collective-permute-done.17.late = f32[64,512]{1,0:T(8,128)S(1)} collective-permute-done((f32[64,512]{1,0:T(8,128)S(1)}, f32[64,512]{1,0:T(8,128)S(1)}, u32[]{:S(2)}, u32[]{:S(2)}) %collective-permute-start.17) | collective-permute-done | bytes 131104 | tf_op jit(solution)/shard_map/ppermute | solution.py:71
  80.6 0.8 finish.1
  (31 shorter events, 3.5 us)
Async XLA Ops:
  2.9 21.3 %copy-start = (f32[512]{0:T(512)S(1)}, f32[512]{0:T(512)}, u32[]{:S(2)}) copy-start(f32[512]{0:T(512)} %param.8) | copy-start | bytes 6148
  2.9 28.5 %collective-permute-start = (f32[1024,512]{1,0:T(8,128)}, f32[1024,512]{1,0:T(8,128)}, u32[]{:S(2)}, u32[]{:S(2)}) collective-permute-start(f32[1024,512]{1,0:T(8,128)} %pick_upper.1), channel_id=1, source_target_pairs={{0,4},{1,5},{2,6},{3,7},{4,0},{5,1},{6,2},{7,3},{8,12},{9,13},{10,... | collective-permute-start | bytes 6291464 | tf_op jit(solution)/shard_map/ppermute | solution.py:71
  6.7 30.5 %collective-permute-start.3 = (f32[1024,512]{1,0:T(8,128)S(1)}, f32[1024,512]{1,0:T(8,128)}, u32[]{:S(2)}, u32[]{:S(2)}) collective-permute-start(f32[1024,512]{1,0:T(8,128)S(1)} %pick_lower.1), channel_id=1, source_target_pairs={{0,1},{1,0},{2,3},{3,2},{4,5},{5,4},{6,7},{7,6},{8,9},{9,8},{10,11... | collective-permute-start | bytes 6291464 | tf_op jit(solution)/shard_map/ppermute | solution.py:71
  22.4 14.8 %collective-permute-start.4 = (f32[64,128]{1,0:T(8,128)S(1)}, f32[64,128]{1,0:T(8,128)S(1)}, u32[]{:S(2)}, u32[]{:S(2)}) collective-permute-start(f32[64,128]{1,0:T(8,128)S(1)} %bitcast.3), channel_id=1, source_target_pairs={{0,1},{1,0},{2,3},{3,2},{4,5},{5,4},{6,7},{7,6},{8,9},{9,8},{10,11... | collective-permute-start | bytes 98312 | tf_op jit(solution)/shard_map/ppermute | solution.py:71
  24.2 7.2 %collective-permute-start.1 = (f32[64,128]{1,0:T(8,128)S(1)}, f32[64,128]{1,0:T(8,128)S(1)}, u32[]{:S(2)}, u32[]{:S(2)}) collective-permute-start(f32[64,128]{1,0:T(8,128)S(1)} %bitcast.4), channel_id=1, source_target_pairs={{0,4},{1,5},{2,6},{3,7},{4,0},{5,1},{6,2},{7,3},{8,12},{9,13},{10,... | collective-permute-start | bytes 98312 | tf_op jit(solution)/shard_map/ppermute | solution.py:71
  33.1 12.2 %collective-permute-start.2 = (f32[264,512]{1,0:T(8,128)S(1)}, f32[264,512]{1,0:T(8,128)S(1)}, u32[]{:S(2)}, u32[]{:S(2)}) collective-permute-start(f32[264,512]{1,0:T(8,128)S(1)} %get-tuple-element.52), channel_id=1, source_target_pairs={{0,28},{1,29},{2,30},{3,31},{4,8},{5,9},{6,10},{7,11},{8,4},{9,5},... | collective-permute-start | bytes 1622024 | tf_op jit(solution)/shard_map/ppermute | solution.py:71
  38.9 9.4 %collective-permute-start.8 = (f32[264,512]{1,0:T(8,128)S(1)}, f32[264,512]{1,0:T(8,128)S(1)}, u32[]{:S(2)}, u32[]{:S(2)}) collective-permute-start(f32[264,512]{1,0:T(8,128)S(1)} %get-tuple-element.61), channel_id=1, source_target_pairs={{0,3},{1,2},{2,1},{3,0},{4,7},{5,6},{6,5},{7,4},{8,11},{9,10},{10,... | collective-permute-start | bytes 1622024 | tf_op jit(solution)/shard_map/ppermute | solution.py:71
  41.0 12.1 %collective-permute-start.7 = (f32[256,512]{1,0:T(8,128)S(1)}, f32[256,512]{1,0:T(8,128)S(1)}, u32[]{:S(2)}, u32[]{:S(2)}) collective-permute-start(f32[256,512]{1,0:T(8,128)S(1)} %meet_0_late.1), channel_id=1, source_target_pairs={{0,28},{1,29},{2,30},{3,31},{4,8},{5,9},{6,10},{7,11},{8,4},{9,5},... | collective-permute-start | bytes 1572872 | tf_op jit(solution)/shard_map/ppermute | solution.py:71
  42.7 11.3 %collective-permute-start.6 = (f32[256,512]{1,0:T(8,128)S(1)}, f32[256,512]{1,0:T(8,128)S(1)}, u32[]{:S(2)}, u32[]{:S(2)}) collective-permute-start(f32[256,512]{1,0:T(8,128)S(1)} %meet_1_late.1.refs_1_), channel_id=1, source_target_pairs={{0,3},{1,2},{2,1},{3,0},{4,7},{5,6},{6,5},{7,4},{8,11},{9,10},{10,... | collective-permute-start | bytes 1572872 | tf_op jit(solution)/shard_map/ppermute | solution.py:71
  45.3 11.6 %collective-permute-start.5 = (f32[136,512]{1,0:T(8,128)S(1)}, f32[136,512]{1,0:T(8,128)S(1)}, u32[]{:S(2)}, u32[]{:S(2)}) collective-permute-start(f32[136,512]{1,0:T(8,128)S(1)} %get-tuple-element.59), channel_id=1, source_target_pairs={{0,3},{1,2},{2,1},{3,0},{4,7},{5,6},{6,5},{7,4},{8,11},{9,10},{10,... | collective-permute-start | bytes 835592 | tf_op jit(solution)/shard_map/ppermute | solution.py:71
  48.4 10.4 %collective-permute-start.9 = (f32[136,512]{1,0:T(8,128)S(1)}, f32[136,512]{1,0:T(8,128)S(1)}, u32[]{:S(2)}, u32[]{:S(2)}) collective-permute-start(f32[136,512]{1,0:T(8,128)S(1)} %get-tuple-element.67), channel_id=1, source_target_pairs={{0,4},{1,5},{2,6},{3,7},{4,0},{5,1},{6,2},{7,3},{8,12},{9,13},{10,... | collective-permute-start | bytes 835592 | tf_op jit(solution)/shard_map/ppermute | solution.py:71
  53.2 8.1 %collective-permute-start.13 = (f32[128,512]{1,0:T(8,128)S(1)}, f32[128,512]{1,0:T(8,128)S(1)}, u32[]{:S(2)}, u32[]{:S(2)}) collective-permute-start(f32[128,512]{1,0:T(8,128)S(1)} %get-tuple-element.78), channel_id=1, source_target_pairs={{0,3},{1,2},{2,1},{3,0},{4,7},{5,6},{6,5},{7,4},{8,11},{9,10},{10,... | collective-permute-start | bytes 786440 | tf_op jit(solution)/shard_map/ppermute | solution.py:71
  54.0 7.7 %collective-permute-start.14 = (f32[128,512]{1,0:T(8,128)S(1)}, f32[128,512]{1,0:T(8,128)S(1)}, u32[]{:S(2)}, u32[]{:S(2)}) collective-permute-start(f32[128,512]{1,0:T(8,128)S(1)} %get-tuple-element.80), channel_id=1, source_target_pairs={{0,4},{1,5},{2,6},{3,7},{4,0},{5,1},{6,2},{7,3},{8,12},{9,13},{10,... | collective-permute-start | bytes 786440 | tf_op jit(solution)/shard_map/ppermute | solution.py:71
  57.0 10.8 %collective-permute-start.10 = (f32[72,512]{1,0:T(8,128)S(1)}, f32[72,512]{1,0:T(8,128)S(1)}, u32[]{:S(2)}, u32[]{:S(2)}) collective-permute-start(f32[72,512]{1,0:T(8,128)S(1)} %get-tuple-element.70), channel_id=1, source_target_pairs={{0,1},{1,0},{2,3},{3,2},{4,5},{5,4},{6,7},{7,6},{8,9},{9,8},{10,11... | collective-permute-start | bytes 442376 | tf_op jit(solution)/shard_map/ppermute | solution.py:71
  58.8 8.9 %collective-permute-start.11 = (f32[72,512]{1,0:T(8,128)S(1)}, f32[72,512]{1,0:T(8,128)S(1)}, u32[]{:S(2)}, u32[]{:S(2)}) collective-permute-start(f32[72,512]{1,0:T(8,128)S(1)} %get-tuple-element.71), channel_id=1, source_target_pairs={{0,28},{1,29},{2,30},{3,31},{4,8},{5,9},{6,10},{7,11},{8,4},{9,5},... | collective-permute-start | bytes 442376 | tf_op jit(solution)/shard_map/ppermute | solution.py:71
  61.8 12.0 %collective-permute-start.16 = (f32[64,512]{1,0:T(8,128)S(1)}, f32[64,512]{1,0:T(8,128)S(1)}, u32[]{:S(2)}, u32[]{:S(2)}) collective-permute-start(f32[64,512]{1,0:T(8,128)S(1)} %get-tuple-element.83), channel_id=1, source_target_pairs={{0,28},{1,29},{2,30},{3,31},{4,8},{5,9},{6,10},{7,11},{8,4},{9,5},... | collective-permute-start | bytes 393224 | tf_op jit(solution)/shard_map/ppermute | solution.py:71
  66.0 7.8 %collective-permute-start.15 = (f32[64,512]{1,0:T(8,128)S(1)}, f32[64,512]{1,0:T(8,128)S(1)}, u32[]{:S(2)}, u32[]{:S(2)}) collective-permute-start(f32[64,512]{1,0:T(8,128)S(1)} %get-tuple-element.82), channel_id=1, source_target_pairs={{0,1},{1,0},{2,3},{3,2},{4,5},{5,4},{6,7},{7,6},{8,9},{9,8},{10,11... | collective-permute-start | bytes 393224 | tf_op jit(solution)/shard_map/ppermute | solution.py:71
  67.8 12.8 %collective-permute-start.12 = (f32[72,512]{1,0:T(8,128)S(1)}, f32[72,512]{1,0:T(8,128)S(1)}, u32[]{:S(2)}, u32[]{:S(2)}) collective-permute-start(f32[72,512]{1,0:T(8,128)S(1)} %get-tuple-element.75), channel_id=1, source_target_pairs={{0,12},{1,13},{2,14},{3,15},{4,24},{5,25},{6,26},{7,27},{8,20},{9,... | collective-permute-start | bytes 442376 | tf_op jit(solution)/shard_map/ppermute | solution.py:71
  73.8 6.9 %collective-permute-start.17 = (f32[64,512]{1,0:T(8,128)S(1)}, f32[64,512]{1,0:T(8,128)S(1)}, u32[]{:S(2)}, u32[]{:S(2)}) collective-permute-start(f32[64,512]{1,0:T(8,128)S(1)} %get-tuple-element.84), channel_id=1, source_target_pairs={{0,12},{1,13},{2,14},{3,15},{4,24},{5,25},{6,26},{7,27},{8,20},{9,... | collective-permute-start | bytes 393224 | tf_op jit(solution)/shard_map/ppermute | solution.py:71

commit v3 on v2

--- a/solution.py
+++ b/solution.py
@@ -64,6 +64,7 @@
     return pairs
 
 
+CORES = [(device, device ^ 32) for device in range(256)]
 PARTNERS = tuple(tuple(partners(stream, phase) for phase in range(5)) for stream in range(2))
 
 
@@ -115,8 +116,8 @@
     return copies
 
 
-def pick_upper_kernel(vectors, out, rows, sems):
-    arriving = copy_rows(0, 16, vectors, rows, sems.at[0])
+def pick_kernel(stream, vectors, out, rows, sems):
+    arriving = copy_rows(stream, 16, vectors, rows, sems.at[0])
     for copy in arriving:
         copy.start()
     leaving = []
@@ -129,37 +130,16 @@
         copy.wait()
 
 
-def pick_lower_kernel(vectors, out, sems):
-    copies = copy_rows(1, 16, vectors, out, sems)
-    for copy in copies:
-        copy.start()
-    for copy in copies:
-        copy.wait()
-
-
-def pick_upper(vectors):
+def pick(stream, vectors):
     return pl.pallas_call(
-        pick_upper_kernel,
+        functools.partial(pick_kernel, stream),
         out_shape=jax.ShapeDtypeStruct((16 * ROWS, WIDE), F32),
         in_specs=[HBM],
         out_specs=HBM,
         scratch_shapes=[pltpu.VMEM((16 * ROWS, WIDE), F32), pltpu.SemaphoreType.DMA((2, 32))],
         compiler_params=pltpu.CompilerParams(vmem_limit_bytes=4 << 20),
         cost_estimate=pl.CostEstimate(flops=0, bytes_accessed=4 << 20, transcendentals=0),
-        name="pick_upper",
-    )(vectors)
-
-
-def pick_lower(vectors):
-    return pl.pallas_call(
-        pick_lower_kernel,
-        out_shape=jax.ShapeDtypeStruct((16 * ROWS, WIDE), F32),
-        in_specs=[HBM],
-        out_specs=VMEM,
-        scratch_shapes=[pltpu.SemaphoreType.DMA((32,))],
-        compiler_params=pltpu.CompilerParams(vmem_limit_bytes=4 << 20),
-        cost_estimate=pl.CostEstimate(flops=0, bytes_accessed=4 << 20, transcendentals=0),
-        name="pick_lower",
+        name=f"pick_{stream}",
     )(vectors)
 
 
@@ -282,6 +262,16 @@
         copy.wait()
 
 
+def meet_direct(stream, *arrays):
+    return call(
+        functools.partial(meet_direct_kernel, stream),
+        [shape(256, True), COEFFICIENT, SQUARES],
+        *arrays,
+        name=f"meet_{stream}",
+        flops=1 << 30,
+    )
+
+
 def meet(stream, *arrays):
     return call(
         functools.partial(meet_kernel, stream),
@@ -294,6 +284,13 @@
     )
 
 
+def meet_direct_kernel(stream, vectors, own, roots, poles, squares, send, coefficient, sums):
+    total = squares[...] + loewner(stream, roots[...], poles[...], coefficient)
+    send[256:, :] = total
+    sums[...] = total
+    send[:256, :] = own[256:512, :] + product(vectors[256:512, :], coefficient[0], coefficient[1])
+
+
 def add_own_kernel(first, vectors, own, coefficient, out):
     at = slice(first, first + 256)
     out[...] = own[at, :] + product(vectors[at, :], coefficient[0], coefficient[1])
@@ -324,7 +321,7 @@
 
 def join_kernel(upper, lower, upper_in, lower_in, *refs):
     if len(refs) > 4:
-        upper_squares, lower_squares, send, up, low, sums = refs
+        upper_squares, lower_squares, _, send, up, low, sums = refs
         total = upper_squares[...] + lower_squares[...]
         total = total + (upper_in[2 * PART :, :] + lower_in[2 * PART :, :])
         send[2 * PART :, :] = total
@@ -352,8 +349,9 @@
 def local(upper_vectors, lower_vectors, secular_roots, pole_values, pole_weights, undeflated):
     vectors = [pltpu.with_memory_space_constraint(v, pltpu.HBM) for v in (upper_vectors, lower_vectors)]
     roots = secular_roots.reshape(1, WIDE)
-    sent = (pick_upper(vectors[0]), pick_lower(vectors[1]))
-    raw = [pltpu.with_memory_space_constraint(exchange(sent[s], s, 0), pltpu.HBM) for s in (0, 1)]
+    sent = [pick(s, vectors[s]) for s in (0, 1)]
+    raw = [exchange(sent[s], s, 0) for s in (0, 1)]
+    raw[0] = pltpu.with_memory_space_constraint(raw[0], pltpu.HBM)
     packed = pack(pole_values, pole_weights, undeflated)
     poles = lax.all_to_all(packed, "row", split_axis=0, concat_axis=0, tiled=True)
     met = [exchange(poles, s, 0) for s in (0, 1)]
@@ -363,8 +361,8 @@
     streams = [(s, batch) for batch in (0, 1) for s in (0, 1)]
     squares = {(s, 1): None for s in (0, 1)} | {(0, 0): upper_squares, (1, 0): lower_squares}
     send, keep, arrived, parts = {}, {}, {}, {}
-    for s in (0, 1):
-        send[s, 0], parts[s], squares[s, 0], raw[s] = meet(s, raw[s], own[s], roots, met[s], squares[s, 0])
+    send[0, 0], parts[0], squares[0, 0], raw[0] = meet(0, raw[0], own[0], roots, met[0], squares[0, 0])
+    send[1, 0], parts[1], squares[1, 0] = meet_direct(1, raw[1], own[1], roots, met[1], squares[1, 0])
     for s in (0, 1):
         send[s, 1] = add_own(768, raw[s], own[s], parts[s], name=f"meet_{s}_late")
     for s, batch in streams:
@@ -379,7 +377,8 @@
             after = keep[at]
     for at in streams:
         arrived[at] = exchange(send[at], at[0], 3)
-    early = join(0, *(group[s, 0] for group in (keep, arrived, squares) for s in (0, 1)))
+    ready = lax.ppermute(after, ("row", "col"), CORES)
+    early = join(0, *(group[s, 0] for group in (keep, arrived, squares) for s in (0, 1)), ready)
     late = join(1, *(group[s, 1] for group in (keep, arrived) for s in (0, 1)), early[1])
     return call(
         finish_kernel,

time: 82.9 us -> 81.7 us (0.986)
  waiting for transfers between devices: 18.7 us -> 15.7 us
  starting transfers between devices: 27.5 us -> 29.5 us
    ppermute x18, waiting for transfers between devices: 18.7 us -> 15.7 us  [exchange(): return lax.ppermute(block, ('row', 'col'), PARTNERS[stream][phase])]
    ppermute x18, starting transfers between devices: 27.5 us -> 29.4 us  [exchange(): return lax.ppermute(block, ('row', 'col'), PARTNERS[stream][phase])]
    pallas_call x2, Pallas kernels: 4.69 us -> 5.73 us  [pick(): pl.pallas_call(functools.partial(pick_kernel, stream), out_shape=jax.Shap...]
  transfers between devices with their start and end apart: 18 -> 19, of which waited for: 8 -> 5; matrix products, arithmetic and copies ran while one was open for 0% -> 0% of each run, Pallas kernels for 22% -> 22%
where the time goes in v3:
time: 81.7 us; the launch traced here: 80.8 us
  starting transfers between devices  29.5 us (36%)
  Pallas kernels  21.6 us (26%)
  waiting for transfers between devices  15.7 us (19%)
  blocking collectives  13.7 us (17%)
    ppermute x18, starting transfers between devices, exchange(): return lax.ppermute(block, ('row', 'col'), PARTNERS[stream][phase])  29.4 us
    ppermute x18, waiting for transfers between devices, exchange(): return lax.ppermute(block, ('row', 'col'), PARTNERS[stream][phase])  15.7 us
    all_to_all x1, blocking collectives, local(): lax.all_to_all(packed, 'row', split_axis=0, concat_axis=0, tiled=True)  13.7 us
    pallas_call x19, Pallas kernels, call(): pl.pallas_call(kernel, out_shape=out_shape, in_specs=[HBM if n == from_hb...  7.42 us
    pallas_call x1, Pallas kernels, own_products(): pl.pallas_call(own_kernel, out_shape=[out, out], in_specs=[HBM] * 2 + [VM...  6.41 us
    pallas_call x2, Pallas kernels, pick(): pl.pallas_call(functools.partial(pick_kernel, stream), out_shape=jax.Shap...  5.73 us
  transfers between devices with their start and end apart: 19, of which 5 were waited for; matrix products, arithmetic and copies ran while one was open for 0% of the time, Pallas kernels for 22%

profile of v3, /device:TPU:2, one launch (start us, length us, event | category | flops | bytes accessed | tf_op | source)
XLA Modules:
  0.0 80.8 jit_solution(165797296774221116)
XLA Ops:
  0.0 2.9 %pick_0.1 = f32[1024,512]{1,0:T(8,128)} custom-call(f32[2048,512]{1,0:T(8,128)} %upper.1), custom_call_target="tpu_custom_call" | custom-call | bytes 4194304 | tf_op jit(solution)/shard_map/pick_0/pallas_call | solution.py:134
  2.9 2.0 %collective-permute-start = (f32[1024,512]{1,0:T(8,128)}, f32[1024,512]{1,0:T(8,128)}, u32[]{:S(2)}, u32[]{:S(2)}) collective-permute-start(f32[1024,512]{1,0:T(8,128)} %pick_0.1), channel_id=1, source_target_pairs={{0,4},{1,5},{2,6},{3,7},{4,0},{5,1},{6,2},{7,3},{8,12},{9,13},{10,... | collective-permute-start | bytes 6291464 | tf_op jit(solution)/shard_map/ppermute | solution.py:72
  4.9 2.9 %pick_1.1 = f32[1024,512]{1,0:T(8,128)} custom-call(f32[2048,512]{1,0:T(8,128)} %vectors.3), custom_call_target="tpu_custom_call" | custom-call | bytes 4194304 | tf_op jit(solution)/shard_map/pick_1/pallas_call | solution.py:134
  7.8 0.6 collective-permute-start.3
  8.4 1.3 %pack.1 = f32[64,128]{1,0:T(8,128)} custom-call(f32[2,64]{1,0:T(2,128)} %poles.1, f32[2,64]{1,0:T(2,128)} %weights.1, s32[2,64]{1,0:T(2,128)} %undeflated.1), custom_call_target="tpu_custom_call" | custom-call | tf_op jit(solution)/shard_map/pack/pallas_call | solution.py:155
  9.7 13.7 %all_to_all.11 = f32[8,8,128]{2,1,0:T(8,128)S(1)} all-to-all(f32[8,8,128]{2,1,0:T(8,128)} %bitcast.9), channel_id=1, replica_groups=mesh['row'=8,'col'=32] {'row'}, dimensions={0} | all-to-all | bytes 65536 | tf_op jit(solution)/shard_map/all_to_all | solution.py:356
  23.4 1.8 %collective-permute-start.4 = (f32[64,128]{1,0:T(8,128)S(1)}, f32[64,128]{1,0:T(8,128)S(1)}, u32[]{:S(2)}, u32[]{:S(2)}) collective-permute-start(f32[64,128]{1,0:T(8,128)S(1)} %bitcast.3), channel_id=1, source_target_pairs={{0,1},{1,0},{2,3},{3,2},{4,5},{5,4},{6,7},{7,6},{8,9},{9,8},{10,11... | collective-permute-start | bytes 98312 | tf_op jit(solution)/shard_map/ppermute | solution.py:72
  25.2 0.8 loewner.1
  26.0 6.4 %own.1 = (f32[1024,512]{1,0:T(8,128)S(1)}, f32[1024,512]{1,0:T(8,128)S(1)}) custom-call(f32[2048,512]{1,0:T(8,128)} %upper.1, f32[2048,512]{1,0:T(8,128)} %vectors.3, bf16[2,512,512]{2,1,0:T(8,128)(2,1)S(1)} %get-tuple-element.45.upper_part, bf16[2,512,512]{2,1,0:T(8,128)(2,1)S(1)} %get-tuple-element.46.lower_part), custom_call_target="tpu_custom_call" | custom-call | flops 6442450944 | bytes 8388608 | tf_op jit(solution)/shard_map/own/pallas_call | solution.py:221
  32.4 1.7 %meet_0.1 = (f32[264,512]{1,0:T(8,128)S(1)}, bf16[2,512,512]{2,1,0:T(8,128)(2,1)S(1)}, f32[8,512]{1,0:T(8,128)S(1)}, f32[1024,512]{1,0:T(8,128)S(1)}) custom-call(f32[1024,512]{1,0:T(8,128)} %collective-permute-done.vectors, f32[1024,512]{1,0:T(8,128)S(1)} %get-tuple-element.47.own, f32[1,512]{1,0:T(1,128)S(1)} %bitcast.7, ...), custom_call_target="tpu_custom_call" | custom-call | flops 1073741824 | bytes 1048576 | tf_op jit(solution)/shard_map/meet_0/pallas_call | solution.py:238
  34.1 3.1 %collective-permute-start.2 = (f32[264,512]{1,0:T(8,128)S(1)}, f32[264,512]{1,0:T(8,128)S(1)}, u32[]{:S(2)}, u32[]{:S(2)}) collective-permute-start(f32[264,512]{1,0:T(8,128)S(1)} %get-tuple-element.51), channel_id=1, source_target_pairs={{0,28},{1,29},{2,30},{3,31},{4,8},{5,9},{6,10},{7,11},{8,4},{9,5},... | collective-permute-start | bytes 1622024 | tf_op jit(solution)/shard_map/ppermute | solution.py:72
  37.2 1.0 %meet_1.1 = (f32[264,512]{1,0:T(8,128)S(1)}, bf16[2,512,512]{2,1,0:T(8,128)(2,1)S(1)}, f32[8,512]{1,0:T(8,128)S(1)}) custom-call(f32[1024,512]{1,0:T(8,128)S(1)} %collective-permute-done.3.vectors, f32[1024,512]{1,0:T(8,128)S(1)} %get-tuple-element.53.own, f32[1,512]{1,0:T(1,128)S(1)} %bitcast.8, f32[64,128]{1,0:T(8,128)S(1)} %collective-permute-done.4.poles, ...), custom_call_target="tpu_custom_call" | custom-call | flops 1073741824 | bytes 1048576 | tf_op jit(solution)/shard_map/meet_1/pallas_call | solution.py:238
  38.2 1.6 %collective-permute-start.8 = (f32[264,512]{1,0:T(8,128)S(1)}, f32[264,512]{1,0:T(8,128)S(1)}, u32[]{:S(2)}, u32[]{:S(2)}) collective-permute-start(f32[264,512]{1,0:T(8,128)S(1)} %get-tuple-element.59), channel_id=1, source_target_pairs={{0,3},{1,2},{2,1},{3,0},{4,7},{5,6},{6,5},{7,4},{8,11},{9,10},{10,... | collective-permute-start | bytes 1622024 | tf_op jit(solution)/shard_map/ppermute | solution.py:72
  39.7 0.6 meet_0_late.1
  40.3 2.3 %collective-permute-start.7 = (f32[256,512]{1,0:T(8,128)S(1)}, f32[256,512]{1,0:T(8,128)S(1)}, u32[]{:S(2)}, u32[]{:S(2)}) collective-permute-start(f32[256,512]{1,0:T(8,128)S(1)} %meet_0_late.1), channel_id=1, source_target_pairs={{0,28},{1,29},{2,30},{3,31},{4,8},{5,9},{6,10},{7,11},{8,4},{9,5},... | collective-permute-start | bytes 1572872 | tf_op jit(solution)/shard_map/ppermute | solution.py:72
  42.6 0.6 meet_1_late.1.refs_1_
  43.2 0.8 collective-permute-start.6
  44.0 0.6 rest_0_1.1.kept
  45.9 1.6 %collective-permute-start.5 = (f32[136,512]{1,0:T(8,128)S(1)}, f32[136,512]{1,0:T(8,128)S(1)}, u32[]{:S(2)}, u32[]{:S(2)}) collective-permute-start(f32[136,512]{1,0:T(8,128)S(1)} %get-tuple-element.57), channel_id=1, source_target_pairs={{0,3},{1,2},{2,1},{3,0},{4,7},{5,6},{6,5},{7,4},{8,11},{9,10},{10,... | collective-permute-start | bytes 835592 | tf_op jit(solution)/shard_map/ppermute | solution.py:72
  47.8 0.6 rest_1_1.1.kept
  48.4 3.6 %collective-permute-done.7.arrived = f32[256,512]{1,0:T(8,128)S(1)} collective-permute-done((f32[256,512]{1,0:T(8,128)S(1)}, f32[256,512]{1,0:T(8,128)S(1)}, u32[]{:S(2)}, u32[]{:S(2)}) %collective-permute-start.7) | collective-permute-done | bytes 524320 | tf_op jit(solution)/shard_map/ppermute | solution.py:72
  52.1 1.2 %collective-permute-start.13 = (f32[128,512]{1,0:T(8,128)S(1)}, f32[128,512]{1,0:T(8,128)S(1)}, u32[]{:S(2)}, u32[]{:S(2)}) collective-permute-start(f32[128,512]{1,0:T(8,128)S(1)} %get-tuple-element.73), channel_id=1, source_target_pairs={{0,3},{1,2},{2,1},{3,0},{4,7},{5,6},{6,5},{7,4},{8,11},{9,10},{10,... | collective-permute-start | bytes 786440 | tf_op jit(solution)/shard_map/ppermute | solution.py:72
  53.6 2.6 %collective-permute-done.5.arrived = f32[136,512]{1,0:T(8,128)S(1)} collective-permute-done((f32[136,512]{1,0:T(8,128)S(1)}, f32[136,512]{1,0:T(8,128)S(1)}, u32[]{:S(2)}, u32[]{:S(2)}) %collective-permute-start.5) | collective-permute-done | bytes 278560 | tf_op jit(solution)/shard_map/ppermute | solution.py:72
  56.2 2.5 %collective-permute-start.10 = (f32[72,512]{1,0:T(8,128)S(1)}, f32[72,512]{1,0:T(8,128)S(1)}, u32[]{:S(2)}, u32[]{:S(2)}) collective-permute-start(f32[72,512]{1,0:T(8,128)S(1)} %get-tuple-element.68), channel_id=1, source_target_pairs={{0,1},{1,0},{2,3},{3,2},{4,5},{5,4},{6,7},{7,6},{8,9},{9,8},{10,11... | collective-permute-start | bytes 442376 | tf_op jit(solution)/shard_map/ppermute | solution.py:72
  58.8 1.6 %collective-permute-start.11 = (f32[72,512]{1,0:T(8,128)S(1)}, f32[72,512]{1,0:T(8,128)S(1)}, u32[]{:S(2)}, u32[]{:S(2)}) collective-permute-start(f32[72,512]{1,0:T(8,128)S(1)} %get-tuple-element.69), channel_id=1, source_target_pairs={{0,28},{1,29},{2,30},{3,31},{4,8},{5,9},{6,10},{7,11},{8,4},{9,5},... | collective-permute-start | bytes 442376 | tf_op jit(solution)/shard_map/ppermute | solution.py:72
  60.6 4.0 %collective-permute-start.17 = (f32[64,512]{1,0:T(8,128)S(1)}, f32[64,512]{1,0:T(8,128)S(1)}, u32[]{:S(2)}, u32[]{:S(2)}) collective-permute-start(f32[64,512]{1,0:T(8,128)S(1)} %get-tuple-element.81), channel_id=1, source_target_pairs={{0,28},{1,29},{2,30},{3,31},{4,8},{5,9},{6,10},{7,11},{8,4},{9,5},... | collective-permute-start | bytes 393224 | tf_op jit(solution)/shard_map/ppermute | solution.py:72
  64.6 2.0 %collective-permute-start.16 = (f32[64,512]{1,0:T(8,128)S(1)}, f32[64,512]{1,0:T(8,128)S(1)}, u32[]{:S(2)}, u32[]{:S(2)}) collective-permute-start(f32[64,512]{1,0:T(8,128)S(1)} %get-tuple-element.80), channel_id=1, source_target_pairs={{0,1},{1,0},{2,3},{3,2},{4,5},{5,4},{6,7},{7,6},{8,9},{9,8},{10,11... | collective-permute-start | bytes 393224 | tf_op jit(solution)/shard_map/ppermute | solution.py:72
  66.7 2.0 %collective-permute-start.15 = (f32[72,512]{1,0:T(8,128)S(1)}, f32[72,512]{1,0:T(8,128)S(1)}, u32[]{:S(2)}, u32[]{:S(2)}) collective-permute-start(f32[72,512]{1,0:T(8,128)S(1)} %get-tuple-element.77), channel_id=1, source_target_pairs={{0,12},{1,13},{2,14},{3,15},{4,24},{5,25},{6,26},{7,27},{8,20},{9,... | collective-permute-start | bytes 442376 | tf_op jit(solution)/shard_map/ppermute | solution.py:72
  68.6 0.9 %collective-permute-done.16.upper_in = f32[64,512]{1,0:T(8,128)S(1)} collective-permute-done((f32[64,512]{1,0:T(8,128)S(1)}, f32[64,512]{1,0:T(8,128)S(1)}, u32[]{:S(2)}, u32[]{:S(2)}) %collective-permute-start.16) | collective-permute-done | bytes 131104 | tf_op jit(solution)/shard_map/ppermute | solution.py:72
  69.6 2.0 %collective-permute-start.18 = (f32[64,512]{1,0:T(8,128)S(1)}, f32[64,512]{1,0:T(8,128)S(1)}, u32[]{:S(2)}, u32[]{:S(2)}) collective-permute-start(f32[64,512]{1,0:T(8,128)S(1)} %get-tuple-element.82), channel_id=1, source_target_pairs={{0,12},{1,13},{2,14},{3,15},{4,24},{5,25},{6,26},{7,27},{8,20},{9,... | collective-permute-start | bytes 393224 | tf_op jit(solution)/shard_map/ppermute | solution.py:72
  71.6 8.4 %collective-permute-done.18.late = f32[64,512]{1,0:T(8,128)S(1)} collective-permute-done((f32[64,512]{1,0:T(8,128)S(1)}, f32[64,512]{1,0:T(8,128)S(1)}, u32[]{:S(2)}, u32[]{:S(2)}) %collective-permute-start.18) | collective-permute-done | bytes 131104 | tf_op jit(solution)/shard_map/ppermute | solution.py:72
  80.0 0.8 finish.1
  (33 shorter events, 2.3 us)
Async XLA Ops:
  2.9 22.4 %copy-start = (f32[512]{0:T(512)S(1)}, f32[512]{0:T(512)}, u32[]{:S(2)}) copy-start(f32[512]{0:T(512)} %param.8) | copy-start | bytes 6148
  2.9 29.5 %collective-permute-start = (f32[1024,512]{1,0:T(8,128)}, f32[1024,512]{1,0:T(8,128)}, u32[]{:S(2)}, u32[]{:S(2)}) collective-permute-start(f32[1024,512]{1,0:T(8,128)} %pick_0.1), channel_id=1, source_target_pairs={{0,4},{1,5},{2,6},{3,7},{4,0},{5,1},{6,2},{7,3},{8,12},{9,13},{10,... | collective-permute-start | bytes 6291464 | tf_op jit(solution)/shard_map/ppermute | solution.py:72
  7.8 29.4 %collective-permute-start.3 = (f32[1024,512]{1,0:T(8,128)}, f32[1024,512]{1,0:T(8,128)S(1)}, u32[]{:S(2)}, u32[]{:S(2)}) collective-permute-start(f32[1024,512]{1,0:T(8,128)} %pick_1.1), channel_id=1, source_target_pairs={{0,1},{1,0},{2,3},{3,2},{4,5},{5,4},{6,7},{7,6},{8,9},{9,8},{10,11... | collective-permute-start | bytes 6291464 | tf_op jit(solution)/shard_map/ppermute | solution.py:72
  23.4 13.8 %collective-permute-start.4 = (f32[64,128]{1,0:T(8,128)S(1)}, f32[64,128]{1,0:T(8,128)S(1)}, u32[]{:S(2)}, u32[]{:S(2)}) collective-permute-start(f32[64,128]{1,0:T(8,128)S(1)} %bitcast.3), channel_id=1, source_target_pairs={{0,1},{1,0},{2,3},{3,2},{4,5},{5,4},{6,7},{7,6},{8,9},{9,8},{10,11... | collective-permute-start | bytes 98312 | tf_op jit(solution)/shard_map/ppermute | solution.py:72
  25.2 7.2 %collective-permute-start.1 = (f32[64,128]{1,0:T(8,128)S(1)}, f32[64,128]{1,0:T(8,128)S(1)}, u32[]{:S(2)}, u32[]{:S(2)}) collective-permute-start(f32[64,128]{1,0:T(8,128)S(1)} %bitcast.4), channel_id=1, source_target_pairs={{0,4},{1,5},{2,6},{3,7},{4,0},{5,1},{6,2},{7,3},{8,12},{9,13},{10,... | collective-permute-start | bytes 98312 | tf_op jit(solution)/shard_map/ppermute | solution.py:72
  34.1 11.7 %collective-permute-start.2 = (f32[264,512]{1,0:T(8,128)S(1)}, f32[264,512]{1,0:T(8,128)S(1)}, u32[]{:S(2)}, u32[]{:S(2)}) collective-permute-start(f32[264,512]{1,0:T(8,128)S(1)} %get-tuple-element.51), channel_id=1, source_target_pairs={{0,28},{1,29},{2,30},{3,31},{4,8},{5,9},{6,10},{7,11},{8,4},{9,5},... | collective-permute-start | bytes 1622024 | tf_op jit(solution)/shard_map/ppermute | solution.py:72
  38.2 9.4 %collective-permute-start.8 = (f32[264,512]{1,0:T(8,128)S(1)}, f32[264,512]{1,0:T(8,128)S(1)}, u32[]{:S(2)}, u32[]{:S(2)}) collective-permute-start(f32[264,512]{1,0:T(8,128)S(1)} %get-tuple-element.59), channel_id=1, source_target_pairs={{0,3},{1,2},{2,1},{3,0},{4,7},{5,6},{6,5},{7,4},{8,11},{9,10},{10,... | collective-permute-start | bytes 1622024 | tf_op jit(solution)/shard_map/ppermute | solution.py:72
  40.3 11.7 %collective-permute-start.7 = (f32[256,512]{1,0:T(8,128)S(1)}, f32[256,512]{1,0:T(8,128)S(1)}, u32[]{:S(2)}, u32[]{:S(2)}) collective-permute-start(f32[256,512]{1,0:T(8,128)S(1)} %meet_0_late.1), channel_id=1, source_target_pairs={{0,28},{1,29},{2,30},{3,31},{4,8},{5,9},{6,10},{7,11},{8,4},{9,5},... | collective-permute-start | bytes 1572872 | tf_op jit(solution)/shard_map/ppermute | solution.py:72
  43.2 10.1 %collective-permute-start.6 = (f32[256,512]{1,0:T(8,128)S(1)}, f32[256,512]{1,0:T(8,128)S(1)}, u32[]{:S(2)}, u32[]{:S(2)}) collective-permute-start(f32[256,512]{1,0:T(8,128)S(1)} %meet_1_late.1.refs_1_), channel_id=1, source_target_pairs={{0,3},{1,2},{2,1},{3,0},{4,7},{5,6},{6,5},{7,4},{8,11},{9,10},{10,... | collective-permute-start | bytes 1572872 | tf_op jit(solution)/shard_map/ppermute | solution.py:72
  45.9 10.3 %collective-permute-start.5 = (f32[136,512]{1,0:T(8,128)S(1)}, f32[136,512]{1,0:T(8,128)S(1)}, u32[]{:S(2)}, u32[]{:S(2)}) collective-permute-start(f32[136,512]{1,0:T(8,128)S(1)} %get-tuple-element.57), channel_id=1, source_target_pairs={{0,3},{1,2},{2,1},{3,0},{4,7},{5,6},{6,5},{7,4},{8,11},{9,10},{10,... | collective-permute-start | bytes 835592 | tf_op jit(solution)/shard_map/ppermute | solution.py:72
  47.7 11.1 %collective-permute-start.9 = (f32[136,512]{1,0:T(8,128)S(1)}, f32[136,512]{1,0:T(8,128)S(1)}, u32[]{:S(2)}, u32[]{:S(2)}) collective-permute-start(f32[136,512]{1,0:T(8,128)S(1)} %get-tuple-element.65), channel_id=1, source_target_pairs={{0,4},{1,5},{2,6},{3,7},{4,0},{5,1},{6,2},{7,3},{8,12},{9,13},{10,... | collective-permute-start | bytes 835592 | tf_op jit(solution)/shard_map/ppermute | solution.py:72
  52.1 8.3 %collective-permute-start.13 = (f32[128,512]{1,0:T(8,128)S(1)}, f32[128,512]{1,0:T(8,128)S(1)}, u32[]{:S(2)}, u32[]{:S(2)}) collective-permute-start(f32[128,512]{1,0:T(8,128)S(1)} %get-tuple-element.73), channel_id=1, source_target_pairs={{0,3},{1,2},{2,1},{3,0},{4,7},{5,6},{6,5},{7,4},{8,11},{9,10},{10,... | collective-permute-start | bytes 786440 | tf_op jit(solution)/shard_map/ppermute | solution.py:72
  53.4 7.1 %collective-permute-start.12 = (f32[128,512]{1,0:T(8,128)S(1)}, f32[128,512]{1,0:T(8,128)S(1)}, u32[]{:S(2)}, u32[]{:S(2)}) collective-permute-start(f32[128,512]{1,0:T(8,128)S(1)} %get-tuple-element.72), channel_id=1, source_target_pairs={{0,4},{1,5},{2,6},{3,7},{4,0},{5,1},{6,2},{7,3},{8,12},{9,13},{10,... | collective-permute-start | bytes 786440 | tf_op jit(solution)/shard_map/ppermute | solution.py:72
  56.2 10.4 %collective-permute-start.10 = (f32[72,512]{1,0:T(8,128)S(1)}, f32[72,512]{1,0:T(8,128)S(1)}, u32[]{:S(2)}, u32[]{:S(2)}) collective-permute-start(f32[72,512]{1,0:T(8,128)S(1)} %get-tuple-element.68), channel_id=1, source_target_pairs={{0,1},{1,0},{2,3},{3,2},{4,5},{5,4},{6,7},{7,6},{8,9},{9,8},{10,11... | collective-permute-start | bytes 442376 | tf_op jit(solution)/shard_map/ppermute | solution.py:72
  58.8 7.8 %collective-permute-start.11 = (f32[72,512]{1,0:T(8,128)S(1)}, f32[72,512]{1,0:T(8,128)S(1)}, u32[]{:S(2)}, u32[]{:S(2)}) collective-permute-start(f32[72,512]{1,0:T(8,128)S(1)} %get-tuple-element.69), channel_id=1, source_target_pairs={{0,28},{1,29},{2,30},{3,31},{4,8},{5,9},{6,10},{7,11},{8,4},{9,5},... | collective-permute-start | bytes 442376 | tf_op jit(solution)/shard_map/ppermute | solution.py:72
  60.5 6.1 %collective-permute-start.14 = (f32[64,512]{1,0:T(8,128)S(1)}, f32[64,512]{1,0:T(8,128)S(1)}, u32[]{:S(2)}, u32[]{:S(2)}) collective-permute-start(f32[64,512]{1,0:T(8,128)S(1)} %get-tuple-element.75.lower), channel_id=1, source_target_pairs={{0,32},{1,33},{2,34},{3,35},{4,36},{5,37},{6,38},{7,39},{8,40},{9,... | collective-permute-start | bytes 393224 | tf_op jit(solution)/shard_map/ppermute | solution.py:380
  60.6 8.0 %collective-permute-start.17 = (f32[64,512]{1,0:T(8,128)S(1)}, f32[64,512]{1,0:T(8,128)S(1)}, u32[]{:S(2)}, u32[]{:S(2)}) collective-permute-start(f32[64,512]{1,0:T(8,128)S(1)} %get-tuple-element.81), channel_id=1, source_target_pairs={{0,28},{1,29},{2,30},{3,31},{4,8},{5,9},{6,10},{7,11},{8,4},{9,5},... | collective-permute-start | bytes 393224 | tf_op jit(solution)/shard_map/ppermute | solution.py:72
  64.6 5.0 %collective-permute-start.16 = (f32[64,512]{1,0:T(8,128)S(1)}, f32[64,512]{1,0:T(8,128)S(1)}, u32[]{:S(2)}, u32[]{:S(2)}) collective-permute-start(f32[64,512]{1,0:T(8,128)S(1)} %get-tuple-element.80), channel_id=1, source_target_pairs={{0,1},{1,0},{2,3},{3,2},{4,5},{5,4},{6,7},{7,6},{8,9},{9,8},{10,11... | collective-permute-start | bytes 393224 | tf_op jit(solution)/shard_map/ppermute | solution.py:72
  66.7 13.4 %collective-permute-start.15 = (f32[72,512]{1,0:T(8,128)S(1)}, f32[72,512]{1,0:T(8,128)S(1)}, u32[]{:S(2)}, u32[]{:S(2)}) collective-permute-start(f32[72,512]{1,0:T(8,128)S(1)} %get-tuple-element.77), channel_id=1, source_target_pairs={{0,12},{1,13},{2,14},{3,15},{4,24},{5,25},{6,26},{7,27},{8,20},{9,... | collective-permute-start | bytes 442376 | tf_op jit(solution)/shard_map/ppermute | solution.py:72
  69.6 10.4 %collective-permute-start.18 = (f32[64,512]{1,0:T(8,128)S(1)}, f32[64,512]{1,0:T(8,128)S(1)}, u32[]{:S(2)}, u32[]{:S(2)}) collective-permute-start(f32[64,512]{1,0:T(8,128)S(1)} %get-tuple-element.82), channel_id=1, source_target_pairs={{0,12},{1,13},{2,14},{3,15},{4,24},{5,25},{6,26},{7,27},{8,20},{9,... | collective-permute-start | bytes 393224 | tf_op jit(solution)/shard_map/ppermute | solution.py:72

commit v4 on v3

--- a/solution.py
+++ b/solution.py
@@ -371,7 +371,7 @@
     for phase in (1, 2):
         for at in streams:
             arrived[at] = exchange(send[at], at[0], phase)
-        for at in streams:
+        for at in sorted(streams) if phase == 1 else streams:
             half, name = PART << (3 - phase), "add_{}_{}_{}".format(phase, *at)
             send[at], keep[at], squares[at] = add(half, keep[at], arrived[at], squares[at], after, name)
             after = keep[at]

time: 81.7 us -> 81.4 us (level)
  the two profiles are of different devices: /device:TPU:2 before, /device:TPU:6 now
where the time goes in v4:
time: 81.4 us; the launch traced here: 81 us
  starting transfers between devices  28.8 us (35%)
  Pallas kernels  21.6 us (27%)
  waiting for transfers between devices  18 us (22%)
  blocking collectives  12.4 us (15%)
    ppermute x18, starting transfers between devices, exchange(): return lax.ppermute(block, ('row', 'col'), PARTNERS[stream][phase])  28.7 us
    ppermute x18, waiting for transfers between devices, exchange(): return lax.ppermute(block, ('row', 'col'), PARTNERS[stream][phase])  18 us
    all_to_all x1, blocking collectives, local(): lax.all_to_all(packed, 'row', split_axis=0, concat_axis=0, tiled=True)  12.4 us
    pallas_call x19, Pallas kernels, call(): pl.pallas_call(kernel, out_shape=out_shape, in_specs=[HBM if n == from_hb...  7.42 us
    pallas_call x1, Pallas kernels, own_products(): pl.pallas_call(own_kernel, out_shape=[out, out], in_specs=[HBM] * 2 + [VM...  6.4 us
    pallas_call x2, Pallas kernels, pick(): pl.pallas_call(functools.partial(pick_kernel, stream), out_shape=jax.Shap...  5.73 us
  transfers between devices with their start and end apart: 19, of which 7 were waited for; matrix products, arithmetic and copies ran while one was open for 0% of the time, Pallas kernels for 22%

profile of v4, /device:TPU:6, one launch (start us, length us, event | category | flops | bytes accessed | tf_op | source)
XLA Modules:
  0.0 81.0 jit_solution(15171026201379752193)
XLA Ops:
  0.0 2.9 %pick_0.1 = f32[1024,512]{1,0:T(8,128)} custom-call(f32[2048,512]{1,0:T(8,128)} %upper.1), custom_call_target="tpu_custom_call" | custom-call | bytes 4194304 | tf_op jit(solution)/shard_map/pick_0/pallas_call | solution.py:134
  2.9 2.0 %collective-permute-start = (f32[1024,512]{1,0:T(8,128)}, f32[1024,512]{1,0:T(8,128)}, u32[]{:S(2)}, u32[]{:S(2)}) collective-permute-start(f32[1024,512]{1,0:T(8,128)} %pick_0.1), channel_id=1, source_target_pairs={{0,4},{1,5},{2,6},{3,7},{4,0},{5,1},{6,2},{7,3},{8,12},{9,13},{10,... | collective-permute-start | bytes 6291464 | tf_op jit(solution)/shard_map/ppermute | solution.py:72
  4.9 2.9 %pick_1.1 = f32[1024,512]{1,0:T(8,128)} custom-call(f32[2048,512]{1,0:T(8,128)} %vectors.3), custom_call_target="tpu_custom_call" | custom-call | bytes 4194304 | tf_op jit(solution)/shard_map/pick_1/pallas_call | solution.py:134
  7.8 0.9 %collective-permute-start.3 = (f32[1024,512]{1,0:T(8,128)}, f32[1024,512]{1,0:T(8,128)S(1)}, u32[]{:S(2)}, u32[]{:S(2)}) collective-permute-start(f32[1024,512]{1,0:T(8,128)} %pick_1.1), channel_id=1, source_target_pairs={{0,1},{1,0},{2,3},{3,2},{4,5},{5,4},{6,7},{7,6},{8,9},{9,8},{10,11... | collective-permute-start | bytes 6291464 | tf_op jit(solution)/shard_map/ppermute | solution.py:72
  8.7 1.3 %pack.1 = f32[64,128]{1,0:T(8,128)} custom-call(f32[2,64]{1,0:T(2,128)} %poles.1, f32[2,64]{1,0:T(2,128)} %weights.1, s32[2,64]{1,0:T(2,128)} %undeflated.1), custom_call_target="tpu_custom_call" | custom-call | tf_op jit(solution)/shard_map/pack/pallas_call | solution.py:155
  10.0 12.4 %all_to_all.11 = f32[8,8,128]{2,1,0:T(8,128)S(1)} all-to-all(f32[8,8,128]{2,1,0:T(8,128)} %bitcast.9), channel_id=1, replica_groups=mesh['row'=8,'col'=32] {'row'}, dimensions={0} | all-to-all | bytes 65536 | tf_op jit(solution)/shard_map/all_to_all | solution.py:356
  22.4 0.9 %collective-permute-start.4 = (f32[64,128]{1,0:T(8,128)S(1)}, f32[64,128]{1,0:T(8,128)S(1)}, u32[]{:S(2)}, u32[]{:S(2)}) collective-permute-start(f32[64,128]{1,0:T(8,128)S(1)} %bitcast.3), channel_id=1, source_target_pairs={{0,1},{1,0},{2,3},{3,2},{4,5},{5,4},{6,7},{7,6},{8,9},{9,8},{10,11... | collective-permute-start | bytes 98312 | tf_op jit(solution)/shard_map/ppermute | solution.py:72
  23.3 0.8 loewner.1
  24.0 6.4 %own.1 = (f32[1024,512]{1,0:T(8,128)S(1)}, f32[1024,512]{1,0:T(8,128)S(1)}) custom-call(f32[2048,512]{1,0:T(8,128)} %upper.1, f32[2048,512]{1,0:T(8,128)} %vectors.3, bf16[2,512,512]{2,1,0:T(8,128)(2,1)S(1)} %get-tuple-element.45.upper_part, bf16[2,512,512]{2,1,0:T(8,128)(2,1)S(1)} %get-tuple-element.46.lower_part), custom_call_target="tpu_custom_call" | custom-call | flops 6442450944 | bytes 8388608 | tf_op jit(solution)/shard_map/own/pallas_call | solution.py:221
  30.5 1.7 %meet_0.1 = (f32[264,512]{1,0:T(8,128)S(1)}, bf16[2,512,512]{2,1,0:T(8,128)(2,1)S(1)}, f32[8,512]{1,0:T(8,128)S(1)}, f32[1024,512]{1,0:T(8,128)S(1)}) custom-call(f32[1024,512]{1,0:T(8,128)} %collective-permute-done.vectors, f32[1024,512]{1,0:T(8,128)S(1)} %get-tuple-element.47.own, f32[1,512]{1,0:T(1,128)S(1)} %bitcast.7, ...), custom_call_target="tpu_custom_call" | custom-call | flops 1073741824 | bytes 1048576 | tf_op jit(solution)/shard_map/meet_0/pallas_call | solution.py:238
  32.2 5.0 %collective-permute-start.2 = (f32[264,512]{1,0:T(8,128)S(1)}, f32[264,512]{1,0:T(8,128)S(1)}, u32[]{:S(2)}, u32[]{:S(2)}) collective-permute-start(f32[264,512]{1,0:T(8,128)S(1)} %get-tuple-element.51), channel_id=1, source_target_pairs={{0,28},{1,29},{2,30},{3,31},{4,8},{5,9},{6,10},{7,11},{8,4},{9,5},... | collective-permute-start | bytes 1622024 | tf_op jit(solution)/shard_map/ppermute | solution.py:72
  37.2 1.0 %meet_1.1 = (f32[264,512]{1,0:T(8,128)S(1)}, bf16[2,512,512]{2,1,0:T(8,128)(2,1)S(1)}, f32[8,512]{1,0:T(8,128)S(1)}) custom-call(f32[1024,512]{1,0:T(8,128)S(1)} %collective-permute-done.3.vectors, f32[1024,512]{1,0:T(8,128)S(1)} %get-tuple-element.53.own, f32[1,512]{1,0:T(1,128)S(1)} %bitcast.8, f32[64,128]{1,0:T(8,128)S(1)} %collective-permute-done.4.poles, ...), custom_call_target="tpu_custom_call" | custom-call | flops 1073741824 | bytes 1048576 | tf_op jit(solution)/shard_map/meet_1/pallas_call | solution.py:238
  39.3 2.3 %collective-permute-start.8 = (f32[256,512]{1,0:T(8,128)S(1)}, f32[256,512]{1,0:T(8,128)S(1)}, u32[]{:S(2)}, u32[]{:S(2)}) collective-permute-start(f32[256,512]{1,0:T(8,128)S(1)} %meet_0_late.1), channel_id=1, source_target_pairs={{0,28},{1,29},{2,30},{3,31},{4,8},{5,9},{6,10},{7,11},{8,4},{9,5},... | collective-permute-start | bytes 1572872 | tf_op jit(solution)/shard_map/ppermute | solution.py:72
  41.6 0.6 meet_1_late.1.refs_1_
  42.2 3.0 %collective-permute-start.6 = (f32[256,512]{1,0:T(8,128)S(1)}, f32[256,512]{1,0:T(8,128)S(1)}, u32[]{:S(2)}, u32[]{:S(2)}) collective-permute-start(f32[256,512]{1,0:T(8,128)S(1)} %meet_1_late.1.refs_1_), channel_id=1, source_target_pairs={{0,3},{1,2},{2,1},{3,0},{4,7},{5,6},{6,5},{7,4},{8,11},{9,10},{10,... | collective-permute-start | bytes 1572872 | tf_op jit(solution)/shard_map/ppermute | solution.py:72
  45.2 0.6 rest_0_1.1.kept
  45.8 0.6 rest_0_0.1.kept
  47.6 2.5 %collective-permute-done.8.arrived = f32[256,512]{1,0:T(8,128)S(1)} collective-permute-done((f32[256,512]{1,0:T(8,128)S(1)}, f32[256,512]{1,0:T(8,128)S(1)}, u32[]{:S(2)}, u32[]{:S(2)}) %collective-permute-start.8) | collective-permute-done | bytes 524320 | tf_op jit(solution)/shard_map/ppermute | solution.py:72
  51.0 2.5 %collective-permute-start.13 = (f32[128,512]{1,0:T(8,128)S(1)}, f32[128,512]{1,0:T(8,128)S(1)}, u32[]{:S(2)}, u32[]{:S(2)}) collective-permute-start(f32[128,512]{1,0:T(8,128)S(1)} %get-tuple-element.73), channel_id=1, source_target_pairs={{0,3},{1,2},{2,1},{3,0},{4,7},{5,6},{6,5},{7,4},{8,11},{9,10},{10,... | collective-permute-start | bytes 786440 | tf_op jit(solution)/shard_map/ppermute | solution.py:72
  53.5 0.9 %collective-permute-done.6.arrived = f32[256,512]{1,0:T(8,128)S(1)} collective-permute-done((f32[256,512]{1,0:T(8,128)S(1)}, f32[256,512]{1,0:T(8,128)S(1)}, u32[]{:S(2)}, u32[]{:S(2)}) %collective-permute-start.6) | collective-permute-done | bytes 524320 | tf_op jit(solution)/shard_map/ppermute | solution.py:72
  54.5 1.2 %collective-permute-start.12 = (f32[128,512]{1,0:T(8,128)S(1)}, f32[128,512]{1,0:T(8,128)S(1)}, u32[]{:S(2)}, u32[]{:S(2)}) collective-permute-start(f32[128,512]{1,0:T(8,128)S(1)} %get-tuple-element.72), channel_id=1, source_target_pairs={{0,4},{1,5},{2,6},{3,7},{4,0},{5,1},{6,2},{7,3},{8,12},{9,13},{10,... | collective-permute-start | bytes 786440 | tf_op jit(solution)/shard_map/ppermute | solution.py:72
  55.7 1.7 %collective-permute-done.5.arrived = f32[136,512]{1,0:T(8,128)S(1)} collective-permute-done((f32[136,512]{1,0:T(8,128)S(1)}, f32[136,512]{1,0:T(8,128)S(1)}, u32[]{:S(2)}, u32[]{:S(2)}) %collective-permute-start.5) | collective-permute-done | bytes 278560 | tf_op jit(solution)/shard_map/ppermute | solution.py:72
  57.6 2.7 %collective-permute-start.11 = (f32[72,512]{1,0:T(8,128)S(1)}, f32[72,512]{1,0:T(8,128)S(1)}, u32[]{:S(2)}, u32[]{:S(2)}) collective-permute-start(f32[72,512]{1,0:T(8,128)S(1)} %get-tuple-element.69), channel_id=1, source_target_pairs={{0,28},{1,29},{2,30},{3,31},{4,8},{5,9},{6,10},{7,11},{8,4},{9,5},... | collective-permute-start | bytes 442376 | tf_op jit(solution)/shard_map/ppermute | solution.py:72
  60.3 2.2 %collective-permute-done.12.arrived = f32[128,512]{1,0:T(8,128)S(1)} collective-permute-done((f32[128,512]{1,0:T(8,128)S(1)}, f32[128,512]{1,0:T(8,128)S(1)}, u32[]{:S(2)}, u32[]{:S(2)}) %collective-permute-start.12) | collective-permute-done | bytes 262176 | tf_op jit(solution)/shard_map/ppermute | solution.py:72
  62.7 2.3 %collective-permute-start.17 = (f32[64,512]{1,0:T(8,128)S(1)}, f32[64,512]{1,0:T(8,128)S(1)}, u32[]{:S(2)}, u32[]{:S(2)}) collective-permute-start(f32[64,512]{1,0:T(8,128)S(1)} %get-tuple-element.81), channel_id=1, source_target_pairs={{0,28},{1,29},{2,30},{3,31},{4,8},{5,9},{6,10},{7,11},{8,4},{9,5},... | collective-permute-start | bytes 393224 | tf_op jit(solution)/shard_map/ppermute | solution.py:72
  65.0 0.6 collective-permute-start.16
  65.7 2.0 %collective-permute-start.15 = (f32[72,512]{1,0:T(8,128)S(1)}, f32[72,512]{1,0:T(8,128)S(1)}, u32[]{:S(2)}, u32[]{:S(2)}) collective-permute-start(f32[72,512]{1,0:T(8,128)S(1)} %get-tuple-element.77), channel_id=1, source_target_pairs={{0,12},{1,13},{2,14},{3,15},{4,24},{5,25},{6,26},{7,27},{8,20},{9,... | collective-permute-start | bytes 442376 | tf_op jit(solution)/shard_map/ppermute | solution.py:72
  67.7 1.3 %collective-permute-done.17.lower_in = f32[64,512]{1,0:T(8,128)S(1)} collective-permute-done((f32[64,512]{1,0:T(8,128)S(1)}, f32[64,512]{1,0:T(8,128)S(1)}, u32[]{:S(2)}, u32[]{:S(2)}) %collective-permute-start.17) | collective-permute-done | bytes 131104 | tf_op jit(solution)/shard_map/ppermute | solution.py:72
  69.0 1.0 %collective-permute-done.16.upper_in = f32[64,512]{1,0:T(8,128)S(1)} collective-permute-done((f32[64,512]{1,0:T(8,128)S(1)}, f32[64,512]{1,0:T(8,128)S(1)}, u32[]{:S(2)}, u32[]{:S(2)}) %collective-permute-start.16) | collective-permute-done | bytes 131104 | tf_op jit(solution)/shard_map/ppermute | solution.py:72
  70.0 2.0 %collective-permute-start.18 = (f32[64,512]{1,0:T(8,128)S(1)}, f32[64,512]{1,0:T(8,128)S(1)}, u32[]{:S(2)}, u32[]{:S(2)}) collective-permute-start(f32[64,512]{1,0:T(8,128)S(1)} %get-tuple-element.82), channel_id=1, source_target_pairs={{0,12},{1,13},{2,14},{3,15},{4,24},{5,25},{6,26},{7,27},{8,20},{9,... | collective-permute-start | bytes 393224 | tf_op jit(solution)/shard_map/ppermute | solution.py:72
  72.0 8.2 %collective-permute-done.18.late = f32[64,512]{1,0:T(8,128)S(1)} collective-permute-done((f32[64,512]{1,0:T(8,128)S(1)}, f32[64,512]{1,0:T(8,128)S(1)}, u32[]{:S(2)}, u32[]{:S(2)}) %collective-permute-start.18) | collective-permute-done | bytes 131104 | tf_op jit(solution)/shard_map/ppermute | solution.py:72
  80.2 0.8 finish.1
  (33 shorter events, 3.7 us)
Async XLA Ops:
  2.9 20.4 %copy-start = (f32[512]{0:T(512)S(1)}, f32[512]{0:T(512)}, u32[]{:S(2)}) copy-start(f32[512]{0:T(512)} %param.8) | copy-start | bytes 6148
  2.9 27.6 %collective-permute-start = (f32[1024,512]{1,0:T(8,128)}, f32[1024,512]{1,0:T(8,128)}, u32[]{:S(2)}, u32[]{:S(2)}) collective-permute-start(f32[1024,512]{1,0:T(8,128)} %pick_0.1), channel_id=1, source_target_pairs={{0,4},{1,5},{2,6},{3,7},{4,0},{5,1},{6,2},{7,3},{8,12},{9,13},{10,... | collective-permute-start | bytes 6291464 | tf_op jit(solution)/shard_map/ppermute | solution.py:72
  7.8 29.4 %collective-permute-start.3 = (f32[1024,512]{1,0:T(8,128)}, f32[1024,512]{1,0:T(8,128)S(1)}, u32[]{:S(2)}, u32[]{:S(2)}) collective-permute-start(f32[1024,512]{1,0:T(8,128)} %pick_1.1), channel_id=1, source_target_pairs={{0,1},{1,0},{2,3},{3,2},{4,5},{5,4},{6,7},{7,6},{8,9},{9,8},{10,11... | collective-permute-start | bytes 6291464 | tf_op jit(solution)/shard_map/ppermute | solution.py:72
  22.4 14.8 %collective-permute-start.4 = (f32[64,128]{1,0:T(8,128)S(1)}, f32[64,128]{1,0:T(8,128)S(1)}, u32[]{:S(2)}, u32[]{:S(2)}) collective-permute-start(f32[64,128]{1,0:T(8,128)S(1)} %bitcast.3), channel_id=1, source_target_pairs={{0,1},{1,0},{2,3},{3,2},{4,5},{5,4},{6,7},{7,6},{8,9},{9,8},{10,11... | collective-permute-start | bytes 98312 | tf_op jit(solution)/shard_map/ppermute | solution.py:72
  23.3 7.2 %collective-permute-start.1 = (f32[64,128]{1,0:T(8,128)S(1)}, f32[64,128]{1,0:T(8,128)S(1)}, u32[]{:S(2)}, u32[]{:S(2)}) collective-permute-start(f32[64,128]{1,0:T(8,128)S(1)} %bitcast.4), channel_id=1, source_target_pairs={{0,4},{1,5},{2,6},{3,7},{4,0},{5,1},{6,2},{7,3},{8,12},{9,13},{10,... | collective-permute-start | bytes 98312 | tf_op jit(solution)/shard_map/ppermute | solution.py:72
  32.2 14.8 %collective-permute-start.2 = (f32[264,512]{1,0:T(8,128)S(1)}, f32[264,512]{1,0:T(8,128)S(1)}, u32[]{:S(2)}, u32[]{:S(2)}) collective-permute-start(f32[264,512]{1,0:T(8,128)S(1)} %get-tuple-element.51), channel_id=1, source_target_pairs={{0,28},{1,29},{2,30},{3,31},{4,8},{5,9},{6,10},{7,11},{8,4},{9,5},... | collective-permute-start | bytes 1622024 | tf_op jit(solution)/shard_map/ppermute | solution.py:72
  38.2 12.0 %collective-permute-start.7 = (f32[264,512]{1,0:T(8,128)S(1)}, f32[264,512]{1,0:T(8,128)S(1)}, u32[]{:S(2)}, u32[]{:S(2)}) collective-permute-start(f32[264,512]{1,0:T(8,128)S(1)} %get-tuple-element.59), channel_id=1, source_target_pairs={{0,3},{1,2},{2,1},{3,0},{4,7},{5,6},{6,5},{7,4},{8,11},{9,10},{10,... | collective-permute-start | bytes 1622024 | tf_op jit(solution)/shard_map/ppermute | solution.py:72
  39.3 10.8 %collective-permute-start.8 = (f32[256,512]{1,0:T(8,128)S(1)}, f32[256,512]{1,0:T(8,128)S(1)}, u32[]{:S(2)}, u32[]{:S(2)}) collective-permute-start(f32[256,512]{1,0:T(8,128)S(1)} %meet_0_late.1), channel_id=1, source_target_pairs={{0,28},{1,29},{2,30},{3,31},{4,8},{5,9},{6,10},{7,11},{8,4},{9,5},... | collective-permute-start | bytes 1572872 | tf_op jit(solution)/shard_map/ppermute | solution.py:72
  42.2 12.2 %collective-permute-start.6 = (f32[256,512]{1,0:T(8,128)S(1)}, f32[256,512]{1,0:T(8,128)S(1)}, u32[]{:S(2)}, u32[]{:S(2)}) collective-permute-start(f32[256,512]{1,0:T(8,128)S(1)} %meet_1_late.1.refs_1_), channel_id=1, source_target_pairs={{0,3},{1,2},{2,1},{3,0},{4,7},{5,6},{6,5},{7,4},{8,11},{9,10},{10,... | collective-permute-start | bytes 1572872 | tf_op jit(solution)/shard_map/ppermute | solution.py:72
  47.1 10.3 %collective-permute-start.5 = (f32[136,512]{1,0:T(8,128)S(1)}, f32[136,512]{1,0:T(8,128)S(1)}, u32[]{:S(2)}, u32[]{:S(2)}) collective-permute-start(f32[136,512]{1,0:T(8,128)S(1)} %get-tuple-element.57), channel_id=1, source_target_pairs={{0,3},{1,2},{2,1},{3,0},{4,7},{5,6},{6,5},{7,4},{8,11},{9,10},{10,... | collective-permute-start | bytes 835592 | tf_op jit(solution)/shard_map/ppermute | solution.py:72
  50.3 7.3 %collective-permute-start.9 = (f32[136,512]{1,0:T(8,128)S(1)}, f32[136,512]{1,0:T(8,128)S(1)}, u32[]{:S(2)}, u32[]{:S(2)}) collective-permute-start(f32[136,512]{1,0:T(8,128)S(1)} %get-tuple-element.65), channel_id=1, source_target_pairs={{0,4},{1,5},{2,6},{3,7},{4,0},{5,1},{6,2},{7,3},{8,12},{9,13},{10,... | collective-permute-start | bytes 835592 | tf_op jit(solution)/shard_map/ppermute | solution.py:72
  51.0 9.3 %collective-permute-start.13 = (f32[128,512]{1,0:T(8,128)S(1)}, f32[128,512]{1,0:T(8,128)S(1)}, u32[]{:S(2)}, u32[]{:S(2)}) collective-permute-start(f32[128,512]{1,0:T(8,128)S(1)} %get-tuple-element.73), channel_id=1, source_target_pairs={{0,3},{1,2},{2,1},{3,0},{4,7},{5,6},{6,5},{7,4},{8,11},{9,10},{10,... | collective-permute-start | bytes 786440 | tf_op jit(solution)/shard_map/ppermute | solution.py:72
  54.5 8.0 %collective-permute-start.12 = (f32[128,512]{1,0:T(8,128)S(1)}, f32[128,512]{1,0:T(8,128)S(1)}, u32[]{:S(2)}, u32[]{:S(2)}) collective-permute-start(f32[128,512]{1,0:T(8,128)S(1)} %get-tuple-element.72), channel_id=1, source_target_pairs={{0,4},{1,5},{2,6},{3,7},{4,0},{5,1},{6,2},{7,3},{8,12},{9,13},{10,... | collective-permute-start | bytes 786440 | tf_op jit(solution)/shard_map/ppermute | solution.py:72
  57.5 8.1 %collective-permute-start.10 = (f32[72,512]{1,0:T(8,128)S(1)}, f32[72,512]{1,0:T(8,128)S(1)}, u32[]{:S(2)}, u32[]{:S(2)}) collective-permute-start(f32[72,512]{1,0:T(8,128)S(1)} %get-tuple-element.68), channel_id=1, source_target_pairs={{0,1},{1,0},{2,3},{3,2},{4,5},{5,4},{6,7},{7,6},{8,9},{9,8},{10,11... | collective-permute-start | bytes 442376 | tf_op jit(solution)/shard_map/ppermute | solution.py:72
  57.6 8.0 %collective-permute-start.11 = (f32[72,512]{1,0:T(8,128)S(1)}, f32[72,512]{1,0:T(8,128)S(1)}, u32[]{:S(2)}, u32[]{:S(2)}) collective-permute-start(f32[72,512]{1,0:T(8,128)S(1)} %get-tuple-element.69), channel_id=1, source_target_pairs={{0,28},{1,29},{2,30},{3,31},{4,8},{5,9},{6,10},{7,11},{8,4},{9,5},... | collective-permute-start | bytes 442376 | tf_op jit(solution)/shard_map/ppermute | solution.py:72
  62.6 3.0 %collective-permute-start.14 = (f32[64,512]{1,0:T(8,128)S(1)}, f32[64,512]{1,0:T(8,128)S(1)}, u32[]{:S(2)}, u32[]{:S(2)}) collective-permute-start(f32[64,512]{1,0:T(8,128)S(1)} %get-tuple-element.75.lower), channel_id=1, source_target_pairs={{0,32},{1,33},{2,34},{3,35},{4,36},{5,37},{6,38},{7,39},{8,40},{9,... | collective-permute-start | bytes 393224 | tf_op jit(solution)/shard_map/ppermute | solution.py:380
  62.7 6.3 %collective-permute-start.17 = (f32[64,512]{1,0:T(8,128)S(1)}, f32[64,512]{1,0:T(8,128)S(1)}, u32[]{:S(2)}, u32[]{:S(2)}) collective-permute-start(f32[64,512]{1,0:T(8,128)S(1)} %get-tuple-element.81), channel_id=1, source_target_pairs={{0,28},{1,29},{2,30},{3,31},{4,8},{5,9},{6,10},{7,11},{8,4},{9,5},... | collective-permute-start | bytes 393224 | tf_op jit(solution)/shard_map/ppermute | solution.py:72
  65.0 5.0 %collective-permute-start.16 = (f32[64,512]{1,0:T(8,128)S(1)}, f32[64,512]{1,0:T(8,128)S(1)}, u32[]{:S(2)}, u32[]{:S(2)}) collective-permute-start(f32[64,512]{1,0:T(8,128)S(1)} %get-tuple-element.80), channel_id=1, source_target_pairs={{0,1},{1,0},{2,3},{3,2},{4,5},{5,4},{6,7},{7,6},{8,9},{9,8},{10,11... | collective-permute-start | bytes 393224 | tf_op jit(solution)/shard_map/ppermute | solution.py:72
  65.7 14.6 %collective-permute-start.15 = (f32[72,512]{1,0:T(8,128)S(1)}, f32[72,512]{1,0:T(8,128)S(1)}, u32[]{:S(2)}, u32[]{:S(2)}) collective-permute-start(f32[72,512]{1,0:T(8,128)S(1)} %get-tuple-element.77), channel_id=1, source_target_pairs={{0,12},{1,13},{2,14},{3,15},{4,24},{5,25},{6,26},{7,27},{8,20},{9,... | collective-permute-start | bytes 442376 | tf_op jit(solution)/shard_map/ppermute | solution.py:72
  70.0 10.2 %collective-permute-start.18 = (f32[64,512]{1,0:T(8,128)S(1)}, f32[64,512]{1,0:T(8,128)S(1)}, u32[]{:S(2)}, u32[]{:S(2)}) collective-permute-start(f32[64,512]{1,0:T(8,128)S(1)} %get-tuple-element.82), channel_id=1, source_target_pairs={{0,12},{1,13},{2,14},{3,15},{4,24},{5,25},{6,26},{7,27},{8,20},{9,... | collective-permute-start | bytes 393224 | tf_op jit(solution)/shard_map/ppermute | solution.py:72

commit v5 on v4

--- a/solution.py
+++ b/solution.py
@@ -66,6 +66,9 @@
 
 CORES = [(device, device ^ 32) for device in range(256)]
 PARTNERS = tuple(tuple(partners(stream, phase) for phase in range(5)) for stream in range(2))
+
+
+POLES = tuple([(source ^ 32, to) for source, to in PARTNERS[stream][0]] for stream in range(2))
 
 
 def exchange(block, stream, phase):
@@ -196,6 +199,25 @@
     )(roots, poles)
 
 
+def partner_loewner_kernel(
+    roots, to_upper, to_lower, upper_own, lower_own, _, upper, lower, upper_squares, lower_squares
+):
+    upper_squares[...] = upper_own[...] + loewner(0, roots[...], to_upper[...], upper)
+    lower_squares[...] = lower_own[...] + loewner(1, roots[...], to_lower[...], lower)
+
+
+def partner_loewner(*arrays):
+    return pl.pallas_call(
+        partner_loewner_kernel,
+        out_shape=[COEFFICIENT, COEFFICIENT, SQUARES, SQUARES],
+        in_specs=[VMEM] * 6,
+        out_specs=[VMEM] * 4,
+        compiler_params=KERNEL,
+        cost_estimate=pl.CostEstimate(flops=1 << 23, bytes_accessed=2 << 20, transcendentals=1 << 19),
+        name="partner",
+    )(*arrays)
+
+
 def product(vectors, high, low):
     a = vectors.astype(BF16)
     rest = (vectors - a.astype(F32)).astype(BF16)
@@ -247,48 +269,38 @@
     )(*arrays)
 
 
-def meet_kernel(stream, vectors, own, roots, poles, squares, send, coefficient, sums, rows, sems):
+def meet_kernel(vectors, own, coefficient, squares, send, rows, sems):
     copies = []
     for n, first in enumerate((256, 768, 0, 512)):
         at = pl.ds(first, 256)
         copies.append(pltpu.make_async_copy(vectors.at[at, :], rows.at[at, :], sems.at[n]))
         copies[n].start()
-    total = squares[...] + loewner(stream, roots[...], poles[...], coefficient)
-    send[256:, :] = total
-    sums[...] = total
+    send[256:, :] = squares[...]
     copies[0].wait()
     send[:256, :] = own[256:512, :] + product(rows[256:512, :], coefficient[0], coefficient[1])
     for copy in copies[1:]:
         copy.wait()
 
 
-def meet_direct(stream, *arrays):
+def meet_direct_kernel(vectors, own, coefficient, squares, send):
+    send[256:, :] = squares[...]
+    send[:256, :] = own[256:512, :] + product(vectors[256:512, :], coefficient[0], coefficient[1])
+
+
+def meet(*arrays):
     return call(
-        functools.partial(meet_direct_kernel, stream),
-        [shape(256, True), COEFFICIENT, SQUARES],
+        meet_kernel,
+        [shape(256, True), shape(16 * ROWS)],
         *arrays,
-        name=f"meet_{stream}",
-        flops=1 << 30,
-    )
-
-
-def meet(stream, *arrays):
-    return call(
-        functools.partial(meet_kernel, stream),
-        [shape(256, True), COEFFICIENT, SQUARES, shape(16 * ROWS)],
-        *arrays,
-        name=f"meet_{stream}",
+        name="meet_0",
         flops=1 << 30,
         from_hbm=0,
         scratch=[pltpu.SemaphoreType.DMA((4,))],
     )
 
 
-def meet_direct_kernel(stream, vectors, own, roots, poles, squares, send, coefficient, sums):
-    total = squares[...] + loewner(stream, roots[...], poles[...], coefficient)
-    send[256:, :] = total
-    sums[...] = total
-    send[:256, :] = own[256:512, :] + product(vectors[256:512, :], coefficient[0], coefficient[1])
+def meet_direct(*arrays):
+    return call(meet_direct_kernel, shape(256, True), *arrays, name="meet_1", flops=1 << 30)
 
 
 def add_own_kernel(first, vectors, own, coefficient, out):
@@ -354,15 +366,16 @@
     raw[0] = pltpu.with_memory_space_constraint(raw[0], pltpu.HBM)
     packed = pack(pole_values, pole_weights, undeflated)
     poles = lax.all_to_all(packed, "row", split_axis=0, concat_axis=0, tiled=True)
-    met = [exchange(poles, s, 0) for s in (0, 1)]
+    met = [lax.ppermute(poles, ("row", "col"), POLES[s]) for s in (0, 1)]
     *coefficients, upper_squares, lower_squares = own_loewner(roots, poles)
     own = own_products(*vectors, *coefficients)
 
     streams = [(s, batch) for batch in (0, 1) for s in (0, 1)]
     squares = {(s, 1): None for s in (0, 1)} | {(0, 0): upper_squares, (1, 0): lower_squares}
-    send, keep, arrived, parts = {}, {}, {}, {}
-    send[0, 0], parts[0], squares[0, 0], raw[0] = meet(0, raw[0], own[0], roots, met[0], squares[0, 0])
-    send[1, 0], parts[1], squares[1, 0] = meet_direct(1, raw[1], own[1], roots, met[1], squares[1, 0])
+    send, keep, arrived = {}, {}, {}
+    *parts, squares[0, 0], squares[1, 0] = partner_loewner(roots, *met, squares[0, 0], squares[1, 0], own[1])
+    send[0, 0], raw[0] = meet(raw[0], own[0], parts[0], squares[0, 0])
+    send[1, 0] = meet_direct(raw[1], own[1], parts[1], squares[1, 0])
     for s in (0, 1):
         send[s, 1] = add_own(768, raw[s], own[s], parts[s], name=f"meet_{s}_late")
     for s, batch in streams:

time: 81.4 us -> 81.2 us (level)
  the two profiles are of different devices: /device:TPU:6 before, /device:TPU:2 now
where the time goes in v5:
time: 81.2 us; the launch traced here: 80.7 us
  starting transfers between devices  29.6 us (36%)
  Pallas kernels  22 us (27%)
  waiting for transfers between devices  15.2 us (19%)
  blocking collectives  13.7 us (17%)
    ppermute x16, starting transfers between devices, exchange(): return lax.ppermute(block, ('row', 'col'), PARTNERS[stream][phase])  28.9 us
    ppermute x16, waiting for transfers between devices, exchange(): return lax.ppermute(block, ('row', 'col'), PARTNERS[stream][phase])  15.2 us
    all_to_all x1, blocking collectives, local(): lax.all_to_all(packed, 'row', split_axis=0, concat_axis=0, tiled=True)  13.7 us
    pallas_call x19, Pallas kernels, call(): pl.pallas_call(kernel, out_shape=out_shape, in_specs=[HBM if n == from_hb...  6.98 us
    pallas_call x1, Pallas kernels, own_products(): pl.pallas_call(own_kernel, out_shape=[out, out], in_specs=[HBM] * 2 + [VM...  6.42 us
    pallas_call x2, Pallas kernels, pick(): pl.pallas_call(functools.partial(pick_kernel, stream), out_shape=jax.Shap...  5.73 us
  transfers between devices with their start and end apart: 19, of which 5 were waited for; matrix products, arithmetic and copies ran while one was open for 0% of the time, Pallas kernels for 23%

profile of v5, /device:TPU:2, one launch (start us, length us, event | category | flops | bytes accessed | tf_op | source)
XLA Modules:
  0.0 80.7 jit_solution(14460605977088271787)
XLA Ops:
  0.0 2.9 %pick_0.1 = f32[1024,512]{1,0:T(8,128)} custom-call(f32[2048,512]{1,0:T(8,128)} %upper.1), custom_call_target="tpu_custom_call" | custom-call | bytes 4194304 | tf_op jit(solution)/shard_map/pick_0/pallas_call | solution.py:137
  2.9 2.0 %collective-permute-start = (f32[1024,512]{1,0:T(8,128)}, f32[1024,512]{1,0:T(8,128)}, u32[]{:S(2)}, u32[]{:S(2)}) collective-permute-start(f32[1024,512]{1,0:T(8,128)} %pick_0.1), channel_id=1, source_target_pairs={{0,4},{1,5},{2,6},{3,7},{4,0},{5,1},{6,2},{7,3},{8,12},{9,13},{10,... | collective-permute-start | bytes 6291464 | tf_op jit(solution)/shard_map/ppermute | solution.py:75
  4.9 2.9 %pick_1.1 = f32[1024,512]{1,0:T(8,128)} custom-call(f32[2048,512]{1,0:T(8,128)} %vectors.3), custom_call_target="tpu_custom_call" | custom-call | bytes 4194304 | tf_op jit(solution)/shard_map/pick_1/pallas_call | solution.py:137
  7.8 0.6 collective-permute-start.4
  8.4 1.3 %pack.1 = f32[64,128]{1,0:T(8,128)} custom-call(f32[2,64]{1,0:T(2,128)} %poles.1, f32[2,64]{1,0:T(2,128)} %weights.1, s32[2,64]{1,0:T(2,128)} %undeflated.1), custom_call_target="tpu_custom_call" | custom-call | tf_op jit(solution)/shard_map/pack/pallas_call | solution.py:158
  9.7 13.7 %all_to_all.11 = f32[8,8,128]{2,1,0:T(8,128)S(1)} all-to-all(f32[8,8,128]{2,1,0:T(8,128)} %bitcast.8), channel_id=1, replica_groups=mesh['row'=8,'col'=32] {'row'}, dimensions={0} | all-to-all | bytes 65536 | tf_op jit(solution)/shard_map/all_to_all | solution.py:368
  24.0 0.8 loewner.1
  24.7 6.4 %own.1 = (f32[1024,512]{1,0:T(8,128)S(1)}, f32[1024,512]{1,0:T(8,128)S(1)}) custom-call(f32[2048,512]{1,0:T(8,128)} %upper.1, f32[2048,512]{1,0:T(8,128)} %vectors.3, bf16[2,512,512]{2,1,0:T(8,128)(2,1)S(1)} %get-tuple-element.44.upper_part, bf16[2,512,512]{2,1,0:T(8,128)(2,1)S(1)} %get-tuple-element.45.lower_part), custom_call_target="tpu_custom_call" | custom-call | flops 6442450944 | bytes 8388608 | tf_op jit(solution)/shard_map/own/pallas_call | solution.py:243
  31.2 0.8 partner.1
  32.0 1.7 %meet_0.1 = (f32[264,512]{1,0:T(8,128)S(1)}, f32[1024,512]{1,0:T(8,128)S(1)}) custom-call(f32[1024,512]{1,0:T(8,128)} %collective-permute-done.vectors, f32[1024,512]{1,0:T(8,128)S(1)} %get-tuple-element.46.own, bf16[2,512,512]{2,1,0:T(8,128)(2,1)S(1)} %get-tuple-element.50.coefficient, f32[8,512]{1,0:T(8,128)S(1)} %get-tuple-element.51.squares.refs_0_), custom_call_target="tpu_custom_call" | custom-call | flops 1073741824 | bytes 1048576 | tf_op jit(solution)/shard_map/meet_0/pallas_call | solution.py:260
  33.6 3.6 %collective-permute-start.3 = (f32[264,512]{1,0:T(8,128)S(1)}, f32[264,512]{1,0:T(8,128)S(1)}, u32[]{:S(2)}, u32[]{:S(2)}) collective-permute-start(f32[264,512]{1,0:T(8,128)S(1)} %get-tuple-element.53), channel_id=1, source_target_pairs={{0,28},{1,29},{2,30},{3,31},{4,8},{5,9},{6,10},{7,11},{8,4},{9,5},... | collective-permute-start | bytes 1622024 | tf_op jit(solution)/shard_map/ppermute | solution.py:75
  37.9 1.6 %collective-permute-start.7 = (f32[264,512]{1,0:T(8,128)S(1)}, f32[264,512]{1,0:T(8,128)S(1)}, u32[]{:S(2)}, u32[]{:S(2)}) collective-permute-start(f32[264,512]{1,0:T(8,128)S(1)} %meet_1.1), channel_id=1, source_target_pairs={{0,3},{1,2},{2,1},{3,0},{4,7},{5,6},{6,5},{7,4},{8,11},{9,10},{10,... | collective-permute-start | bytes 1622024 | tf_op jit(solution)/shard_map/ppermute | solution.py:75
  40.0 2.2 %collective-permute-start.8 = (f32[256,512]{1,0:T(8,128)S(1)}, f32[256,512]{1,0:T(8,128)S(1)}, u32[]{:S(2)}, u32[]{:S(2)}) collective-permute-start(f32[256,512]{1,0:T(8,128)S(1)} %meet_0_late.1), channel_id=1, source_target_pairs={{0,28},{1,29},{2,30},{3,31},{4,8},{5,9},{6,10},{7,11},{8,4},{9,5},... | collective-permute-start | bytes 1572872 | tf_op jit(solution)/shard_map/ppermute | solution.py:75
  42.2 0.6 meet_1_late.1.refs_1_
  42.8 0.8 collective-permute-start.6
  44.2 0.6 rest_0_0.1.kept
  44.8 0.6 rest_1_0.1.kept
  45.5 1.6 %collective-permute-start.5 = (f32[136,512]{1,0:T(8,128)S(1)}, f32[136,512]{1,0:T(8,128)S(1)}, u32[]{:S(2)}, u32[]{:S(2)}) collective-permute-start(f32[136,512]{1,0:T(8,128)S(1)} %get-tuple-element.56), channel_id=1, source_target_pairs={{0,3},{1,2},{2,1},{3,0},{4,7},{5,6},{6,5},{7,4},{8,11},{9,10},{10,... | collective-permute-start | bytes 835592 | tf_op jit(solution)/shard_map/ppermute | solution.py:75
  47.1 3.4 %collective-permute-done.8.arrived = f32[256,512]{1,0:T(8,128)S(1)} collective-permute-done((f32[256,512]{1,0:T(8,128)S(1)}, f32[256,512]{1,0:T(8,128)S(1)}, u32[]{:S(2)}, u32[]{:S(2)}) %collective-permute-start.8) | collective-permute-done | bytes 524320 | tf_op jit(solution)/shard_map/ppermute | solution.py:75
  51.3 1.6 %collective-permute-start.13 = (f32[128,512]{1,0:T(8,128)S(1)}, f32[128,512]{1,0:T(8,128)S(1)}, u32[]{:S(2)}, u32[]{:S(2)}) collective-permute-start(f32[128,512]{1,0:T(8,128)S(1)} %get-tuple-element.71), channel_id=1, source_target_pairs={{0,3},{1,2},{2,1},{3,0},{4,7},{5,6},{6,5},{7,4},{8,11},{9,10},{10,... | collective-permute-start | bytes 786440 | tf_op jit(solution)/shard_map/ppermute | solution.py:75
  53.0 2.1 %collective-permute-start.12 = (f32[128,512]{1,0:T(8,128)S(1)}, f32[128,512]{1,0:T(8,128)S(1)}, u32[]{:S(2)}, u32[]{:S(2)}) collective-permute-start(f32[128,512]{1,0:T(8,128)S(1)} %get-tuple-element.70), channel_id=1, source_target_pairs={{0,4},{1,5},{2,6},{3,7},{4,0},{5,1},{6,2},{7,3},{8,12},{9,13},{10,... | collective-permute-start | bytes 786440 | tf_op jit(solution)/shard_map/ppermute | solution.py:75
  55.1 0.8 collective-permute-done.5.arrived
  55.9 1.3 %collective-permute-done.9.arrived = f32[136,512]{1,0:T(8,128)S(1)} collective-permute-done((f32[136,512]{1,0:T(8,128)S(1)}, f32[136,512]{1,0:T(8,128)S(1)}, u32[]{:S(2)}, u32[]{:S(2)}) %collective-permute-start.9) | collective-permute-done | bytes 278560 | tf_op jit(solution)/shard_map/ppermute | solution.py:75
  57.3 3.0 %collective-permute-start.11 = (f32[72,512]{1,0:T(8,128)S(1)}, f32[72,512]{1,0:T(8,128)S(1)}, u32[]{:S(2)}, u32[]{:S(2)}) collective-permute-start(f32[72,512]{1,0:T(8,128)S(1)} %get-tuple-element.67), channel_id=1, source_target_pairs={{0,28},{1,29},{2,30},{3,31},{4,8},{5,9},{6,10},{7,11},{8,4},{9,5},... | collective-permute-start | bytes 442376 | tf_op jit(solution)/shard_map/ppermute | solution.py:75
  60.4 1.4 %collective-permute-start.10 = (f32[72,512]{1,0:T(8,128)S(1)}, f32[72,512]{1,0:T(8,128)S(1)}, u32[]{:S(2)}, u32[]{:S(2)}) collective-permute-start(f32[72,512]{1,0:T(8,128)S(1)} %get-tuple-element.66), channel_id=1, source_target_pairs={{0,1},{1,0},{2,3},{3,2},{4,5},{5,4},{6,7},{7,6},{8,9},{9,8},{10,11... | collective-permute-start | bytes 442376 | tf_op jit(solution)/shard_map/ppermute | solution.py:75
  61.9 2.9 %collective-permute-start.17 = (f32[64,512]{1,0:T(8,128)S(1)}, f32[64,512]{1,0:T(8,128)S(1)}, u32[]{:S(2)}, u32[]{:S(2)}) collective-permute-start(f32[64,512]{1,0:T(8,128)S(1)} %get-tuple-element.79), channel_id=1, source_target_pairs={{0,28},{1,29},{2,30},{3,31},{4,8},{5,9},{6,10},{7,11},{8,4},{9,5},... | collective-permute-start | bytes 393224 | tf_op jit(solution)/shard_map/ppermute | solution.py:75
  64.8 1.4 %collective-permute-start.16 = (f32[64,512]{1,0:T(8,128)S(1)}, f32[64,512]{1,0:T(8,128)S(1)}, u32[]{:S(2)}, u32[]{:S(2)}) collective-permute-start(f32[64,512]{1,0:T(8,128)S(1)} %get-tuple-element.78), channel_id=1, source_target_pairs={{0,1},{1,0},{2,3},{3,2},{4,5},{5,4},{6,7},{7,6},{8,9},{9,8},{10,11... | collective-permute-start | bytes 393224 | tf_op jit(solution)/shard_map/ppermute | solution.py:75
  66.3 2.0 %collective-permute-start.15 = (f32[72,512]{1,0:T(8,128)S(1)}, f32[72,512]{1,0:T(8,128)S(1)}, u32[]{:S(2)}, u32[]{:S(2)}) collective-permute-start(f32[72,512]{1,0:T(8,128)S(1)} %get-tuple-element.75), channel_id=1, source_target_pairs={{0,12},{1,13},{2,14},{3,15},{4,24},{5,25},{6,26},{7,27},{8,20},{9,... | collective-permute-start | bytes 442376 | tf_op jit(solution)/shard_map/ppermute | solution.py:75
  68.3 1.5 %collective-permute-done.16.upper_in = f32[64,512]{1,0:T(8,128)S(1)} collective-permute-done((f32[64,512]{1,0:T(8,128)S(1)}, f32[64,512]{1,0:T(8,128)S(1)}, u32[]{:S(2)}, u32[]{:S(2)}) %collective-permute-start.16) | collective-permute-done | bytes 131104 | tf_op jit(solution)/shard_map/ppermute | solution.py:75
  69.8 2.0 %collective-permute-start.18 = (f32[64,512]{1,0:T(8,128)S(1)}, f32[64,512]{1,0:T(8,128)S(1)}, u32[]{:S(2)}, u32[]{:S(2)}) collective-permute-start(f32[64,512]{1,0:T(8,128)S(1)} %get-tuple-element.80), channel_id=1, source_target_pairs={{0,12},{1,13},{2,14},{3,15},{4,24},{5,25},{6,26},{7,27},{8,20},{9,... | collective-permute-start | bytes 393224 | tf_op jit(solution)/shard_map/ppermute | solution.py:75
  71.8 8.1 %collective-permute-done.18.late = f32[64,512]{1,0:T(8,128)S(1)} collective-permute-done((f32[64,512]{1,0:T(8,128)S(1)}, f32[64,512]{1,0:T(8,128)S(1)}, u32[]{:S(2)}, u32[]{:S(2)}) %collective-permute-start.18) | collective-permute-done | bytes 131104 | tf_op jit(solution)/shard_map/ppermute | solution.py:75
  80.0 0.8 finish.1
  (34 shorter events, 3.5 us)
Async XLA Ops:
  2.9 21.1 %copy-start = (f32[512]{0:T(512)S(1)}, f32[512]{0:T(512)}, u32[]{:S(2)}) copy-start(f32[512]{0:T(512)} %param.8) | copy-start | bytes 6148
  2.9 29.1 %collective-permute-start = (f32[1024,512]{1,0:T(8,128)}, f32[1024,512]{1,0:T(8,128)}, u32[]{:S(2)}, u32[]{:S(2)}) collective-permute-start(f32[1024,512]{1,0:T(8,128)} %pick_0.1), channel_id=1, source_target_pairs={{0,4},{1,5},{2,6},{3,7},{4,0},{5,1},{6,2},{7,3},{8,12},{9,13},{10,... | collective-permute-start | bytes 6291464 | tf_op jit(solution)/shard_map/ppermute | solution.py:75
  7.8 29.5 %collective-permute-start.4 = (f32[1024,512]{1,0:T(8,128)}, f32[1024,512]{1,0:T(8,128)S(1)}, u32[]{:S(2)}, u32[]{:S(2)}) collective-permute-start(f32[1024,512]{1,0:T(8,128)} %pick_1.1), channel_id=1, source_target_pairs={{0,1},{1,0},{2,3},{3,2},{4,5},{5,4},{6,7},{7,6},{8,9},{9,8},{10,11... | collective-permute-start | bytes 6291464 | tf_op jit(solution)/shard_map/ppermute | solution.py:75
  23.4 7.8 %collective-permute-start.1 = (f32[64,128]{1,0:T(8,128)S(1)}, f32[64,128]{1,0:T(8,128)S(1)}, u32[]{:S(2)}, u32[]{:S(2)}) collective-permute-start(f32[64,128]{1,0:T(8,128)S(1)} %bitcast.3), channel_id=1, source_target_pairs={{32,4},{33,5},{34,6},{35,7},{36,0},{37,1},{38,2},{39,3},{40,12},{4... | collective-permute-start | bytes 98312 | tf_op jit(solution)/shard_map/ppermute | solution.py:369
  24.0 7.2 %collective-permute-start.2 = (f32[64,128]{1,0:T(8,128)S(1)}, f32[64,128]{1,0:T(8,128)S(1)}, u32[]{:S(2)}, u32[]{:S(2)}) collective-permute-start(f32[64,128]{1,0:T(8,128)S(1)} %bitcast.4), channel_id=1, source_target_pairs={{32,1},{33,0},{34,3},{35,2},{36,5},{37,4},{38,7},{39,6},{40,9},{41... | collective-permute-start | bytes 98312 | tf_op jit(solution)/shard_map/ppermute | solution.py:369
  33.6 11.8 %collective-permute-start.3 = (f32[264,512]{1,0:T(8,128)S(1)}, f32[264,512]{1,0:T(8,128)S(1)}, u32[]{:S(2)}, u32[]{:S(2)}) collective-permute-start(f32[264,512]{1,0:T(8,128)S(1)} %get-tuple-element.53), channel_id=1, source_target_pairs={{0,28},{1,29},{2,30},{3,31},{4,8},{5,9},{6,10},{7,11},{8,4},{9,5},... | collective-permute-start | bytes 1622024 | tf_op jit(solution)/shard_map/ppermute | solution.py:75
  37.9 12.7 %collective-permute-start.7 = (f32[264,512]{1,0:T(8,128)S(1)}, f32[264,512]{1,0:T(8,128)S(1)}, u32[]{:S(2)}, u32[]{:S(2)}) collective-permute-start(f32[264,512]{1,0:T(8,128)S(1)} %meet_1.1), channel_id=1, source_target_pairs={{0,3},{1,2},{2,1},{3,0},{4,7},{5,6},{6,5},{7,4},{8,11},{9,10},{10,... | collective-permute-start | bytes 1622024 | tf_op jit(solution)/shard_map/ppermute | solution.py:75
  40.0 10.5 %collective-permute-start.8 = (f32[256,512]{1,0:T(8,128)S(1)}, f32[256,512]{1,0:T(8,128)S(1)}, u32[]{:S(2)}, u32[]{:S(2)}) collective-permute-start(f32[256,512]{1,0:T(8,128)S(1)} %meet_0_late.1), channel_id=1, source_target_pairs={{0,28},{1,29},{2,30},{3,31},{4,8},{5,9},{6,10},{7,11},{8,4},{9,5},... | collective-permute-start | bytes 1572872 | tf_op jit(solution)/shard_map/ppermute | solution.py:75
  42.8 10.2 %collective-permute-start.6 = (f32[256,512]{1,0:T(8,128)S(1)}, f32[256,512]{1,0:T(8,128)S(1)}, u32[]{:S(2)}, u32[]{:S(2)}) collective-permute-start(f32[256,512]{1,0:T(8,128)S(1)} %meet_1_late.1.refs_1_), channel_id=1, source_target_pairs={{0,3},{1,2},{2,1},{3,0},{4,7},{5,6},{6,5},{7,4},{8,11},{9,10},{10,... | collective-permute-start | bytes 1572872 | tf_op jit(solution)/shard_map/ppermute | solution.py:75
  45.5 10.4 %collective-permute-start.5 = (f32[136,512]{1,0:T(8,128)S(1)}, f32[136,512]{1,0:T(8,128)S(1)}, u32[]{:S(2)}, u32[]{:S(2)}) collective-permute-start(f32[136,512]{1,0:T(8,128)S(1)} %get-tuple-element.56), channel_id=1, source_target_pairs={{0,3},{1,2},{2,1},{3,0},{4,7},{5,6},{6,5},{7,4},{8,11},{9,10},{10,... | collective-permute-start | bytes 835592 | tf_op jit(solution)/shard_map/ppermute | solution.py:75
  50.6 6.6 %collective-permute-start.9 = (f32[136,512]{1,0:T(8,128)S(1)}, f32[136,512]{1,0:T(8,128)S(1)}, u32[]{:S(2)}, u32[]{:S(2)}) collective-permute-start(f32[136,512]{1,0:T(8,128)S(1)} %get-tuple-element.63), channel_id=1, source_target_pairs={{0,4},{1,5},{2,6},{3,7},{4,0},{5,1},{6,2},{7,3},{8,12},{9,13},{10,... | collective-permute-start | bytes 835592 | tf_op jit(solution)/shard_map/ppermute | solution.py:75
  51.3 10.4 %collective-permute-start.13 = (f32[128,512]{1,0:T(8,128)S(1)}, f32[128,512]{1,0:T(8,128)S(1)}, u32[]{:S(2)}, u32[]{:S(2)}) collective-permute-start(f32[128,512]{1,0:T(8,128)S(1)} %get-tuple-element.71), channel_id=1, source_target_pairs={{0,3},{1,2},{2,1},{3,0},{4,7},{5,6},{6,5},{7,4},{8,11},{9,10},{10,... | collective-permute-start | bytes 786440 | tf_op jit(solution)/shard_map/ppermute | solution.py:75
  53.0 8.7 %collective-permute-start.12 = (f32[128,512]{1,0:T(8,128)S(1)}, f32[128,512]{1,0:T(8,128)S(1)}, u32[]{:S(2)}, u32[]{:S(2)}) collective-permute-start(f32[128,512]{1,0:T(8,128)S(1)} %get-tuple-element.70), channel_id=1, source_target_pairs={{0,4},{1,5},{2,6},{3,7},{4,0},{5,1},{6,2},{7,3},{8,12},{9,13},{10,... | collective-permute-start | bytes 786440 | tf_op jit(solution)/shard_map/ppermute | solution.py:75
  57.3 8.9 %collective-permute-start.11 = (f32[72,512]{1,0:T(8,128)S(1)}, f32[72,512]{1,0:T(8,128)S(1)}, u32[]{:S(2)}, u32[]{:S(2)}) collective-permute-start(f32[72,512]{1,0:T(8,128)S(1)} %get-tuple-element.67), channel_id=1, source_target_pairs={{0,28},{1,29},{2,30},{3,31},{4,8},{5,9},{6,10},{7,11},{8,4},{9,5},... | collective-permute-start | bytes 442376 | tf_op jit(solution)/shard_map/ppermute | solution.py:75
  60.4 5.9 %collective-permute-start.10 = (f32[72,512]{1,0:T(8,128)S(1)}, f32[72,512]{1,0:T(8,128)S(1)}, u32[]{:S(2)}, u32[]{:S(2)}) collective-permute-start(f32[72,512]{1,0:T(8,128)S(1)} %get-tuple-element.66), channel_id=1, source_target_pairs={{0,1},{1,0},{2,3},{3,2},{4,5},{5,4},{6,7},{7,6},{8,9},{9,8},{10,11... | collective-permute-start | bytes 442376 | tf_op jit(solution)/shard_map/ppermute | solution.py:75
  61.8 4.4 %collective-permute-start.14 = (f32[64,512]{1,0:T(8,128)S(1)}, f32[64,512]{1,0:T(8,128)S(1)}, u32[]{:S(2)}, u32[]{:S(2)}) collective-permute-start(f32[64,512]{1,0:T(8,128)S(1)} %get-tuple-element.73.lower), channel_id=1, source_target_pairs={{0,32},{1,33},{2,34},{3,35},{4,36},{5,37},{6,38},{7,39},{8,40},{9,... | collective-permute-start | bytes 393224 | tf_op jit(solution)/shard_map/ppermute | solution.py:393
  61.9 6.4 %collective-permute-start.17 = (f32[64,512]{1,0:T(8,128)S(1)}, f32[64,512]{1,0:T(8,128)S(1)}, u32[]{:S(2)}, u32[]{:S(2)}) collective-permute-start(f32[64,512]{1,0:T(8,128)S(1)} %get-tuple-element.79), channel_id=1, source_target_pairs={{0,28},{1,29},{2,30},{3,31},{4,8},{5,9},{6,10},{7,11},{8,4},{9,5},... | collective-permute-start | bytes 393224 | tf_op jit(solution)/shard_map/ppermute | solution.py:75
  64.8 5.0 %collective-permute-start.16 = (f32[64,512]{1,0:T(8,128)S(1)}, f32[64,512]{1,0:T(8,128)S(1)}, u32[]{:S(2)}, u32[]{:S(2)}) collective-permute-start(f32[64,512]{1,0:T(8,128)S(1)} %get-tuple-element.78), channel_id=1, source_target_pairs={{0,1},{1,0},{2,3},{3,2},{4,5},{5,4},{6,7},{7,6},{8,9},{9,8},{10,11... | collective-permute-start | bytes 393224 | tf_op jit(solution)/shard_map/ppermute | solution.py:75
  66.3 13.7 %collective-permute-start.15 = (f32[72,512]{1,0:T(8,128)S(1)}, f32[72,512]{1,0:T(8,128)S(1)}, u32[]{:S(2)}, u32[]{:S(2)}) collective-permute-start(f32[72,512]{1,0:T(8,128)S(1)} %get-tuple-element.75), channel_id=1, source_target_pairs={{0,12},{1,13},{2,14},{3,15},{4,24},{5,25},{6,26},{7,27},{8,20},{9,... | collective-permute-start | bytes 442376 | tf_op jit(solution)/shard_map/ppermute | solution.py:75
  69.8 10.1 %collective-permute-start.18 = (f32[64,512]{1,0:T(8,128)S(1)}, f32[64,512]{1,0:T(8,128)S(1)}, u32[]{:S(2)}, u32[]{:S(2)}) collective-permute-start(f32[64,512]{1,0:T(8,128)S(1)} %get-tuple-element.80), channel_id=1, source_target_pairs={{0,12},{1,13},{2,14},{3,15},{4,24},{5,25},{6,26},{7,27},{8,20},{9,... | collective-permute-start | bytes 393224 | tf_op jit(solution)/shard_map/ppermute | solution.py:75

commit v6 on v5

--- a/solution.py
+++ b/solution.py
@@ -303,7 +303,8 @@
     return call(meet_direct_kernel, shape(256, True), *arrays, name="meet_1", flops=1 << 30)
 
 
-def add_own_kernel(first, vectors, own, coefficient, out):
+def add_own_kernel(first, vectors, own, coefficient, *refs):
+    out = refs[-1]
     at = slice(first, first + 256)
     out[...] = own[at, :] + product(vectors[at, :], coefficient[0], coefficient[1])
 
@@ -378,13 +379,16 @@
     send[1, 0] = meet_direct(raw[1], own[1], parts[1], squares[1, 0])
     for s in (0, 1):
         send[s, 1] = add_own(768, raw[s], own[s], parts[s], name=f"meet_{s}_late")
-    for s, batch in streams:
-        keep[s, batch] = add_own(512 * batch, raw[s], own[s], parts[s], name=f"rest_{s}_{batch}")
+    for s in (0, 1):
+        keep[s, 0] = add_own(0, raw[s], own[s], parts[s], name=f"rest_{s}_0")
     after = send[1, 1]
     for phase in (1, 2):
         for at in streams:
             arrived[at] = exchange(send[at], at[0], phase)
         for at in sorted(streams) if phase == 1 else streams:
+            if phase == 1 and at[1]:
+                s = at[0]
+                keep[at] = add_own(512, raw[s], own[s], parts[s], after, name=f"rest_{s}_1")
             half, name = PART << (3 - phase), "add_{}_{}_{}".format(phase, *at)
             send[at], keep[at], squares[at] = add(half, keep[at], arrived[at], squares[at], after, name)
             after = keep[at]

time: 81.2 us -> 82.8 us (1.020)
  starting transfers between devices: 29.6 us -> 30.6 us
    ppermute x16, starting transfers between devices: 28.9 us -> 29.9 us  [exchange(): return lax.ppermute(block, ('row', 'col'), PARTNERS[stream][phase])]
  transfers between devices with their start and end apart: 19 -> 19, of which waited for: 5 -> 5; matrix products, arithmetic and copies ran while one was open for 0% -> 0% of each run, Pallas kernels for 23% -> 22%
where the time goes in v6:
time: 82.8 us; the launch traced here: 82.4 us
  starting transfers between devices  30.6 us (37%)
  Pallas kernels  22 us (27%)
  waiting for transfers between devices  16 us (19%)
  blocking collectives  13.7 us (17%)
    ppermute x16, starting transfers between devices, exchange(): return lax.ppermute(block, ('row', 'col'), PARTNERS[stream][phase])  29.9 us
    ppermute x16, waiting for transfers between devices, exchange(): return lax.ppermute(block, ('row', 'col'), PARTNERS[stream][phase])  16 us
    all_to_all x1, blocking collectives, local(): lax.all_to_all(packed, 'row', split_axis=0, concat_axis=0, tiled=True)  13.7 us
    pallas_call x19, Pallas kernels, call(): pl.pallas_call(kernel, out_shape=out_shape, in_specs=[HBM if n == from_hb...  6.97 us
    pallas_call x1, Pallas kernels, own_products(): pl.pallas_call(own_kernel, out_shape=[out, out], in_specs=[HBM] * 2 + [VM...  6.42 us
    pallas_call x2, Pallas kernels, pick(): pl.pallas_call(functools.partial(pick_kernel, stream), out_shape=jax.Shap...  5.73 us
  transfers between devices with their start and end apart: 19, of which 5 were waited for; matrix products, arithmetic and copies ran while one was open for 0% of the time, Pallas kernels for 22%

profile of v6, /device:TPU:2, one launch (start us, length us, event | category | flops | bytes accessed | tf_op | source)
XLA Modules:
  0.0 82.4 jit_solution(14709939733230253902)
XLA Ops:
  0.0 2.9 %pick_0.1 = f32[1024,512]{1,0:T(8,128)} custom-call(f32[2048,512]{1,0:T(8,128)} %upper.1), custom_call_target="tpu_custom_call" | custom-call | bytes 4194304 | tf_op jit(solution)/shard_map/pick_0/pallas_call | solution.py:137
  2.9 2.0 %collective-permute-start = (f32[1024,512]{1,0:T(8,128)}, f32[1024,512]{1,0:T(8,128)}, u32[]{:S(2)}, u32[]{:S(2)}) collective-permute-start(f32[1024,512]{1,0:T(8,128)} %pick_0.1), channel_id=1, source_target_pairs={{0,4},{1,5},{2,6},{3,7},{4,0},{5,1},{6,2},{7,3},{8,12},{9,13},{10,... | collective-permute-start | bytes 6291464 | tf_op jit(solution)/shard_map/ppermute | solution.py:75
  4.9 2.9 %pick_1.1 = f32[1024,512]{1,0:T(8,128)} custom-call(f32[2048,512]{1,0:T(8,128)} %vectors.3), custom_call_target="tpu_custom_call" | custom-call | bytes 4194304 | tf_op jit(solution)/shard_map/pick_1/pallas_call | solution.py:137
  7.8 0.6 collective-permute-start.4
  8.4 1.3 %pack.1 = f32[64,128]{1,0:T(8,128)} custom-call(f32[2,64]{1,0:T(2,128)} %poles.1, f32[2,64]{1,0:T(2,128)} %weights.1, s32[2,64]{1,0:T(2,128)} %undeflated.1), custom_call_target="tpu_custom_call" | custom-call | tf_op jit(solution)/shard_map/pack/pallas_call | solution.py:158
  9.7 13.7 %all_to_all.11 = f32[8,8,128]{2,1,0:T(8,128)S(1)} all-to-all(f32[8,8,128]{2,1,0:T(8,128)} %bitcast.8), channel_id=1, replica_groups=mesh['row'=8,'col'=32] {'row'}, dimensions={0} | all-to-all | bytes 65536 | tf_op jit(solution)/shard_map/all_to_all | solution.py:369
  24.0 0.8 loewner.1
  24.7 6.4 %own.1 = (f32[1024,512]{1,0:T(8,128)S(1)}, f32[1024,512]{1,0:T(8,128)S(1)}) custom-call(f32[2048,512]{1,0:T(8,128)} %upper.1, f32[2048,512]{1,0:T(8,128)} %vectors.3, bf16[2,512,512]{2,1,0:T(8,128)(2,1)S(1)} %get-tuple-element.44.upper_part, bf16[2,512,512]{2,1,0:T(8,128)(2,1)S(1)} %get-tuple-element.45.lower_part), custom_call_target="tpu_custom_call" | custom-call | flops 6442450944 | bytes 8388608 | tf_op jit(solution)/shard_map/own/pallas_call | solution.py:243
  31.2 0.8 partner.1
  32.0 1.7 %meet_0.1 = (f32[264,512]{1,0:T(8,128)S(1)}, f32[1024,512]{1,0:T(8,128)S(1)}) custom-call(f32[1024,512]{1,0:T(8,128)} %collective-permute-done.vectors, f32[1024,512]{1,0:T(8,128)S(1)} %get-tuple-element.46.own, bf16[2,512,512]{2,1,0:T(8,128)(2,1)S(1)} %get-tuple-element.50.coefficient, f32[8,512]{1,0:T(8,128)S(1)} %get-tuple-element.51.squares.refs_0_), custom_call_target="tpu_custom_call" | custom-call | flops 1073741824 | bytes 1048576 | tf_op jit(solution)/shard_map/meet_0/pallas_call | solution.py:260
  33.6 3.6 %collective-permute-start.3 = (f32[264,512]{1,0:T(8,128)S(1)}, f32[264,512]{1,0:T(8,128)S(1)}, u32[]{:S(2)}, u32[]{:S(2)}) collective-permute-start(f32[264,512]{1,0:T(8,128)S(1)} %get-tuple-element.53), channel_id=1, source_target_pairs={{0,28},{1,29},{2,30},{3,31},{4,8},{5,9},{6,10},{7,11},{8,4},{9,5},... | collective-permute-start | bytes 1622024 | tf_op jit(solution)/shard_map/ppermute | solution.py:75
  37.9 1.6 %collective-permute-start.6 = (f32[264,512]{1,0:T(8,128)S(1)}, f32[264,512]{1,0:T(8,128)S(1)}, u32[]{:S(2)}, u32[]{:S(2)}) collective-permute-start(f32[264,512]{1,0:T(8,128)S(1)} %meet_1.1), channel_id=1, source_target_pairs={{0,3},{1,2},{2,1},{3,0},{4,7},{5,6},{6,5},{7,4},{8,11},{9,10},{10,... | collective-permute-start | bytes 1622024 | tf_op jit(solution)/shard_map/ppermute | solution.py:75
  40.0 2.2 %collective-permute-start.7 = (f32[256,512]{1,0:T(8,128)S(1)}, f32[256,512]{1,0:T(8,128)S(1)}, u32[]{:S(2)}, u32[]{:S(2)}) collective-permute-start(f32[256,512]{1,0:T(8,128)S(1)} %meet_0_late.1), channel_id=1, source_target_pairs={{0,28},{1,29},{2,30},{3,31},{4,8},{5,9},{6,10},{7,11},{8,4},{9,5},... | collective-permute-start | bytes 1572872 | tf_op jit(solution)/shard_map/ppermute | solution.py:75
  42.2 0.6 meet_1_late.1.refs_1_
  42.8 0.8 collective-permute-start.8
  43.6 0.6 rest_0_0.1.kept
  44.2 0.6 rest_1_0.1.kept
  44.9 1.7 %collective-permute-start.5 = (f32[136,512]{1,0:T(8,128)S(1)}, f32[136,512]{1,0:T(8,128)S(1)}, u32[]{:S(2)}, u32[]{:S(2)}) collective-permute-start(f32[136,512]{1,0:T(8,128)S(1)} %get-tuple-element.56), channel_id=1, source_target_pairs={{0,3},{1,2},{2,1},{3,0},{4,7},{5,6},{6,5},{7,4},{8,11},{9,10},{10,... | collective-permute-start | bytes 835592 | tf_op jit(solution)/shard_map/ppermute | solution.py:75
  47.2 3.3 %collective-permute-done.7.arrived = f32[256,512]{1,0:T(8,128)S(1)} collective-permute-done((f32[256,512]{1,0:T(8,128)S(1)}, f32[256,512]{1,0:T(8,128)S(1)}, u32[]{:S(2)}, u32[]{:S(2)}) %collective-permute-start.7) | collective-permute-done | bytes 524320 | tf_op jit(solution)/shard_map/ppermute | solution.py:75
  50.7 1.6 %collective-permute-start.13 = (f32[128,512]{1,0:T(8,128)S(1)}, f32[128,512]{1,0:T(8,128)S(1)}, u32[]{:S(2)}, u32[]{:S(2)}) collective-permute-start(f32[128,512]{1,0:T(8,128)S(1)} %get-tuple-element.71), channel_id=1, source_target_pairs={{0,3},{1,2},{2,1},{3,0},{4,7},{5,6},{6,5},{7,4},{8,11},{9,10},{10,... | collective-permute-start | bytes 786440 | tf_op jit(solution)/shard_map/ppermute | solution.py:75
  52.4 0.6 rest_1_1.1.kept
  53.1 2.0 %collective-permute-start.12 = (f32[128,512]{1,0:T(8,128)S(1)}, f32[128,512]{1,0:T(8,128)S(1)}, u32[]{:S(2)}, u32[]{:S(2)}) collective-permute-start(f32[128,512]{1,0:T(8,128)S(1)} %get-tuple-element.70), channel_id=1, source_target_pairs={{0,4},{1,5},{2,6},{3,7},{4,0},{5,1},{6,2},{7,3},{8,12},{9,13},{10,... | collective-permute-start | bytes 786440 | tf_op jit(solution)/shard_map/ppermute | solution.py:75
  55.1 0.8 %collective-permute-done.5.arrived = f32[136,512]{1,0:T(8,128)S(1)} collective-permute-done((f32[136,512]{1,0:T(8,128)S(1)}, f32[136,512]{1,0:T(8,128)S(1)}, u32[]{:S(2)}, u32[]{:S(2)}) %collective-permute-start.5) | collective-permute-done | bytes 278560 | tf_op jit(solution)/shard_map/ppermute | solution.py:75
  55.9 2.7 %collective-permute-start.10 = (f32[72,512]{1,0:T(8,128)S(1)}, f32[72,512]{1,0:T(8,128)S(1)}, u32[]{:S(2)}, u32[]{:S(2)}) collective-permute-start(f32[72,512]{1,0:T(8,128)S(1)} %get-tuple-element.66), channel_id=1, source_target_pairs={{0,1},{1,0},{2,3},{3,2},{4,5},{5,4},{6,7},{7,6},{8,9},{9,8},{10,11... | collective-permute-start | bytes 442376 | tf_op jit(solution)/shard_map/ppermute | solution.py:75
  58.7 1.7 %collective-permute-start.11 = (f32[72,512]{1,0:T(8,128)S(1)}, f32[72,512]{1,0:T(8,128)S(1)}, u32[]{:S(2)}, u32[]{:S(2)}) collective-permute-start(f32[72,512]{1,0:T(8,128)S(1)} %get-tuple-element.67), channel_id=1, source_target_pairs={{0,28},{1,29},{2,30},{3,31},{4,8},{5,9},{6,10},{7,11},{8,4},{9,5},... | collective-permute-start | bytes 442376 | tf_op jit(solution)/shard_map/ppermute | solution.py:75
  60.9 2.1 %collective-permute-start.16 = (f32[64,512]{1,0:T(8,128)S(1)}, f32[64,512]{1,0:T(8,128)S(1)}, u32[]{:S(2)}, u32[]{:S(2)}) collective-permute-start(f32[64,512]{1,0:T(8,128)S(1)} %get-tuple-element.78), channel_id=1, source_target_pairs={{0,1},{1,0},{2,3},{3,2},{4,5},{5,4},{6,7},{7,6},{8,9},{9,8},{10,11... | collective-permute-start | bytes 393224 | tf_op jit(solution)/shard_map/ppermute | solution.py:75
  63.0 3.2 %collective-permute-start.17 = (f32[64,512]{1,0:T(8,128)S(1)}, f32[64,512]{1,0:T(8,128)S(1)}, u32[]{:S(2)}, u32[]{:S(2)}) collective-permute-start(f32[64,512]{1,0:T(8,128)S(1)} %get-tuple-element.79), channel_id=1, source_target_pairs={{0,28},{1,29},{2,30},{3,31},{4,8},{5,9},{6,10},{7,11},{8,4},{9,5},... | collective-permute-start | bytes 393224 | tf_op jit(solution)/shard_map/ppermute | solution.py:75
  66.3 2.0 %collective-permute-start.15 = (f32[72,512]{1,0:T(8,128)S(1)}, f32[72,512]{1,0:T(8,128)S(1)}, u32[]{:S(2)}, u32[]{:S(2)}) collective-permute-start(f32[72,512]{1,0:T(8,128)S(1)} %get-tuple-element.75), channel_id=1, source_target_pairs={{0,12},{1,13},{2,14},{3,15},{4,24},{5,25},{6,26},{7,27},{8,20},{9,... | collective-permute-start | bytes 442376 | tf_op jit(solution)/shard_map/ppermute | solution.py:75
  68.3 3.5 %collective-permute-done.17.lower_in = f32[64,512]{1,0:T(8,128)S(1)} collective-permute-done((f32[64,512]{1,0:T(8,128)S(1)}, f32[64,512]{1,0:T(8,128)S(1)}, u32[]{:S(2)}, u32[]{:S(2)}) %collective-permute-start.17) | collective-permute-done | bytes 131104 | tf_op jit(solution)/shard_map/ppermute | solution.py:75
  71.8 2.0 %collective-permute-start.18 = (f32[64,512]{1,0:T(8,128)S(1)}, f32[64,512]{1,0:T(8,128)S(1)}, u32[]{:S(2)}, u32[]{:S(2)}) collective-permute-start(f32[64,512]{1,0:T(8,128)S(1)} %get-tuple-element.80), channel_id=1, source_target_pairs={{0,12},{1,13},{2,14},{3,15},{4,24},{5,25},{6,26},{7,27},{8,20},{9,... | collective-permute-start | bytes 393224 | tf_op jit(solution)/shard_map/ppermute | solution.py:75
  73.8 7.8 %collective-permute-done.18.late = f32[64,512]{1,0:T(8,128)S(1)} collective-permute-done((f32[64,512]{1,0:T(8,128)S(1)}, f32[64,512]{1,0:T(8,128)S(1)}, u32[]{:S(2)}, u32[]{:S(2)}) %collective-permute-start.18) | collective-permute-done | bytes 131104 | tf_op jit(solution)/shard_map/ppermute | solution.py:75
  81.7 0.8 finish.1
  (34 shorter events, 3.4 us)
Async XLA Ops:
  2.9 21.1 %copy-start = (f32[512]{0:T(512)S(1)}, f32[512]{0:T(512)}, u32[]{:S(2)}) copy-start(f32[512]{0:T(512)} %param.8) | copy-start | bytes 6148
  2.9 29.1 %collective-permute-start = (f32[1024,512]{1,0:T(8,128)}, f32[1024,512]{1,0:T(8,128)}, u32[]{:S(2)}, u32[]{:S(2)}) collective-permute-start(f32[1024,512]{1,0:T(8,128)} %pick_0.1), channel_id=1, source_target_pairs={{0,4},{1,5},{2,6},{3,7},{4,0},{5,1},{6,2},{7,3},{8,12},{9,13},{10,... | collective-permute-start | bytes 6291464 | tf_op jit(solution)/shard_map/ppermute | solution.py:75
  7.8 29.5 %collective-permute-start.4 = (f32[1024,512]{1,0:T(8,128)}, f32[1024,512]{1,0:T(8,128)S(1)}, u32[]{:S(2)}, u32[]{:S(2)}) collective-permute-start(f32[1024,512]{1,0:T(8,128)} %pick_1.1), channel_id=1, source_target_pairs={{0,1},{1,0},{2,3},{3,2},{4,5},{5,4},{6,7},{7,6},{8,9},{9,8},{10,11... | collective-permute-start | bytes 6291464 | tf_op jit(solution)/shard_map/ppermute | solution.py:75
  23.4 7.8 %collective-permute-start.1 = (f32[64,128]{1,0:T(8,128)S(1)}, f32[64,128]{1,0:T(8,128)S(1)}, u32[]{:S(2)}, u32[]{:S(2)}) collective-permute-start(f32[64,128]{1,0:T(8,128)S(1)} %bitcast.3), channel_id=1, source_target_pairs={{32,4},{33,5},{34,6},{35,7},{36,0},{37,1},{38,2},{39,3},{40,12},{4... | collective-permute-start | bytes 98312 | tf_op jit(solution)/shard_map/ppermute | solution.py:370
  24.0 7.2 %collective-permute-start.2 = (f32[64,128]{1,0:T(8,128)S(1)}, f32[64,128]{1,0:T(8,128)S(1)}, u32[]{:S(2)}, u32[]{:S(2)}) collective-permute-start(f32[64,128]{1,0:T(8,128)S(1)} %bitcast.4), channel_id=1, source_target_pairs={{32,1},{33,0},{34,3},{35,2},{36,5},{37,4},{38,7},{39,6},{40,9},{41... | collective-permute-start | bytes 98312 | tf_op jit(solution)/shard_map/ppermute | solution.py:370
  33.6 11.2 %collective-permute-start.3 = (f32[264,512]{1,0:T(8,128)S(1)}, f32[264,512]{1,0:T(8,128)S(1)}, u32[]{:S(2)}, u32[]{:S(2)}) collective-permute-start(f32[264,512]{1,0:T(8,128)S(1)} %get-tuple-element.53), channel_id=1, source_target_pairs={{0,28},{1,29},{2,30},{3,31},{4,8},{5,9},{6,10},{7,11},{8,4},{9,5},... | collective-permute-start | bytes 1622024 | tf_op jit(solution)/shard_map/ppermute | solution.py:75
  37.9 12.7 %collective-permute-start.6 = (f32[264,512]{1,0:T(8,128)S(1)}, f32[264,512]{1,0:T(8,128)S(1)}, u32[]{:S(2)}, u32[]{:S(2)}) collective-permute-start(f32[264,512]{1,0:T(8,128)S(1)} %meet_1.1), channel_id=1, source_target_pairs={{0,3},{1,2},{2,1},{3,0},{4,7},{5,6},{6,5},{7,4},{8,11},{9,10},{10,... | collective-permute-start | bytes 1622024 | tf_op jit(solution)/shard_map/ppermute | solution.py:75
  40.0 10.5 %collective-permute-start.7 = (f32[256,512]{1,0:T(8,128)S(1)}, f32[256,512]{1,0:T(8,128)S(1)}, u32[]{:S(2)}, u32[]{:S(2)}) collective-permute-start(f32[256,512]{1,0:T(8,128)S(1)} %meet_0_late.1), channel_id=1, source_target_pairs={{0,28},{1,29},{2,30},{3,31},{4,8},{5,9},{6,10},{7,11},{8,4},{9,5},... | collective-permute-start | bytes 1572872 | tf_op jit(solution)/shard_map/ppermute | solution.py:75
  42.8 10.2 %collective-permute-start.8 = (f32[256,512]{1,0:T(8,128)S(1)}, f32[256,512]{1,0:T(8,128)S(1)}, u32[]{:S(2)}, u32[]{:S(2)}) collective-permute-start(f32[256,512]{1,0:T(8,128)S(1)} %meet_1_late.1.refs_1_), channel_id=1, source_target_pairs={{0,3},{1,2},{2,1},{3,0},{4,7},{5,6},{6,5},{7,4},{8,11},{9,10},{10,... | collective-permute-start | bytes 1572872 | tf_op jit(solution)/shard_map/ppermute | solution.py:75
  44.9 11.0 %collective-permute-start.5 = (f32[136,512]{1,0:T(8,128)S(1)}, f32[136,512]{1,0:T(8,128)S(1)}, u32[]{:S(2)}, u32[]{:S(2)}) collective-permute-start(f32[136,512]{1,0:T(8,128)S(1)} %get-tuple-element.56), channel_id=1, source_target_pairs={{0,3},{1,2},{2,1},{3,0},{4,7},{5,6},{6,5},{7,4},{8,11},{9,10},{10,... | collective-permute-start | bytes 835592 | tf_op jit(solution)/shard_map/ppermute | solution.py:75
  50.6 8.0 %collective-permute-start.9 = (f32[136,512]{1,0:T(8,128)S(1)}, f32[136,512]{1,0:T(8,128)S(1)}, u32[]{:S(2)}, u32[]{:S(2)}) collective-permute-start(f32[136,512]{1,0:T(8,128)S(1)} %get-tuple-element.63), channel_id=1, source_target_pairs={{0,4},{1,5},{2,6},{3,7},{4,0},{5,1},{6,2},{7,3},{8,12},{9,13},{10,... | collective-permute-start | bytes 835592 | tf_op jit(solution)/shard_map/ppermute | solution.py:75
  50.7 9.6 %collective-permute-start.13 = (f32[128,512]{1,0:T(8,128)S(1)}, f32[128,512]{1,0:T(8,128)S(1)}, u32[]{:S(2)}, u32[]{:S(2)}) collective-permute-start(f32[128,512]{1,0:T(8,128)S(1)} %get-tuple-element.71), channel_id=1, source_target_pairs={{0,3},{1,2},{2,1},{3,0},{4,7},{5,6},{6,5},{7,4},{8,11},{9,10},{10,... | collective-permute-start | bytes 786440 | tf_op jit(solution)/shard_map/ppermute | solution.py:75
  53.1 7.8 %collective-permute-start.12 = (f32[128,512]{1,0:T(8,128)S(1)}, f32[128,512]{1,0:T(8,128)S(1)}, u32[]{:S(2)}, u32[]{:S(2)}) collective-permute-start(f32[128,512]{1,0:T(8,128)S(1)} %get-tuple-element.70), channel_id=1, source_target_pairs={{0,4},{1,5},{2,6},{3,7},{4,0},{5,1},{6,2},{7,3},{8,12},{9,13},{10,... | collective-permute-start | bytes 786440 | tf_op jit(solution)/shard_map/ppermute | solution.py:75
  55.9 10.3 %collective-permute-start.10 = (f32[72,512]{1,0:T(8,128)S(1)}, f32[72,512]{1,0:T(8,128)S(1)}, u32[]{:S(2)}, u32[]{:S(2)}) collective-permute-start(f32[72,512]{1,0:T(8,128)S(1)} %get-tuple-element.66), channel_id=1, source_target_pairs={{0,1},{1,0},{2,3},{3,2},{4,5},{5,4},{6,7},{7,6},{8,9},{9,8},{10,11... | collective-permute-start | bytes 442376 | tf_op jit(solution)/shard_map/ppermute | solution.py:75
  58.7 7.6 %collective-permute-start.11 = (f32[72,512]{1,0:T(8,128)S(1)}, f32[72,512]{1,0:T(8,128)S(1)}, u32[]{:S(2)}, u32[]{:S(2)}) collective-permute-start(f32[72,512]{1,0:T(8,128)S(1)} %get-tuple-element.67), channel_id=1, source_target_pairs={{0,28},{1,29},{2,30},{3,31},{4,8},{5,9},{6,10},{7,11},{8,4},{9,5},... | collective-permute-start | bytes 442376 | tf_op jit(solution)/shard_map/ppermute | solution.py:75
  60.8 5.4 %collective-permute-start.14 = (f32[64,512]{1,0:T(8,128)S(1)}, f32[64,512]{1,0:T(8,128)S(1)}, u32[]{:S(2)}, u32[]{:S(2)}) collective-permute-start(f32[64,512]{1,0:T(8,128)S(1)} %get-tuple-element.73.lower), channel_id=1, source_target_pairs={{0,32},{1,33},{2,34},{3,35},{4,36},{5,37},{6,38},{7,39},{8,40},{9,... | collective-permute-start | bytes 393224 | tf_op jit(solution)/shard_map/ppermute | solution.py:397
  60.9 7.3 %collective-permute-start.16 = (f32[64,512]{1,0:T(8,128)S(1)}, f32[64,512]{1,0:T(8,128)S(1)}, u32[]{:S(2)}, u32[]{:S(2)}) collective-permute-start(f32[64,512]{1,0:T(8,128)S(1)} %get-tuple-element.78), channel_id=1, source_target_pairs={{0,1},{1,0},{2,3},{3,2},{4,5},{5,4},{6,7},{7,6},{8,9},{9,8},{10,11... | collective-permute-start | bytes 393224 | tf_op jit(solution)/shard_map/ppermute | solution.py:75
  63.0 8.7 %collective-permute-start.17 = (f32[64,512]{1,0:T(8,128)S(1)}, f32[64,512]{1,0:T(8,128)S(1)}, u32[]{:S(2)}, u32[]{:S(2)}) collective-permute-start(f32[64,512]{1,0:T(8,128)S(1)} %get-tuple-element.79), channel_id=1, source_target_pairs={{0,28},{1,29},{2,30},{3,31},{4,8},{5,9},{6,10},{7,11},{8,4},{9,5},... | collective-permute-start | bytes 393224 | tf_op jit(solution)/shard_map/ppermute | solution.py:75
  66.3 15.4 %collective-permute-start.15 = (f32[72,512]{1,0:T(8,128)S(1)}, f32[72,512]{1,0:T(8,128)S(1)}, u32[]{:S(2)}, u32[]{:S(2)}) collective-permute-start(f32[72,512]{1,0:T(8,128)S(1)} %get-tuple-element.75), channel_id=1, source_target_pairs={{0,12},{1,13},{2,14},{3,15},{4,24},{5,25},{6,26},{7,27},{8,20},{9,... | collective-permute-start | bytes 442376 | tf_op jit(solution)/shard_map/ppermute | solution.py:75
  71.8 9.8 %collective-permute-start.18 = (f32[64,512]{1,0:T(8,128)S(1)}, f32[64,512]{1,0:T(8,128)S(1)}, u32[]{:S(2)}, u32[]{:S(2)}) collective-permute-start(f32[64,512]{1,0:T(8,128)S(1)} %get-tuple-element.80), channel_id=1, source_target_pairs={{0,12},{1,13},{2,14},{3,15},{4,24},{5,25},{6,26},{7,27},{8,20},{9,... | collective-permute-start | bytes 393224 | tf_op jit(solution)/shard_map/ppermute | solution.py:75
